TPU v7x, 128 devices: a whole 4x4x4 slice. The times are simulated.
128 devices in a mesh: blocks: 128 (over y, z, x, core).
Axes of the slice: x: 4, y: 4, z: 4, core: 2. Of those that a mesh axis runs over, the one named last changes fastest.
Arguments:
- spectra: float32 [4608, 66, 512], P('blocks'), may hold values from 0.05 to 2
- courant: float32 [4608, 3, 512], P('blocks'), may hold values from 0.05 to 0.3
- kernel: bfloat16 [66, 4356], replicated, may hold values from -0.09375 to 0.09375
- old_count: int32 [128], replicated, may hold values from 12 to 36, as said below
- new_count: int32 [128], replicated, may hold values from 12 to 36, as said below
- upwind: int32 [3072, 3], replicated, may hold values from 0 to 3071, as said below
Outputs:
- updated: float32 [4608, 66, 512], P('blocks')
Inputs may be any that keep to these rules, and one draw needn't show every extreme that they name: `old_count`: each count lies in the stated range and both ends are reached in the old and in the new layout; the counts sum to 3072; between the two layouts every device boundary along the curve moves by at most 12 blocks, and in every draw some boundary moves by exactly 12 blocks toward higher devices and another by exactly 12 toward lower devices. `new_count`: as old_count, for the new layout. Blocks form aligned runs of 12 along the curve, each run one cross-section of the grid; upwind[b, 0] = b - s * 12 cyclically over 3072, where s is +1 or -1 and depends only on b's position within its run, both signs occurring; upwind[b, 1] and upwind[b, 2] lie in the same run as b, arranged alike in every run; every block is upwind of exactly one block per direction.
All inputs are finite; a program needn't handle non-finite values.
Results may differ from a plain program's by a relative error of at most 0.0022.
Values sent between devices are 32-bit elements; how exact they have to be, the bound alone decides.
No kernel may reach another device: no remote copies, remote signals or barrier semaphores. Data moves between devices by JAX's collectives and lax.ppermute only.
A program may use at most 128 MiB of HBM per device.

v0:
```python
import jax
import jax.numpy as jnp
from jax import lax
from jax.sharding import PartitionSpec as P

BLK_DEV = 24
HALF = 12
BINS = 66
EDGE = 8
CELLS = 512
FACE = 4224


def passed_along(block, axis, distance):
    devices = range(lax.axis_size(axis))
    route = [((i - distance) % len(devices), i) for i in devices]
    return lax.ppermute(block, axis, route)


def from_behind(block, axis, distance):
    devices = range(lax.axis_size(axis))
    route = [(i - distance, i) for i in devices if i - distance in devices]
    return lax.ppermute(block, axis, route)


def exclusive(counts):
    return jnp.cumsum(counts) - counts


def minmod_value(lower, outer):
    return 0.5 * (jnp.sign(lower) + jnp.sign(outer)) * jnp.minimum(jnp.abs(lower), jnp.abs(outer))


def limited(outer, speeds, upwind_value):
    return speeds * (outer + 0.5 * (1.0 - speeds) * minmod_value(outer - upwind_value, outer))


def cell_coord(stride):
    cells = jnp.arange(CELLS, dtype=jnp.int32)
    return cells // stride % EDGE


def layer_table(stride, layer):
    cells = jnp.arange(CELLS, dtype=jnp.int32)
    coord = cells // stride % EDGE
    other = cells // (stride * EDGE) * stride + cells % stride
    spots = jnp.arange(EDGE * EDGE, dtype=jnp.int32)
    return ((coord == layer)[:, None] & (other[:, None] == spots[None, :])).astype(jnp.float32)


def take_layer(values, table):
    return jnp.einsum("sbc,cf->sbf", values, table, precision=lax.Precision.HIGHEST)


def put_layer(face_values, table):
    return jnp.einsum("sbf,cf->sbc", face_values, table, precision=lax.Precision.HIGHEST)


def shift_cells(values, stride):
    filler = jnp.zeros(values.shape[:-1] + (stride,), jnp.float32)
    return jnp.concatenate([filler, values[..., : CELLS - stride]], axis=-1)


def on_device(spectra, courant, kernel, old_count, new_count, upwind):
    device_count = lax.axis_size("blocks")
    device = lax.axis_index("blocks")
    capacity = spectra.shape[0]
    blocks = device_count * BLK_DEV
    padded_upwind = jnp.concatenate([upwind, jnp.zeros((capacity, 3), jnp.int32)], axis=0)
    strides = [EDGE * EDGE, EDGE, 1]
    last_tables = [layer_table(stride, EDGE - 1) for stride in strides]
    inner_tables = [layer_table(stride, EDGE - 2) for stride in strides]
    first_tables = [layer_table(stride, 0) for stride in strides]
    first_masks = [cell_coord(stride) == 0 for stride in strides]

    def gather_faces(payload, counts):
        starts = exclusive(counts)
        own_count = counts[device]
        prev_count = counts[(device - 1) % device_count]
        own_start = starts[device]
        upwind_rows = lax.dynamic_slice_in_dim(padded_upwind, own_start, capacity, 0)
        tail_faces = lax.dynamic_slice_in_dim(payload, own_count - HALF, HALF, 0)
        from_prev = passed_along(tail_faces, "blocks", 1)
        from_next = passed_along(payload[:HALF], "blocks", -1)
        face_pool = jnp.concatenate([from_prev, payload, from_next], axis=0)
        pool_offset = HALF
        prev_first = prev_count - HALF
        distance = jnp.mod(upwind_rows - own_start, blocks)
        is_ahead = distance < blocks // 2
        pool_index = jnp.where(
            distance < own_count,
            pool_offset + distance,
            jnp.where(
                is_ahead,
                pool_offset + capacity + distance - own_count,
                distance - blocks + prev_count - prev_first,
            ),
        )
        pool_index = jnp.clip(pool_index, 0, face_pool.shape[0] - 1)
        face_kinds = payload.shape[1]
        pool_index = jnp.tile(pool_index, (1, face_kinds // 3))
        return face_pool[pool_index, jnp.arange(face_kinds, dtype=jnp.int32)[None, :]]

    def face_of(faces, kind):
        return faces[:, kind].reshape(capacity, BINS, EDGE * EDGE)

    state = spectra
    speeds = courant
    fluxes = [speeds[:, direction][:, None] * state for direction in range(3)]
    outflow = jnp.stack(
        [
            take_layer(fluxes[direction], last_tables[direction]).reshape(capacity, FACE)
            for direction in range(3)
        ],
        axis=1,
    )
    inflow_faces = gather_faces(outflow, old_count)
    first = state
    for direction in range(3):
        placed = put_layer(face_of(inflow_faces, direction), first_tables[direction])
        inflow = jnp.where(
            first_masks[direction], placed, shift_cells(fluxes[direction], strides[direction])
        )
        first = first - fluxes[direction] + inflow
    carried = jnp.concatenate([first, courant], axis=1)
    old_starts = exclusive(old_count)
    new_starts = exclusive(new_count)
    old_here = old_count[device]
    upward = from_behind(lax.dynamic_slice_in_dim(carried, old_here - HALF, HALF, 0), "blocks", 1)
    downward = from_behind(carried[:HALF], "blocks", -1)
    moved_pool = jnp.concatenate([upward, carried, downward], axis=0)
    slot_ids = jnp.arange(capacity, dtype=jnp.int32)
    block_id = new_starts[device] + slot_ids
    next_start = old_starts[device] + old_here
    pool_index = jnp.where(
        block_id < next_start,
        HALF + block_id - old_starts[device],
        HALF + capacity + block_id - next_start,
    )
    pool_index = jnp.clip(pool_index, 0, moved_pool.shape[0] - 1)
    migrated = moved_pool[pool_index]
    live_slot = slot_ids < new_count[device]
    state = migrated[:, :BINS]
    speeds = migrated[:, BINS:]
    last_flux = []
    last_layer = []
    for direction in range(3):
        outer = take_layer(state, last_tables[direction])
        upwind_value = take_layer(state, inner_tables[direction])
        outer_speed = take_layer(speeds[:, direction : direction + 1], last_tables[direction])
        last_flux.append(limited(outer, outer_speed, upwind_value).reshape(capacity, FACE))
        last_layer.append(outer.reshape(capacity, FACE))
    edge_faces = gather_faces(jnp.stack(last_flux + last_layer, axis=1), new_count)
    second = state
    for direction in range(3):
        stride = strides[direction]
        layer_in = put_layer(face_of(edge_faces, 3 + direction), first_tables[direction])
        upwind_value = jnp.where(first_masks[direction], layer_in, shift_cells(state, stride))
        cell_flux = limited(state, speeds[:, direction][:, None], upwind_value)
        face_in = put_layer(face_of(edge_faces, direction), first_tables[direction])
        inflow = jnp.where(first_masks[direction], face_in, shift_cells(cell_flux, stride))
        second = second - cell_flux + inflow
    padded_bins = (BINS + 7) // 8 * 8
    kernel_wide = jnp.pad(
        kernel.reshape(BINS, BINS, BINS), ((0, 0), (0, 0), (0, padded_bins - BINS))
    )
    kernel_wide = kernel_wide.reshape(BINS, BINS * padded_bins)
    grouped = second.reshape(capacity // 2, 2, BINS, CELLS)

    def coalesce(pair_block):
        widened = jnp.pad(pair_block, ((0, 0), (0, padded_bins - BINS), (0, 0)))
        pair_terms = (
            (pair_block[:, :, None, :] * widened[:, None, :, :])
            .reshape(2, BINS * padded_bins, CELLS)
            .astype(jnp.bfloat16)
        )
        gained = jnp.einsum(
            "kp,spc->skc", kernel_wide, pair_terms, preferred_element_type=jnp.float32
        )
        return pair_block + gained

    coalesced = lax.map(coalesce, grouped).reshape(capacity, BINS, CELLS)
    return jnp.where(live_slot[:, None, None], coalesced, 0.0)


def solution(mesh):
    in_specs = (P("blocks", None, None), P("blocks", None, None), P(), P(), P(), P())
    out_specs = P("blocks", None, None)
    return jax.shard_map(
        on_device, mesh=mesh, in_specs=in_specs, out_specs=out_specs, check_vma=False
    )
```

profile of v0, /device:TPU:111, one launch (start us, length us, event | category | flops | bytes accessed | tf_op | source)
XLA Modules:
  0.0 512.5 jit_solution(3595825638879755196)
XLA Ops:
  34.6 9.0 %broadcast_multiply_fusion.2 = (f32[36,66,512]{2,1,0:T(8,128)}, f32[36,66,512]{2,1,0:T(8,128)}, f32[36,66,512]{2,1,0:T(8,128)}) fusion(f32[36,66,512]{2,1,0:T(8,128)} %param.8, f32[36,512]{1,0:T(8,128)S(1)} %copy-done.11, f32[36,512]{1,0:T(8,128)S(1)} %copy-done.14, f32[36,512]{1,0:T(8,128)S(1)} %copy-done.8), kind=kLoop, calls=%fused_computation.23 | loop fusion | flops 3649536 | bytes 19685376 | tf_op jit(solution)/shard_map/mul | solution.py:109
  52.9 5.6 %slice_reduce_fusion.6 = (f32[36,4224]{1,0:T(8,128)S(1)}, f32[36,4224]{1,0:T(8,128)}, f32[36,4224]{1,0:T(8,128)}) fusion(f32[36,3,4224]{2,1,0:T(4,128)S(1)} %reshape.316), kind=kLoop, calls=%fused_computation.53 | loop fusion | bytes 3649536 | tf_op jit(solution)/shard_map/slice | solution.py:105
  64.1 6.0 %fusion.86 = f32[36,66,512]{2,1,0:T(8,128)} fusion(f32[36,66,64]{2,1,0:T(8,128)} %reshape_squeeze.27, s32[512]{0:T(512)S(1)} %fusion.148, pred[512]{0:T(512)(128)(4,1)S(1)} %copy-done.30), kind=kOutput, calls=%fused_computation.95 | convolution fusion | flops 934346752 | bytes 5476864 | tf_op jit(solution)/shard_map/sbf,cf->sbc/dot_general | solution.py:56
  74.7 24.5 %select_add_fusion.1 = f32[36,66,512]{2,1,0:T(8,128)} fusion(f32[36,66,511]{2,1,0:T(8,128)} %bitcast.163, f32[36,66,512]{2,1,0:T(8,128)} %fusion.78, f32[36,66,504]{2,1,0:T(8,128)} %bitcast.164, f32[36,66,512]{2,1,0:T(8,128)} %fusion.86, f32[36,66,448]{2,1,0:T(8,128)} %bitcast.162, f32[36,66,512]{2,1,0:T(8,128)S(1)} %bitcast.158, ...), kind=kOutput, calls=%fused_computation.19 | convolution fusion | flops 948944896 | bytes 34201568 | tf_op jit(solution)/shard_map/sbf,cf->sbc/dot_general | solution.py:56
  103.6 7.4 %collective-permute-start.2 = (f32[12,69,512]{2,1,0:T(8,128)}, f32[12,69,512]{2,1,0:T(8,128)S(1)}, u32[]{:S(2)}, u32[]{:S(2)}) collective-permute-start(f32[12,69,512]{2,1,0:T(8,128)} %get-tuple-element.76), channel_id=1, source_target_pairs={{0,1},{1,2},{2,3},{3,4},{4,5},{5,6},{6,7},{7,8},{8,9},{9,10},{10,1... | collective-permute-start | bytes 5087240 | tf_op jit(solution)/shard_map/ppermute | solution.py:23
  119.0 11.8 %collective-permute-done.2 = f32[12,69,512]{2,1,0:T(8,128)S(1)} collective-permute-done((f32[12,69,512]{2,1,0:T(8,128)}, f32[12,69,512]{2,1,0:T(8,128)S(1)}, u32[]{:S(2)}, u32[]{:S(2)}) %collective-permute-start.2) | collective-permute-done | bytes 1695776 | tf_op jit(solution)/shard_map/ppermute | solution.py:23
  130.8 8.6 %collective-permute-done.3 = f32[12,69,512]{2,1,0:T(8,128)} collective-permute-done((f32[12,69,512]{2,1,0:T(8,128)}, f32[12,69,512]{2,1,0:T(8,128)}, u32[]{:S(2)}, u32[]{:S(2)}) %collective-permute-start.3) | collective-permute-done | bytes 1695776 | tf_op jit(solution)/shard_map/ppermute | solution.py:23
  139.4 6.0 %pad_maximum_fusion = f32[60,69,512]{2,1,0:T(8,128)} fusion(f32[12,69,512]{2,1,0:T(8,128)} %collective-permute-done.3, f32[36,3,512]{2,1,0:T(4,128)S(1)} %copy.20, f32[36,66,512]{2,1,0:T(8,128)} %select_add_fusion.1, f32[12,69,512]{2,1,0:T(8,128)S(1)} %collective-permute-done.2), kind=kLoop, calls=%fused_computation.10 | loop fusion | flops 6359040 | bytes 16957440 | tf_op jit(solution)/shard_map/concatenate | solution.py:131
  145.4 6.8 %gather_fusion.1 = f32[36,69,512]{2,1,0:T(8,128)} fusion(f32[60,69,512]{2,1,0:T(8,128)} %pad_maximum_fusion, s32[1024]{0:T(1024)S(1)} %pad_clamp_fusion), kind=kCustom, calls=%fused_computation.1 | custom fusion | bytes 10174608 | tf_op jit(solution)/shard_map/gather | solution.py:141
  152.2 6.3 %fusion.6 = f32[36,66,64]{1,2,0:T(8,128)S(1)} fusion(f32[36,69,512]{2,1,0:T(8,128)} %gather_fusion.1, s32[512]{0:T(512)S(1)} %get-tuple-element.104, pred[512]{0:T(512)(128)(4,1)S(1)} %copy-done.39), kind=kOutput, calls=%fused_computation.26 | convolution fusion | flops 934346752 | bytes 5698048 | tf_op jit(solution)/shard_map/sbc,cf->sbf/dot_general | solution.py:52
  169.3 8.0 %add_multiply_fusion.3 = f32[36,66,64]{1,2,0:T(8,128)} fusion(f32[36,66,64]{1,2,0:T(8,128)S(1)} %fusion.6, f32[36,69,512]{2,1,0:T(8,128)} %gather_fusion.1, f32[36,64]{1,0:T(8,128)} %get-tuple-element.102, f32[36,64]{1,0:T(8,128)} %get-tuple-element.103, s32[512]{0:T(512)S(1)} %get-tuple-element.104, pred[512]{0:T(512)(128)(4,1)} %get-tuple-element.106), kind=kOutput, calls=%fused_computation.44 | convolution fusion | flops 936171520 | bytes 6324736 | tf_op jit(solution)/shard_map/sbc,cf->sbf/dot_general | solution.py:52
  184.5 7.6 %add_multiply_fusion.4 = f32[36,66,64]{1,2,0:T(8,128)} fusion(f32[36,66,64]{1,2,0:T(8,128)S(1)} %fusion.10, f32[36,69,512]{2,1,0:T(8,128)} %gather_fusion.1, f32[36,64]{1,0:T(8,128)S(1)} %get-tuple-element.100, f32[36,64]{1,0:T(8,128)S(1)} %get-tuple-element.101, s32[512]{0:T(512)S(1)} %get-tuple-element.105, pred[512]{0:T(512)(128)(4,1)S(1)} %copy-done.46), kind=kOutput, calls=%fused_computation.45 | convolution fusion | flops 936171520 | bytes 6324736 | tf_op jit(solution)/shard_map/sbc,cf->sbf/dot_general | solution.py:52
  196.8 7.6 %add_multiply_fusion.5 = f32[36,66,64]{1,2,0:T(8,128)} fusion(f32[36,66,64]{1,2,0:T(8,128)S(1)} %fusion.14, f32[36,69,512]{2,1,0:T(8,128)} %gather_fusion.1, f32[36,64]{1,0:T(8,128)S(1)} %get-tuple-element.98, f32[36,64]{1,0:T(8,128)S(1)} %get-tuple-element.99, s32[512]{0:T(512)S(1)} %fusion.148, pred[512]{0:T(512)(128)(4,1)S(1)} %copy-done.45), kind=kOutput, calls=%fused_computation.46 | convolution fusion | flops 936171520 | bytes 6324736 | tf_op jit(solution)/shard_map/sbc,cf->sbf/dot_general | solution.py:52
  239.1 7.2 %collective-permute-done.4 = f32[12,6,4224]{2,0,1:T(8,128)} collective-permute-done((f32[12,6,4224]{2,0,1:T(8,128)}, f32[12,6,4224]{2,0,1:T(8,128)}, u32[]{:S(2)}, u32[]{:S(2)}) %collective-permute-start.4) | collective-permute-done | bytes 1216544 | tf_op jit(solution)/shard_map/ppermute | solution.py:17
  246.3 6.7 %collective-permute-done.5 = f32[12,6,4224]{2,0,1:T(8,128)} collective-permute-done((f32[12,6,4224]{2,0,1:T(8,128)}, f32[12,6,4224]{2,0,1:T(8,128)}, u32[]{:S(2)}, u32[]{:S(2)}) %collective-permute-start.5) | collective-permute-done | bytes 1216544 | tf_op jit(solution)/shard_map/ppermute | solution.py:17
  253.0 6.4 %pad_maximum_fusion.1 = f32[60,6,4224]{2,0,1:T(8,128)} fusion(f32[12,6,4224]{2,0,1:T(8,128)} %collective-permute-done.5, f32[36,6,4224]{2,0,1:T(8,128)} %constant_dynamic-update-slice_fusion.3, f32[12,6,4224]{2,0,1:T(8,128)} %collective-permute-done.4), kind=kLoop, calls=%fused_computation.11 | loop fusion | flops 3041280 | bytes 12165120 | tf_op jit(solution)/shard_map/concatenate | solution.py:85
  259.4 10.4 %gather_fusion.2 = f32[216,4224]{1,0:T(8,128)} fusion(f32[60,6,4224]{2,0,1:T(8,128)} %pad_maximum_fusion.1, s32[216]{0:T(256)S(1)} %reshape.327), kind=kCustom, calls=%fused_computation.2 | custom fusion | bytes 7300800 | tf_op jit(solution)/shard_map/gather | solution.py:102
  274.8 22.4 %slice_reduce_fusion = (f32[36,4224]{1,0:T(8,128)}, f32[36,4224]{1,0:T(8,128)}, f32[36,4224]{1,0:T(8,128)}, f32[36,4224]{1,0:T(8,128)S(1)}, f32[36,4224]{1,0:T(8,128)S(1)}, /*index=5*/f32[36,4224]{1,0:T(8,128)S(1)}) fusion(f32[36,6,4224]{2,1,0:T(8,128)} %reshape.330), kind=kLoop, calls=%fused_computation.47 | loop fusion | bytes 7299072 | tf_op jit(solution)/shard_map/slice | solution.py:105
  315.4 11.2 %add_multiply_fusion.2 = f32[36,66,512]{2,1,0:T(8,128)} fusion(f32[36,66,448]{2,1,0:T(8,128)} %bitcast.152, f32[36,512]{1,0:T(8,128)} %bitcast.171, f32[36,512]{1,0:T(8,128)S(1)} %bitcast.168, pred[512]{0:T(512)(128)(4,1)S(1)} %copy-done.31, f32[36,69,512]{2,1,0:T(8,128)} %gather_fusion.1, f32[36,66,64]{2,1,0:T(8,128)} %reshape_squeeze.30, s32[512]{0:T(512)S(1)} %fusion.148), kind=kOutput, calls=%fused_computation.18 | convolution fusion | flops 950161408 | bytes 14756864 | tf_op jit(solution)/shard_map/sbf,cf->sbc/dot_general | solution.py:56
  326.7 8.6 %add_multiply_fusion.1 = f32[36,66,512]{2,1,0:T(8,128)} fusion(f32[36,66,504]{2,1,0:T(8,128)S(1)} %bitcast.155, f32[36,512]{1,0:T(8,128)S(1)} %bitcast.170, f32[36,512]{1,0:T(8,128)S(1)} %bitcast.167, pred[512]{0:T(512)(128)(4,1)S(1)} %copy-done.33, f32[36,69,512]{2,1,0:T(8,128)S(1)} %bitcast.154, f32[36,66,64]{2,1,0:T(8,128)S(1)} %copy-done.5, ...), kind=kOutput, calls=%fused_computation.17 | convolution fusion | flops 950161408 | bytes 16976896 | tf_op jit(solution)/shard_map/sbf,cf->sbc/dot_general | solution.py:56
  335.3 8.1 %add_multiply_fusion = f32[36,66,512]{2,1,0:T(8,128)} fusion(f32[36,66,511]{2,1,0:T(8,128)S(1)} %bitcast.156, f32[36,512]{1,0:T(8,128)S(1)} %bitcast.169, f32[36,512]{1,0:T(8,128)S(1)} %bitcast.166, pred[512]{0:T(512)(128)(4,1)S(1)} %copy-done.44, f32[36,69,512]{2,1,0:T(8,128)S(1)} %bitcast.154, f32[36,66,64]{2,1,0:T(8,128)S(1)} %copy-done.6, ...), kind=kOutput, calls=%fused_computation.16 | convolution fusion | flops 950161408 | bytes 16976896 | tf_op jit(solution)/shard_map/sbf,cf->sbc/dot_general | solution.py:56
  343.4 21.0 %select_add_fusion = f32[36,66,512]{2,1,0:T(8,128)} fusion(f32[36,66,511]{2,1,0:T(8,128)} %bitcast.161, f32[36,66,512]{2,1,0:T(8,128)} %add_multiply_fusion, f32[36,66,512]{2,1,0:T(8,128)} %fusion.74, f32[36,66,504]{2,1,0:T(8,128)} %bitcast.160, f32[36,66,512]{2,1,0:T(8,128)} %add_multiply_fusion.1, f32[36,66,512]{2,1,0:T(8,128)} %fusion.82, ...), kind=kOutput, calls=%fused_computation.15 | convolution fusion | flops 945295360 | bytes 49297888 | tf_op jit(solution)/shard_map/sbf,cf->sbc/dot_general | solution.py:56
  364.4 142.2 %while.12 = (s32[]{:T(128)}, f32[18,2,66,512]{3,2,1,0:T(8,128)}, f32[18,2,66,512]{3,2,1,0:T(8,128)}, bf16[66,4752]{1,0:T(8,128)(2,1)S(1)}, s32[]{:T(128)}, /*index=5*/f32[]{:T(128)}) while((s32[]{:T(128)}, f32[18,2,66,512]{3,2,1,0:T(8,128)}, f32[18,2,66,512]{3,2,1,0:T(8,128)}, bf16[66,4752]{1,0:T(8,128)(2,1)S(1)}, s32[]{:T(128)}, ...), condition=%wide.region_3.4_spmd, body=%wide.region_2.3_spmd.sunk | while | flops 652118016 | bytes 22353036 | solution.py:182
  506.6 5.7 %bitcast_select_fusion = f32[36,66,512]{2,1,0:T(8,128)} fusion(f32[18,2,66,512]{3,2,1,0:T(8,128)} %get-tuple-element.58, pred[36]{0:T(512)(128)(4,1)S(1)} %iota_compare_fusion.3), kind=kLoop, calls=%fused_computation.14 | loop fusion | flops 1216512 | bytes 9732132 | tf_op jit(solution)/shard_map/jit(_where)/select_n | solution.py:183
  (277 shorter events, 279.2 us)
Async XLA Ops:
  0.0 16.2 %copy-start.34 = (pred[512]{0:T(512)(128)(4,1)}, pred[512]{0:T(512)(128)(4,1)S(1)}, u32[]{:S(2)}) copy-start(pred[512]{0:T(512)(128)(4,1)S(1)} %get-tuple-element.111) | copy-start | bytes 1540
  0.0 16.2 %copy-start.36 = (pred[512]{0:T(512)(128)(4,1)}, pred[512]{0:T(512)(128)(4,1)S(1)}, u32[]{:S(2)}) copy-start(pred[512]{0:T(512)(128)(4,1)S(1)} %get-tuple-element.110) | copy-start | bytes 1540
  0.6 16.0 %copy-start.38 = (pred[512]{0:T(512)(128)(4,1)}, pred[512]{0:T(512)(128)(4,1)S(1)}, u32[]{:S(2)}) copy-start(pred[512]{0:T(512)(128)(4,1)S(1)} %get-tuple-element.109) | copy-start | bytes 1540
  4.2 12.0 %copy-start.10 = (f32[36,512]{1,0:T(8,128)}, f32[36,512]{1,0:T(8,128)S(1)}, u32[]{:S(2)}) copy-start(f32[36,512]{1,0:T(8,128)S(1)} %get-tuple-element.92) | copy-start | bytes 221188
  4.2 12.4 %copy-start.13 = (f32[36,512]{1,0:T(8,128)}, f32[36,512]{1,0:T(8,128)S(1)}, u32[]{:S(2)}) copy-start(f32[36,512]{1,0:T(8,128)S(1)} %get-tuple-element.93) | copy-start | bytes 221188
  23.0 11.6 %copy-start.11 = (f32[36,512]{1,0:T(8,128)S(1)}, f32[36,512]{1,0:T(8,128)}, u32[]{:S(2)}) copy-start(f32[36,512]{1,0:T(8,128)} %copy-done.10) | copy-start | bytes 221188
  23.0 11.6 %copy-start.14 = (f32[36,512]{1,0:T(8,128)S(1)}, f32[36,512]{1,0:T(8,128)}, u32[]{:S(2)}) copy-start(f32[36,512]{1,0:T(8,128)} %copy-done.13) | copy-start | bytes 221188
  25.4 18.2 %copy-start.1 = (f32[36,3,4224]{2,0,1:T(8,128)}, f32[36,3,4224]{2,0,1:T(8,128)S(1)}, u32[]{:S(2)}) copy-start(f32[36,3,4224]{2,0,1:T(8,128)S(1)} %constant_dynamic-update-slice_fusion) | copy-start | bytes 5474308
  26.8 16.8 %collective-permute-start = (f32[12,3,4224]{2,0,1:T(8,128)}, f32[12,3,4224]{2,0,1:T(8,128)}, u32[]{:S(2)}, u32[]{:S(2)}) collective-permute-start(f32[12,3,4224]{2,0,1:T(8,128)} %get-tuple-element.89), channel_id=1, source_target_pairs={{127,0},{0,1},{1,2},{2,3},{3,4},{4,5},{5,6},{6,7},{7,8},{8,9},{9,1... | collective-permute-start | bytes 1824776 | tf_op jit(solution)/shard_map/ppermute | solution.py:17
  27.2 16.6 %collective-permute-start.1 = (f32[12,3,4224]{2,0,1:T(8,128)}, f32[12,3,4224]{2,0,1:T(8,128)}, u32[]{:S(2)}, u32[]{:S(2)}) collective-permute-start(f32[12,3,4224]{2,0,1:T(8,128)} %get-tuple-element.90), channel_id=1, source_target_pairs={{1,0},{2,1},{3,2},{4,3},{5,4},{6,5},{7,6},{8,7},{9,8},{10,9},{11,1... | collective-permute-start | bytes 1824776 | tf_op jit(solution)/shard_map/ppermute | solution.py:17
  99.2 16.3 %copy-start.42 = (s32[128]{0:T(128)S(1)}, s32[128]{0:T(128)}, u32[]{:S(2)}) copy-start(s32[128]{0:T(128)} %param.12) | copy-start | bytes 1540
  103.6 27.2 %collective-permute-start.2 = (f32[12,69,512]{2,1,0:T(8,128)}, f32[12,69,512]{2,1,0:T(8,128)S(1)}, u32[]{:S(2)}, u32[]{:S(2)}) collective-permute-start(f32[12,69,512]{2,1,0:T(8,128)} %get-tuple-element.76), channel_id=1, source_target_pairs={{0,1},{1,2},{2,3},{3,4},{4,5},{5,6},{6,7},{7,8},{8,9},{9,10},{10,1... | collective-permute-start | bytes 5087240 | tf_op jit(solution)/shard_map/ppermute | solution.py:23
  111.1 28.4 %collective-permute-start.3 = (f32[12,69,512]{2,1,0:T(8,128)}, f32[12,69,512]{2,1,0:T(8,128)}, u32[]{:S(2)}, u32[]{:S(2)}) collective-permute-start(f32[12,69,512]{2,1,0:T(8,128)} %get-tuple-element.77), channel_id=1, source_target_pairs={{1,0},{2,1},{3,2},{4,3},{5,4},{6,5},{7,6},{8,7},{9,8},{10,9},{11,1... | collective-permute-start | bytes 5087240 | tf_op jit(solution)/shard_map/ppermute | solution.py:23
  218.9 12.1 %copy-start.26 = (s32[3072,3]{0,1:T(4,128)S(1)}, s32[3072,3]{0,1:T(4,128)}, u32[]{:S(2)}) copy-start(s32[3072,3]{0,1:T(4,128)} %param.13) | copy-start | bytes 110596
  218.9 14.3 %copy-start.21 = (bf16[66,4356]{1,0:T(8,128)(2,1)S(1)}, bf16[66,4356]{1,0:T(8,128)(2,1)}, u32[]{:S(2)}) copy-start(bf16[66,4356]{1,0:T(8,128)(2,1)} %param.10) | copy-start | bytes 1724980
  223.9 13.2 %copy-start.19 = (f32[36,1,512]{2,1,0:T(1,128)S(1)}, f32[36,1,512]{2,1,0:T(1,128)}, u32[]{:S(2)}) copy-start(f32[36,1,512]{2,1,0:T(1,128)} %get-tuple-element.82) | copy-start | bytes 221188
  223.9 13.8 %copy-start.18 = (f32[36,1,512]{2,1,0:T(1,128)S(1)}, f32[36,1,512]{2,1,0:T(1,128)}, u32[]{:S(2)}) copy-start(f32[36,1,512]{2,1,0:T(1,128)} %copy-done.17) | copy-start | bytes 221188
  223.9 14.5 %copy-start.24 = (f32[36,1,512]{2,1,0:T(1,128)S(1)}, f32[36,1,512]{2,1,0:T(1,128)}, u32[]{:S(2)}) copy-start(f32[36,1,512]{2,1,0:T(1,128)} %get-tuple-element.78) | copy-start | bytes 221188
  223.9 15.1 %copy-start.23 = (f32[36,1,512]{2,1,0:T(1,128)S(1)}, f32[36,1,512]{2,1,0:T(1,128)}, u32[]{:S(2)}) copy-start(f32[36,1,512]{2,1,0:T(1,128)} %get-tuple-element.79) | copy-start | bytes 221188
  223.9 15.1 %copy-start.22 = (f32[36,1,512]{2,1,0:T(1,128)S(1)}, f32[36,1,512]{2,1,0:T(1,128)}, u32[]{:S(2)}) copy-start(f32[36,1,512]{2,1,0:T(1,128)} %get-tuple-element.80) | copy-start | bytes 221188
  228.1 18.2 %collective-permute-start.4 = (f32[12,6,4224]{2,0,1:T(8,128)}, f32[12,6,4224]{2,0,1:T(8,128)}, u32[]{:S(2)}, u32[]{:S(2)}) collective-permute-start(f32[12,6,4224]{2,0,1:T(8,128)} %get-tuple-element.87), channel_id=1, source_target_pairs={{127,0},{0,1},{1,2},{2,3},{3,4},{4,5},{5,6},{6,7},{7,8},{8,9},{9,1... | collective-permute-start | bytes 3649544 | tf_op jit(solution)/shard_map/ppermute | solution.py:17
  228.1 24.9 %collective-permute-start.5 = (f32[12,6,4224]{2,0,1:T(8,128)}, f32[12,6,4224]{2,0,1:T(8,128)}, u32[]{:S(2)}, u32[]{:S(2)}) collective-permute-start(f32[12,6,4224]{2,0,1:T(8,128)} %get-tuple-element.88), channel_id=1, source_target_pairs={{1,0},{2,1},{3,2},{4,3},{5,4},{6,5},{7,6},{8,7},{9,8},{10,9},{11,1... | collective-permute-start | bytes 3649544 | tf_op jit(solution)/shard_map/ppermute | solution.py:17
  274.8 27.0 %copy-start.33 = (pred[512]{0:T(512)(128)(4,1)S(1)}, pred[512]{0:T(512)(128)(4,1)}, u32[]{:S(2)}) copy-start(pred[512]{0:T(512)(128)(4,1)} %get-tuple-element.113) | copy-start | bytes 1540
  311.3 15.3 %slice-start = ((s8[5308416]{0:T(1024)(128)(4,1)}), s8[1114112]{0:T(1024)(128)(4,1)S(1)}, s32[]{:S(2)}) async-start(s8[5308416]{0:T(1024)(128)(4,1)} %bitcast.153), calls=%async_computation | async-start | bytes 2228224
  (33 other events, 287.8 us)
where the time goes:
time: 523 us; the launch traced here: 513 us
  matrix products  210 us (40%)
  local copies, waits for them, and re-layouts  142 us (27%)
  other arithmetic  104 us (20%)
  waiting for transfers between devices  34.5 us (7%)
  starting transfers between devices  10.9 us (2%)
  between operations  9.79 us (2%)
    dot_general x9, matrix products, put_layer(): jnp.einsum('sbf,cf->sbc', face_values, table, precision=lax.Precision.HIG...  93.1 us
    dot_general x18, matrix products, coalesce(): jnp.einsum('kp,spc->skc', kernel_wide, pair_terms, preferred_element_type...  62.9 us
    convert_element_type x18, other arithmetic, coalesce(): pair_terms = (pair_block[:, :, None, :] * widened[:, None, :, :]).reshape...  60.7 us
    dot_general x12, matrix products, take_layer(): jnp.einsum('sbc,cf->sbf', values, table, precision=lax.Precision.HIGHEST)  54.4 us
    slice x2, local copies, waits for them, and re-layouts, face_of(): return faces[:, kind].reshape(capacity, BINS, EDGE * EDGE)  28.1 us
    gather x4, local copies, waits for them, and re-layouts, gather_faces(): face_pool[pool_index, jnp.arange(face_kinds, dtype=jnp.int32)[None, :]]  22.3 us
    ppermute x2, waiting for transfers between devices, from_behind(): return lax.ppermute(block, axis, route)  20.4 us
    squeeze x18, local copies, waits for them, and re-layouts, on_device(): coalesced = lax.map(coalesce, grouped).reshape(capacity, BINS, CELLS)  17.7 us
  transfers between devices with their start and end apart: 6, of which 5 were waited for; matrix products, arithmetic and copies ran while one was open for 5% of the time, Pallas kernels for 0%

commit v1 on v0

v1 whole, which is shorter than its diff:
```python
import functools

import jax
import jax.numpy as jnp
from jax import lax
from jax.experimental import pallas as pl
from jax.experimental.pallas import tpu as pltpu
from jax.sharding import PartitionSpec as P

RUN = 12
BINS = 66
CELLS = 512
HALF = 256
LANES = 128
PACKED = 72
FULL = 64
TERMS = 2304
FACES = 18
F32 = jnp.float32
VMEM = pl.BlockSpec(memory_space=pltpu.VMEM)
SMEM = pl.BlockSpec(memory_space=pltpu.SMEM)
OLD0, OLD1, MID0, MID1, NEW0, NEW1 = range(6)


def params(mib):
    return pltpu.CompilerParams(vmem_limit_bytes=mib * 2**20)


def lanes():
    return lax.broadcasted_iota(jnp.int32, (1, LANES), 1)


def span(v):
    return slice(v * LANES, (v + 1) * LANES)


def upper():
    return lanes() >= 64


def last_y():
    return lanes() // 8 % 8 == 7


def last_z():
    return lanes() % 8 == 7


def swap(x):
    return pltpu.roll(x, 64, 1)


def step_y(x):
    return jnp.where(lanes() // 8 % 8 == 0, pltpu.roll(x, 72, 1), pltpu.roll(x, 8, 1))


def step_z(x):
    return jnp.where(lanes() % 8 == 0, pltpu.roll(x, 121, 1), pltpu.roll(x, 1, 1))


def minmod(a, e):
    return jnp.maximum(jnp.minimum(a, e), 0.0) + jnp.minimum(jnp.maximum(a, e), 0.0)


def limited(q, c, before):
    return c * (q + (0.5 * (1.0 - c)) * minmod(q - before, q))


def upwind_of(table, position):
    back = table[3 * position] < RUN + position
    return back, table[3 * position + 1] - RUN, table[3 * position + 2] - RUN


def donor(q, c, q_prev, cx_prev, q_y, c_y, q_z, c_z):
    cx, cy, cz = c[0:1], c[1:2], c[2:3]
    up, ly, lz = upper(), last_y(), last_z()
    in_x = swap(jnp.where(up, cx_prev, cx) * jnp.where(up, q_prev, q))
    in_y = step_y(jnp.where(ly, c_y[1:2], cy) * jnp.where(ly, q_y, q))
    in_z = step_z(jnp.where(lz, c_z[2:3], cz) * jnp.where(lz, q_z, q))
    return (1.0 - (cx + cy + cz)) * q + in_x + in_y + in_z


def fetch(block, scal, spectra, courant, low, high, rows, q_dst, c_dst, at):
    own0, own1 = scal[OLD0], scal[OLD1]

    @pl.when((block >= own0) & (block < own1))
    def _():
        q_dst[at] = spectra[block - own0]
        c_dst[at, 0:3] = courant[block - own0]

    @pl.when(block < own0)
    def _():
        i = block - own0 + RUN
        q_dst[at] = low[i, 0:BINS]
        c_dst[at, 0:3] = low[i, BINS : BINS + 3]

    @pl.when(block >= own1)
    def _():
        i = block - own1
        q_dst[at] = high[i, 0:BINS]
        c_dst[at, 0:3] = high[i, BINS : BINS + 3]


def pack_kernel(scal, tail_q, tail_c, head_q, head_c, up, down):
    pad = jnp.zeros((1, PACKED - BINS - 3, CELLS), F32)
    up[...] = jnp.concatenate([tail_q[...], tail_c[...], pad], axis=1)
    down[...] = jnp.concatenate([head_q[...], head_c[...], pad], axis=1)


def pack(spectra, courant, tail_start):
    def tail(i, scal):
        return (scal[0] + i, 0, 0)

    def head(i, scal):
        return (i, 0, 0)

    return pl.pallas_call(
        pack_kernel,
        grid_spec=pltpu.PrefetchScalarGridSpec(
            num_scalar_prefetch=1,
            grid=(RUN,),
            in_specs=[
                pl.BlockSpec((1, BINS, CELLS), tail),
                pl.BlockSpec((1, 3, CELLS), tail),
                pl.BlockSpec((1, BINS, CELLS), head),
                pl.BlockSpec((1, 3, CELLS), head),
            ],
            out_specs=[pl.BlockSpec((1, PACKED, CELLS), head)] * 2,
        ),
        out_shape=[jax.ShapeDtypeStruct((RUN, PACKED, CELLS), F32)] * 2,
        compiler_params=params(24),
    )(tail_start, spectra, courant, spectra, courant)


def face_kernel(scal, table, spectra, courant, low, high, up, down, q0, cs):
    count = scal[MID1] - scal[MID0]

    def gather(j, _):
        first = scal[MID0] + jnp.where(j < RUN, j, count - 2 * RUN + j)
        fetch(first, scal, spectra, courant, low, high, BINS, q0, cs, j)
        return 0

    lax.fori_loop(0, 2 * RUN, gather, 0)

    def face(j, position):
        _, y, z = upwind_of(table, position)
        uy, uz = y + (j - position), z + (j - position)
        s, t = span(1), span(0)
        q, c = q0[j, :, s], cs[j, :, s]
        q1 = donor(q, c, q0[j, :, t], cs[j, 0:1, t], q0[uy, :, s], cs[uy, :, s], q0[uz, :, s], cs[uz, :, s])
        other = swap(q1)
        return jnp.where(upper(), limited(q1, c[0:1], other), other), c[0:1] * q

    for base, out in ((0, down), (RUN, up)):

        def pair(i, _, base=base, out=out):
            a0, b0 = face(base + 2 * i, 2 * i)
            a1, b1 = face(base + 2 * i + 1, 2 * i + 1)
            out[2 * i, 0:BINS] = a0
            out[2 * i + 1, 0:BINS] = a1
            out[RUN + i, 0:BINS] = jnp.where(upper(), b1, swap(b0))
            return 0

        lax.fori_loop(0, RUN // 2, pair, 0)


def faces(scal, table, spectra, courant, low, high):
    capacity = spectra.shape[0]

    def half(*dims):
        return pl.BlockSpec(dims + (HALF,), lambda i: (0, 0, 1))

    return pl.pallas_call(
        face_kernel,
        grid=(1,),
        in_specs=[
            SMEM,
            SMEM,
            half(capacity, BINS),
            half(capacity, 3),
            half(RUN, PACKED),
            half(RUN, PACKED),
        ],
        out_specs=[VMEM] * 2,
        out_shape=[jax.ShapeDtypeStruct((FACES, PACKED, LANES), F32)] * 2,
        scratch_shapes=[pltpu.VMEM((2 * RUN, BINS, HALF), F32), pltpu.VMEM((2 * RUN, 3, HALF), F32)],
        compiler_params=params(24),
    )(scal, table, spectra, courant, low, high)


def pair_terms(q):
    wide = q.shape[1]
    group = [q[8 * g : 8 * g + 8, :] for g in range(8)]
    row = [jnp.broadcast_to(q[i : i + 1, :], (8, wide)) for i in range(BINS)]
    out = [row[i] * group[g] for i in range(56) for g in range(i // 8 + 1, 8)]
    out += [row[i] * group[g] for i in (64, 65) for g in range(8)]
    for s in range(5):
        out += [x * (pltpu.roll(x, s, 0) if s else x) for x in group]
    at = lax.broadcasted_iota(jnp.int32, (8, wide), 0)
    rest = jnp.where(at < 2, row[64], row[65]) * jnp.where(at < 1, row[64], row[65])
    out.append(jnp.where(at < 3, rest, 0.0))
    return out + [jnp.zeros((8, wide), F32)] * (TERMS // 8 - len(out))


def symmetric_kernel(kernel):
    k = kernel.astype(F32).reshape(BINS, BINS, BINS)
    both = k + jnp.swapaxes(k, 1, 2)
    parts = [both[:, 8 * g : 8 * g + 8, 8 * g + 8 : FULL].reshape(BINS, -1) for g in range(7)]
    parts.append(both[:, FULL:BINS, 0:FULL].reshape(BINS, -1))
    diag = jnp.stack([both[:, 8 * g : 8 * g + 8, 8 * g : 8 * g + 8] for g in range(8)], axis=1)
    r = jnp.arange(8)
    for s in range(5):
        at = (r[None, :] == (r[:, None] - s) % 8).astype(F32)
        if s == 0:
            at = 0.5 * at
        if s == 4:
            at = at * (r[:, None] < 4)
        parts.append((diag * at).sum(axis=3).reshape(BINS, -1))
    parts.append(jnp.stack([k[:, 64, 64], both[:, 64, 65], k[:, 65, 65]], axis=1))
    used = sum(p.shape[1] for p in parts)
    parts.append(jnp.zeros((BINS, TERMS - used), F32))
    return jnp.pad(jnp.concatenate(parts, axis=1), ((0, 80 - BINS), (0, 0))).astype(jnp.bfloat16)


def coalesce(q, sym):
    terms = pair_terms(q)
    packed = [
        jnp.concatenate(terms[2 * r : 2 * r + 2], axis=0).astype(jnp.bfloat16) for r in range(TERMS // 16)
    ]
    gained = jnp.dot(sym[...], jnp.concatenate(packed, axis=0), preferred_element_type=F32)
    return q + gained[0:BINS]


def emit(l, count, value, out, up, down):
    out[l] = value

    @pl.when(l < RUN)
    def _():
        down[l] = value

    @pl.when(l >= count - RUN)
    def _():
        up[l - (count - RUN)] = value


def upper_kernel(scal, table, spectra, courant, low, high, sym, q1, cs, side, out, up, down, q0, fy, fz, q2):
    count = scal[MID1] - scal[MID0]

    def gather(l, _):
        fetch(scal[MID0] + l, scal, spectra, courant, low, high, BINS, q0, cs, l)
        return 0

    lax.fori_loop(0, count, gather, 0)

    def first(l, _):
        position = lax.rem(l, RUN)
        back, y, z = upwind_of(table, position)
        uy, uz = y + (l - position), z + (l - position)
        ux = jnp.where(back, l - RUN, l + RUN)
        here = ((ux >= 0) & (ux < count)).astype(F32)
        ux = jnp.clip(ux, 0, count - 1)
        q_prev, cx_prev = q0[ux, :, span(3)], cs[ux, 0:1, span(3)] * here
        for v in range(4):
            s = span(v)
            q, c = q0[l, :, s], cs[l, :, s]
            new = donor(q, c, q_prev, cx_prev, q0[uy, :, s], cs[uy, :, s], q0[uz, :, s], cs[uz, :, s])
            q1[l, :, s] = new
            q_prev, cx_prev = q, c[0:1]
        other = swap(new)
        side[l] = jnp.where(upper(), limited(new, c[0:1], other), other)
        return 0

    lax.fori_loop(0, count, first, 0)
    cross_flux(count, table, q1, cs, fy, fz, 2)

    def second(l, _):
        q_prev = q1[l, :, span(1)]
        f_prev = limited(q_prev, cs[l, 0:1, span(1)], swap(q_prev))
        for v in (2, 3):
            q = q1[l, :, span(v)]
            f = limited(q, cs[l, 0:1, span(v)], swap(jnp.where(upper(), q_prev, q)))
            q2[l, :, span(v - 2)] = q - f + swap(jnp.where(upper(), f_prev, f)) + cross(table, l, fy, fz, v - 2)
            q_prev, f_prev = q, f
        return 0

    lax.fori_loop(0, count, second, 0)

    def third(l, _):
        emit(l, count, coalesce(q2[l], sym), out, up, down)
        return 0

    lax.fori_loop(0, count, third, 0)


def cross_flux(count, table, q1, cs, fy, fz, v0):
    def body(l, _):
        position = lax.rem(l, RUN)
        _, y, z = upwind_of(table, position)
        uy, uz = y + (l - position), z + (l - position)
        for w in range(2):
            s = span(v0 + w)
            q, c = q1[l, :, s], cs[l, :, s]
            before_y = step_y(jnp.where(last_y(), q1[uy, :, s], q))
            before_z = step_z(jnp.where(last_z(), q1[uz, :, s], q))
            fy[l, :, span(w)] = limited(q, c[1:2], before_y)
            fz[l, :, span(w)] = limited(q, c[2:3], before_z)
        return 0

    lax.fori_loop(0, count, body, 0)


def cross(table, l, fy, fz, w):
    position = lax.rem(l, RUN)
    _, y, z = upwind_of(table, position)
    uy, uz = y + (l - position), z + (l - position)
    s = span(w)
    y_own, z_own = fy[l, :, s], fz[l, :, s]
    y_in = step_y(jnp.where(last_y(), fy[uy, :, s], y_own))
    z_in = step_z(jnp.where(last_z(), fz[uz, :, s], z_own))
    return (y_in - y_own) + (z_in - z_own)


def upper_half(scal, table, spectra, courant, low, high, sym):
    capacity = spectra.shape[0]
    return pl.pallas_call(
        upper_kernel,
        in_specs=[SMEM, SMEM] + [VMEM] * 5,
        out_specs=[VMEM] * 6,
        out_shape=[
            jax.ShapeDtypeStruct((capacity, BINS, CELLS), F32),
            jax.ShapeDtypeStruct((capacity, 3, CELLS), F32),
            jax.ShapeDtypeStruct((capacity, BINS, LANES), F32),
            jax.ShapeDtypeStruct((capacity, BINS, HALF), F32),
            jax.ShapeDtypeStruct((RUN, BINS, HALF), F32),
            jax.ShapeDtypeStruct((RUN, BINS, HALF), F32),
        ],
        scratch_shapes=[
            pltpu.VMEM((capacity, BINS, CELLS), F32),
            pltpu.VMEM((capacity, BINS, HALF), F32),
            pltpu.VMEM((capacity, BINS, HALF), F32),
            pltpu.VMEM((capacity, BINS, HALF), F32),
        ],
        compiler_params=params(48),
        cost_estimate=pl.CostEstimate(flops=8 * 10**9, bytes_accessed=20 * 10**6, transcendentals=0),
    )(scal, table, spectra, courant, low, high, sym)


def lower_kernel(scal, table, q1_in, cs, side, below, above, sym, out, up, down, q1, fy, fz, fx, q2):
    count = scal[MID1] - scal[MID0]

    def fix(l, _):
        position = lax.rem(l, RUN)
        back, _, _ = upwind_of(table, position)
        ux = jnp.where(back, l - RUN, l + RUN)
        q1[l] = q1_in[l]

        def remote(face):
            fx[l] = face[position, 0:BINS]
            flux = face[RUN + position // 2, 0:BINS]
            flux = jnp.where(lax.rem(position, 2) == 0, flux, swap(flux))
            q1[l, :, span(0)] += jnp.where(upper(), 0.0, flux)

        @pl.when(ux < 0)
        def _():
            remote(below)

        @pl.when(ux >= count)
        def _():
            remote(above)

        @pl.when((ux >= 0) & (ux < count))
        def _():
            fx[l] = side[ux]

        return 0

    lax.fori_loop(0, count, fix, 0)
    cross_flux(count, table, q1, cs, fy, fz, 0)

    def second(l, _):
        face = fx[l]
        q = q1[l, :, span(0)]
        f = limited(q, cs[l, 0:1, span(0)], jnp.where(upper(), swap(q), face))
        q2[l, :, span(0)] = q - f + swap(jnp.where(upper(), face, f)) + cross(table, l, fy, fz, 0)
        q_prev, f_prev = q, f
        q = q1[l, :, span(1)]
        f = limited(q, cs[l, 0:1, span(1)], swap(jnp.where(upper(), q_prev, q)))
        q2[l, :, span(1)] = q - f + swap(jnp.where(upper(), f_prev, f)) + cross(table, l, fy, fz, 1)
        return 0

    lax.fori_loop(0, count, second, 0)

    def third(l, _):
        emit(l, count, coalesce(q2[l], sym), out, up, down)
        return 0

    lax.fori_loop(0, count, third, 0)


def lower_half(scal, table, q1, cs, side, below, above, sym):
    capacity = q1.shape[0]
    halved = jax.ShapeDtypeStruct((capacity, BINS, HALF), F32)
    sent = jax.ShapeDtypeStruct((RUN, BINS, HALF), F32)

    def at_zero(*dims):
        return pl.BlockSpec(dims, lambda i: (0,) * len(dims))

    return pl.pallas_call(
        lower_kernel,
        grid=(1,),
        in_specs=[
            SMEM,
            SMEM,
            at_zero(capacity, BINS, HALF),
            at_zero(capacity, 3, HALF),
            at_zero(capacity, BINS, LANES),
            VMEM,
            VMEM,
            VMEM,
        ],
        out_specs=[VMEM] * 3,
        out_shape=[halved, sent, sent],
        scratch_shapes=[pltpu.VMEM((capacity, BINS, HALF), F32)] * 3
        + [pltpu.VMEM((capacity, BINS, LANES), F32), pltpu.VMEM((capacity, BINS, HALF), F32)],
        compiler_params=params(48),
        cost_estimate=pl.CostEstimate(flops=8 * 10**9, bytes_accessed=20 * 10**6, transcendentals=0),
    )(scal, table, q1, cs, side, below, above, sym)


def place_kernel(scal, own_u, low_u, high_u, own_l, low_l, high_l, out):
    start, end = scal[MID0], scal[MID1]
    count = scal[NEW1] - scal[NEW0]

    def body(s, _):
        block = scal[NEW0] + s
        live = s < count

        def put(lower, upper_, i):
            out[s, :, 0:HALF] = lower[i]
            out[s, :, HALF:CELLS] = upper_[i]

        @pl.when(live & (block >= start) & (block < end))
        def _():
            put(own_l, own_u, block - start)

        @pl.when(live & (block < start))
        def _():
            put(low_l, low_u, block - start + RUN)

        @pl.when(live & (block >= end))
        def _():
            put(high_l, high_u, block - end)

        @pl.when(jnp.logical_not(live))
        def _():
            out[s] = jnp.zeros((BINS, CELLS), F32)

        return 0

    lax.fori_loop(0, out.shape[0], body, 0)


def place(scal, *pieces):
    capacity = pieces[0].shape[0]
    return pl.pallas_call(
        place_kernel,
        in_specs=[SMEM] + [VMEM] * 6,
        out_specs=VMEM,
        out_shape=jax.ShapeDtypeStruct((capacity, BINS, CELLS), F32),
        compiler_params=params(32),
    )(scal, *pieces)


def bounds(device, devices, old_count, new_count):
    ids = jnp.arange(devices, dtype=jnp.int32)
    counts = jnp.stack([old_count, new_count])

    def start(p):
        old, new = jnp.sum(jnp.where(ids < p, counts, 0), axis=1)
        least = (jnp.maximum(old, new) - RUN + RUN - 1 + RUN) // RUN * RUN - RUN
        most = (jnp.minimum(old, new) + RUN) // RUN * RUN
        return old, jnp.clip(2 * RUN * p, least, most), new

    old0, mid0, new0 = start(device)
    old1, mid1, new1 = start(device + 1)
    return jnp.stack([old0, old1, mid0, mid1, new0, new1]).astype(jnp.int32)


def on_device(devices, spectra, courant, kernel, old_count, new_count, upwind):
    device = lax.axis_index("blocks").astype(jnp.int32)
    rise = [(i, i + 1) for i in range(devices - 1)]
    fall = [(i + 1, i) for i in range(devices - 1)]
    around = [(i, (i + 1) % devices) for i in range(devices)]
    reverse = [(j, i) for i, j in around]

    def move(block, route):
        return lax.ppermute(block, "blocks", route)

    tail_start = lax.dynamic_slice(old_count, (device,), (1,)) - RUN
    tail, head = pack(spectra, courant, tail_start)
    low, high = move(tail, rise), move(head, fall)
    scal = bounds(device, devices, old_count, new_count)
    table = upwind[RUN : 2 * RUN].reshape(-1)
    sym = symmetric_kernel(kernel)
    up, down = faces(scal, table, spectra, courant, low, high)
    below, above = move(up, around), move(down, reverse)
    q1, cs, side, own_u, up_u, down_u = upper_half(scal, table, spectra, courant, low, high, sym)
    low_u, high_u = move(up_u, rise), move(down_u, fall)
    own_l, up_l, down_l = lower_half(scal, table, q1, cs, side, below, above, sym)
    low_l, high_l = move(up_l, rise), move(down_l, fall)
    return place(scal, own_u, low_u, high_u, own_l, low_l, high_l)


def solution(mesh):
    in_specs = (P("blocks", None, None), P("blocks", None, None), P(), P(), P(), P())
    out_specs = P("blocks", None, None)
    return jax.shard_map(
        functools.partial(on_device, mesh.shape["blocks"]),
        mesh=mesh,
        in_specs=in_specs,
        out_specs=out_specs,
        check_vma=False,
    )
```

time: 523 us -> 218 us (0.42); the launches traced: 513 us -> 216 us
  matrix products: 210 us -> 0 us
  other arithmetic: 104 us -> 12.2 us
  Pallas kernels: 0 us -> 70.4 us
  local copies, waits for them, and re-layouts: 142 us -> 81.3 us
  starting transfers between devices: 10.9 us -> 29.9 us
  waiting for transfers between devices: 34.5 us -> 16.6 us
    dot_general x39 -> x0, matrix products: 210 us -> none  [the longest x9 93.1 us: put_layer(): jnp.einsum('sbf,cf->sbc', face_values, table, precision=lax.Precision.HIG...]
    pallas_call x0 -> x5, Pallas kernels: none -> 70.4 us  [the longest x1 33.5 us: upper_half(): pl.pallas_call(upper_kernel, in_specs=[SMEM, SMEM] + [VMEM] * 5, out_spec...]
    convert_element_type x18 -> x3, other arithmetic: 60.7 us -> 1.94 us  [the longest x2 1.4 us: symmetric_kernel(): at = (r[None, :] == (r[:, None] - s) % 8).astype(F32)]
    gather x5 -> x0, local copies, waits for them, and re-layouts: 29.1 us -> none  [the longest x4 22.3 us: gather_faces(): face_pool[pool_index, jnp.arange(face_kinds, dtype=jnp.int32)[None, :]]]
    concatenate x6 -> x0, other arithmetic: 21.1 us -> none  [the longest x2 8.64 us: gather_faces(): face_pool = jnp.concatenate([from_prev, payload, from_next], axis=0)]
    ppermute x6 -> x8, starting transfers between devices: 10.9 us -> 29.9 us  [move(): return lax.ppermute(block, 'blocks', route)]
    ppermute x6 -> x8, waiting for transfers between devices: 34.5 us -> 16.6 us  [move(): return lax.ppermute(block, 'blocks', route)]
    squeeze x18 -> x0, local copies, waits for them, and re-layouts: 17.7 us -> none  [on_device(): coalesced = lax.map(coalesce, grouped).reshape(capacity, BINS, CELLS)]
  transfers between devices with their start and end apart: 6 -> 8, of which waited for: 5 -> 2; matrix products, arithmetic and copies ran while one was open for 5% -> 38% of each run, Pallas kernels for 0% -> 26%
where the time goes in v1:
time: 218 us; the launch traced here: 216 us
  local copies, waits for them, and re-layouts  81.3 us (37%)
  Pallas kernels  70.4 us (32%)
  starting transfers between devices  29.9 us (14%)
  waiting for transfers between devices  16.6 us (8%)
  other arithmetic  12.2 us (6%)
  between operations  5.67 us (3%)
    pallas_call x1, Pallas kernels, upper_half(): pl.pallas_call(upper_kernel, in_specs=[SMEM, SMEM] + [VMEM] * 5, out_spec...  33.5 us
    ppermute x8, starting transfers between devices, move(): return lax.ppermute(block, 'blocks', route)  29.9 us
    pallas_call x1, Pallas kernels, lower_half(): pl.pallas_call(lower_kernel, grid=(1,), in_specs=[SMEM, SMEM, at_zero(cap...  23 us
    unnamed x24, local copies, waits for them, and re-layouts  21.1 us
    slice x12, local copies, waits for them, and re-layouts, symmetric_kernel(): both[:, 8 * g:8 * g + 8, 8 * g + 8:FULL].reshape(BINS, -1)  16.9 us
    ppermute x8, waiting for transfers between devices, move(): return lax.ppermute(block, 'blocks', route)  16.6 us
    another operation x10, local copies, waits for them, and re-layouts, symmetric_kernel(): jnp.stack([both[:, 8 * g:8 * g + 8, 8 * g:8 * g + 8] for g in range(8)],...  15.8 us
    reshape x5, local copies, waits for them, and re-layouts, symmetric_kernel(): parts.append((diag * at).sum(axis=3).reshape(BINS, -1))  7.07 us
  transfers between devices with their start and end apart: 8, of which 2 were waited for; matrix products, arithmetic and copies ran while one was open for 38% of the time, Pallas kernels for 26%

profile of v1, /device:TPU:111, one launch (start us, length us, event | category | flops | bytes accessed | tf_op | source)
XLA Modules:
  0.0 216.2 jit_solution(15229039652105746062)
XLA Ops:
  3.0 2.5 %copy-done = f32[36,66,512]{2,1,0:T(8,128)S(1)} copy-done((f32[36,66,512]{2,1,0:T(8,128)S(1)}, f32[36,66,512]{2,1,0:T(8,128)}, u32[]{:S(2)}) %copy-start) | copy-done | bytes 4866072
  5.5 4.6 %shard_map.64 = (f32[12,72,512]{2,1,0:T(8,128)}, f32[12,72,512]{2,1,0:T(8,128)}) custom-call(s32[1]{0:T(128)S(6)} %sub.44.scal, f32[36,66,512]{2,1,0:T(8,128)S(1)} %copy-done, f32[36,3,512]{2,1,0:T(4,128)S(1)} %copy.179.tail_c.head_c.courant, f32[36,66,512]{2,1,0:T(8,128)S(1)} %copy-done, f32[36,3,512]{2,1,0:T(4,128)S(1)} %copy.179.tail_c.head_c.courant), custom_call_target="tpu_custom_call" | custom-call | tf_op jit(solution)/shard_map/pallas_call | solution.py:117
  10.1 2.3 %collective-permute-start = (f32[12,72,512]{2,1,0:T(8,128)}, f32[12,72,512]{2,1,0:T(8,128)S(1)}, u32[]{:S(2)}, u32[]{:S(2)}) collective-permute-start(f32[12,72,512]{2,1,0:T(8,128)} %get-tuple-element.18), channel_id=1, source_target_pairs={{0,1},{1,2},{2,3},{3,4},{4,5},{5,6},{6,7},{7,8},{8,9},{9,10},{10,1... | collective-permute-start | bytes 5308424 | tf_op jit(solution)/shard_map/ppermute | solution.py:497
  12.4 2.2 %collective-permute-start.1 = (f32[12,72,512]{2,1,0:T(8,128)}, f32[12,72,512]{2,1,0:T(8,128)}, u32[]{:S(2)}, u32[]{:S(2)}) collective-permute-start(f32[12,72,512]{2,1,0:T(8,128)} %get-tuple-element.19), channel_id=1, source_target_pairs={{1,0},{2,1},{3,2},{4,3},{5,4},{6,5},{7,6},{8,7},{9,8},{10,9},{11,1... | collective-permute-start | bytes 5308424 | tf_op jit(solution)/shard_map/ppermute | solution.py:497
  18.3 2.3 %reshape.332 = bf16[66,66,66]{2,1,0:T(8,128)(2,1)S(1)} reshape(bf16[66,4356]{1,0:T(8,128)(2,1)} %param.8) | data formatting | bytes 1149984 | tf_op jit(solution)/shard_map/reshape | solution.py:206
  20.6 1.9 copy.142
  22.5 3.0 %fusion.9 = (bf16[66,66,66]{2,1,0:T(8,128)(2,1)}, f32[66,66,66]{2,1,0:T(8,128)S(1)}) fusion(f32[66,66,66]{1,2,0:T(8,128)} %copy.142, bf16[66,66,66]{2,1,0:T(8,128)(2,1)S(1)} %reshape.332), kind=kLoop, calls=%fused_computation.63 | loop fusion | flops 862488 | bytes 3449952 | tf_op jit(solution)/shard_map/convert.46
  25.5 1.8 slice_bitcast_fusion
  27.3 1.7 copy.151
  88.7 2.0 multiply_reduce_fusion
  99.1 2.4 %stack.50.scal = s32[6]{0:T(128)S(1)} concatenate(s32[1]{0:T(128)} %get-tuple-element.54, s32[1]{0:T(128)} %get-tuple-element.51, s32[1]{0:T(128)} %bitcast.6, s32[1]{0:T(128)} %bitcast.11, s32[1]{0:T(128)} %get-tuple-element.55, s32[1]{0:T(128)} %get-tuple-element.50), dimensions={0} | concatenate | bytes 48 | tf_op jit(solution)/shard_map/stack | solution.py:486
  101.6 2.5 %copy-done.1 = f32[36,66,512]{2,1,0:T(8,128)S(1)} copy-done((f32[36,66,512]{2,1,0:T(8,128)S(1)}, f32[36,66,512]{2,1,0:T(8,128)}, u32[]{:S(2)}) %copy-start.1) | copy-done | bytes 4866072
  104.1 5.0 %shard_map.66 = (f32[18,72,128]{2,1,0:T(8,128)S(1)}, f32[18,72,128]{2,1,0:T(8,128)S(1)}) custom-call(s32[6]{0:T(128)S(1)} %stack.50.scal, s32[36]{0:T(128)S(1)} %reshape.331.table, f32[36,66,512]{2,1,0:T(8,128)S(1)} %copy-done.1, f32[36,3,512]{2,1,0:T(4,128)S(1)} %copy.179.tail_c.head_c.courant, f32[12,72,512]{2,1,0:T(8,128)S(1)} %collective-permute-done.low, ...), custom_call_target="tpu_custom_call" | custom-call | tf_op jit(solution)/shard_map/pallas_call | solution.py:173
  109.1 5.8 %collective-permute-start.4 = (f32[18,72,128]{2,1,0:T(8,128)S(1)}, f32[18,72,128]{2,1,0:T(8,128)S(1)}, u32[]{:S(2)}, u32[]{:S(2)}) collective-permute-start(f32[18,72,128]{2,1,0:T(8,128)S(1)} %get-tuple-element.26), channel_id=1, source_target_pairs={{0,1},{1,2},{2,3},{3,4},{4,5},{5,6},{6,7},{7,8},{8,9},{9,10},{10,1... | collective-permute-start | bytes 1990664 | tf_op jit(solution)/shard_map/ppermute | solution.py:497
  114.9 33.5 %shard_map.65 = (f32[36,66,512]{2,1,0:T(8,128)}, f32[36,3,512]{2,1,0:T(4,128)S(1)}, f32[36,66,128]{2,1,0:T(8,128)S(1)}, f32[36,66,256]{2,1,0:T(8,128)}, f32[12,6...) custom-call(s32[6]{0:T(128)S(1)} %stack.50.scal, s32[36]{0:T(128)S(1)} %reshape.331.table, f32[36,66,512]{2,1,0:T(8,128)} %spectra.3, ...), custom_call_target="tpu_custom_call" | custom-call | flops 8000000000 | bytes 20000000 | tf_op jit(solution)/shard_map/pallas_call | solution.py:325
  149.5 7.9 %collective-permute-start.2 = (f32[12,66,256]{2,1,0:T(8,128)S(1)}, f32[12,66,256]{2,1,0:T(8,128)S(1)}, u32[]{:S(2)}, u32[]{:S(2)}) collective-permute-start(f32[12,66,256]{2,1,0:T(8,128)S(1)} %get-tuple-element.21), channel_id=1, source_target_pairs={{0,1},{1,2},{2,3},{3,4},{4,5},{5,6},{6,7},{7,8},{8,9},{9,10},{10,1... | collective-permute-start | bytes 2433032 | tf_op jit(solution)/shard_map/ppermute | solution.py:497
  157.4 1.9 collective-permute-start.3
  160.7 23.0 %shard_map.67 = (f32[36,66,256]{2,1,0:T(8,128)}, f32[12,66,256]{2,1,0:T(8,128)S(1)}, f32[12,66,256]{2,1,0:T(8,128)S(1)}) custom-call(s32[6]{0:T(128)S(1)} %stack.50.scal, s32[36]{0:T(128)S(1)} %reshape.331.table, f32[36,66,512]{2,1,0:T(8,128)} %get-tuple-element.23.q1_in, f32[36,3,512]{2,1,0:T(4,128)S(1)} %get-tuple-element.24.cs, ...), custom_call_target="tpu_custom_call" | custom-call | flops 8000000000 | bytes 20000000 | tf_op jit(solution)/shard_map/pallas_call | solution.py:408
  183.6 7.8 %collective-permute-start.6 = (f32[12,66,256]{2,1,0:T(8,128)S(1)}, f32[12,66,256]{2,1,0:T(8,128)S(1)}, u32[]{:S(2)}, u32[]{:S(2)}) collective-permute-start(f32[12,66,256]{2,1,0:T(8,128)S(1)} %get-tuple-element.29), channel_id=1, source_target_pairs={{0,1},{1,2},{2,3},{3,4},{4,5},{5,6},{6,7},{7,8},{8,9},{9,10},{10,1... | collective-permute-start | bytes 2433032 | tf_op jit(solution)/shard_map/ppermute | solution.py:497
  191.5 1.9 collective-permute-start.7
  193.4 8.0 %collective-permute-done.6.low_l = f32[12,66,256]{2,1,0:T(8,128)S(1)} collective-permute-done((f32[12,66,256]{2,1,0:T(8,128)S(1)}, f32[12,66,256]{2,1,0:T(8,128)S(1)}, u32[]{:S(2)}, u32[]{:S(2)}) %collective-permute-start.6) | collective-permute-done | bytes 811040 | tf_op jit(solution)/shard_map/ppermute | solution.py:497
  201.5 8.6 %collective-permute-done.7.high_l = f32[12,66,256]{2,1,0:T(8,128)S(1)} collective-permute-done((f32[12,66,256]{2,1,0:T(8,128)S(1)}, f32[12,66,256]{2,1,0:T(8,128)S(1)}, u32[]{:S(2)}, u32[]{:S(2)}) %collective-permute-start.7) | collective-permute-done | bytes 811040 | tf_op jit(solution)/shard_map/ppermute | solution.py:497
  210.1 1.7 copy-done.3
  211.8 4.3 %shard_map.68 = f32[36,66,512]{2,1,0:T(8,128)} custom-call(s32[6]{0:T(128)S(1)} %stack.50.scal, f32[36,66,256]{2,1,0:T(8,128)S(1)} %copy-done.2, f32[12,66,256]{2,1,0:T(8,128)S(1)} %collective-permute-done.2.low_u, f32[12,66,256]{2,1,0:T(8,128)S(1)} %collective-permute-done.3.high_u, f32[36,66,256]{2,1,0:T(8,128)S(1)} %copy-done.3, ...), custom_call_target="tpu_custom_call" | custom-call | tf_op jit(solution)/shard_map/pallas_call | solution.py:465
  (84 shorter events, 71.6 us)
Async XLA Ops:
  3.0 2.5 %copy-start = (f32[36,66,512]{2,1,0:T(8,128)S(1)}, f32[36,66,512]{2,1,0:T(8,128)}, u32[]{:S(2)}) copy-start(f32[36,66,512]{2,1,0:T(8,128)} %spectra.3) | copy-start | bytes 14598148
  10.1 91.5 %collective-permute-start = (f32[12,72,512]{2,1,0:T(8,128)}, f32[12,72,512]{2,1,0:T(8,128)S(1)}, u32[]{:S(2)}, u32[]{:S(2)}) collective-permute-start(f32[12,72,512]{2,1,0:T(8,128)} %get-tuple-element.18), channel_id=1, source_target_pairs={{0,1},{1,2},{2,3},{3,4},{4,5},{5,6},{6,7},{7,8},{8,9},{9,10},{10,1... | collective-permute-start | bytes 5308424 | tf_op jit(solution)/shard_map/ppermute | solution.py:497
  12.4 89.2 %collective-permute-start.1 = (f32[12,72,512]{2,1,0:T(8,128)}, f32[12,72,512]{2,1,0:T(8,128)}, u32[]{:S(2)}, u32[]{:S(2)}) collective-permute-start(f32[12,72,512]{2,1,0:T(8,128)} %get-tuple-element.19), channel_id=1, source_target_pairs={{1,0},{2,1},{3,2},{4,3},{5,4},{6,5},{7,6},{8,7},{9,8},{10,9},{11,1... | collective-permute-start | bytes 5308424 | tf_op jit(solution)/shard_map/ppermute | solution.py:497
  25.5 9.9 %copy-start.6 = (s32[128]{0:T(128)S(1)}, s32[128]{0:T(128)}, u32[]{:S(2)}) copy-start(s32[128]{0:T(128)} %param.10) | copy-start | bytes 1540
  101.6 2.5 %copy-start.1 = (f32[36,66,512]{2,1,0:T(8,128)S(1)}, f32[36,66,512]{2,1,0:T(8,128)}, u32[]{:S(2)}) copy-start(f32[36,66,512]{2,1,0:T(8,128)} %spectra.3) | copy-start | bytes 14598148
  109.1 50.2 %collective-permute-start.4 = (f32[18,72,128]{2,1,0:T(8,128)S(1)}, f32[18,72,128]{2,1,0:T(8,128)S(1)}, u32[]{:S(2)}, u32[]{:S(2)}) collective-permute-start(f32[18,72,128]{2,1,0:T(8,128)S(1)} %get-tuple-element.26), channel_id=1, source_target_pairs={{0,1},{1,2},{2,3},{3,4},{4,5},{5,6},{6,7},{7,8},{8,9},{9,10},{10,1... | collective-permute-start | bytes 1990664 | tf_op jit(solution)/shard_map/ppermute | solution.py:497
  114.9 44.4 %collective-permute-start.5 = (f32[18,72,128]{2,1,0:T(8,128)S(1)}, f32[18,72,128]{2,1,0:T(8,128)S(1)}, u32[]{:S(2)}, u32[]{:S(2)}) collective-permute-start(f32[18,72,128]{2,1,0:T(8,128)S(1)} %get-tuple-element.27), channel_id=1, source_target_pairs={{1,0},{2,1},{3,2},{4,3},{5,4},{6,5},{7,6},{8,7},{9,8},{10,9},{11,1... | collective-permute-start | bytes 1990664 | tf_op jit(solution)/shard_map/ppermute | solution.py:497
  148.4 1.1 copy-start.4
  149.5 44.0 %collective-permute-start.2 = (f32[12,66,256]{2,1,0:T(8,128)S(1)}, f32[12,66,256]{2,1,0:T(8,128)S(1)}, u32[]{:S(2)}, u32[]{:S(2)}) collective-permute-start(f32[12,66,256]{2,1,0:T(8,128)S(1)} %get-tuple-element.21), channel_id=1, source_target_pairs={{0,1},{1,2},{2,3},{3,4},{4,5},{5,6},{6,7},{7,8},{8,9},{9,10},{10,1... | collective-permute-start | bytes 2433032 | tf_op jit(solution)/shard_map/ppermute | solution.py:497
  157.4 36.0 %collective-permute-start.3 = (f32[12,66,256]{2,1,0:T(8,128)S(1)}, f32[12,66,256]{2,1,0:T(8,128)S(1)}, u32[]{:S(2)}, u32[]{:S(2)}) collective-permute-start(f32[12,66,256]{2,1,0:T(8,128)S(1)} %get-tuple-element.22), channel_id=1, source_target_pairs={{1,0},{2,1},{3,2},{4,3},{5,4},{6,5},{7,6},{8,7},{9,8},{10,9},{11,1... | collective-permute-start | bytes 2433032 | tf_op jit(solution)/shard_map/ppermute | solution.py:497
  159.3 1.3 copy-start.5
  160.7 49.4 %copy-start.2 = (f32[36,66,256]{2,1,0:T(8,128)S(1)}, f32[36,66,256]{2,1,0:T(8,128)}, u32[]{:S(2)}) copy-start(f32[36,66,256]{2,1,0:T(8,128)} %get-tuple-element.20.own_u) | copy-start | bytes 7299076
  183.6 17.8 %collective-permute-start.6 = (f32[12,66,256]{2,1,0:T(8,128)S(1)}, f32[12,66,256]{2,1,0:T(8,128)S(1)}, u32[]{:S(2)}, u32[]{:S(2)}) collective-permute-start(f32[12,66,256]{2,1,0:T(8,128)S(1)} %get-tuple-element.29), channel_id=1, source_target_pairs={{0,1},{1,2},{2,3},{3,4},{4,5},{5,6},{6,7},{7,8},{8,9},{9,10},{10,1... | collective-permute-start | bytes 2433032 | tf_op jit(solution)/shard_map/ppermute | solution.py:497
  191.5 18.6 %collective-permute-start.7 = (f32[12,66,256]{2,1,0:T(8,128)S(1)}, f32[12,66,256]{2,1,0:T(8,128)S(1)}, u32[]{:S(2)}, u32[]{:S(2)}) collective-permute-start(f32[12,66,256]{2,1,0:T(8,128)S(1)} %get-tuple-element.30), channel_id=1, source_target_pairs={{1,0},{2,1},{3,2},{4,3},{5,4},{6,5},{7,6},{8,7},{9,8},{10,9},{11,1... | collective-permute-start | bytes 2433032 | tf_op jit(solution)/shard_map/ppermute | solution.py:497
  210.1 1.8 copy-start.3

commit v2 on v1

v2 whole, which is shorter than its diff:
```python
import functools

import jax
import jax.numpy as jnp
import numpy as np
from jax import lax
from jax.experimental import pallas as pl
from jax.experimental.pallas import tpu as pltpu
from jax.sharding import PartitionSpec as P

RUN = 12
BINS = 66
CELLS = 512
HALF = 256
LANES = 128
PACKED = 72
FULL = 64
TERMS = 2304
GROUPS = 9
FACES = 18
F32 = jnp.float32
VMEM = pl.BlockSpec(memory_space=pltpu.VMEM)
SMEM = pl.BlockSpec(memory_space=pltpu.SMEM)
OLD0, OLD1, MID0, MID1, NEW0, NEW1 = range(6)


def params(mib):
    return pltpu.CompilerParams(vmem_limit_bytes=mib * 2**20)


def lanes():
    return lax.broadcasted_iota(jnp.int32, (8, LANES), 1)


def span(v):
    return slice(v * LANES, (v + 1) * LANES)


def upper():
    return lanes() >= 64


def last_y():
    return lanes() // 8 % 8 == 7


def last_z():
    return lanes() % 8 == 7


def view(x):
    return x.reshape(GROUPS, 8, LANES)


def flat(x):
    return x.reshape(PACKED, LANES)


def swap(x):
    return pltpu.roll(flat(x), 64, 1).reshape(x.shape)


def permuted(x, source):
    return view(jnp.take_along_axis(flat(x), source, axis=1))


def wide_lanes():
    return lax.broadcasted_iota(jnp.int32, (PACKED, LANES), 1)


def step_y(x):
    at = wide_lanes()
    return permuted(x, jnp.where(at // 8 % 8 == 0, at + 56, at - 8))


def step_z(x):
    at = wide_lanes()
    return permuted(x, jnp.where(at % 8 == 0, at + 7, at - 1))


def minmod(a, e):
    return jnp.maximum(jnp.minimum(a, e), 0.0) + jnp.minimum(jnp.maximum(a, e), 0.0)


def limited(q, c, before):
    return c * (q + (0.5 * (1.0 - c)) * minmod(q - before, q))


def upwind_of(table, position):
    back = table[3 * position] < RUN + position
    return back, table[3 * position + 1] - RUN, table[3 * position + 2] - RUN


def read(ref, l, v):
    return view(ref[l, :, span(v)])


def speed(ref, l, d, v):
    return ref[l, 8 * d : 8 * d + 8, span(v)]


def donor(q0, cs, l, v, q_prev, cx_prev, uy, uz):
    q, cx, cy, cz = read(q0, l, v), speed(cs, l, 0, v), speed(cs, l, 1, v), speed(cs, l, 2, v)
    up, ly, lz = upper(), last_y(), last_z()
    in_x = swap(jnp.where(up, cx_prev, cx) * jnp.where(up, q_prev, q))
    in_y = step_y(jnp.where(ly, speed(cs, uy, 1, v), cy) * jnp.where(ly, read(q0, uy, v), q))
    in_z = step_z(jnp.where(lz, speed(cs, uz, 2, v), cz) * jnp.where(lz, read(q0, uz, v), q))
    return (1.0 - (cx + cy + cz)) * q + in_x + in_y + in_z


def fetch(block, scal, spectra, courant, low, high, q_dst, c_dst, at):
    own0, own1 = scal[OLD0], scal[OLD1]

    def spread(ref, i, row):
        for d in range(3):
            c_dst[at, 8 * d : 8 * d + 8] = jnp.broadcast_to(
                ref[i, row + d : row + d + 1], (8,) + ref.shape[2:]
            )

    @pl.when((block >= own0) & (block < own1))
    def _():
        q_dst[at, 0:BINS] = spectra[block - own0]
        spread(courant, block - own0, 0)

    def received(ref, i):
        q_dst[at] = ref[i]
        spread(ref, i, BINS)

    @pl.when(block < own0)
    def _():
        received(low, block - own0 + RUN)

    @pl.when(block >= own1)
    def _():
        received(high, block - own1)


def pack_kernel(scal, tail_q, tail_c, head_q, head_c, up, down):
    pad = jnp.zeros((1, PACKED - BINS - 3, CELLS), F32)
    up[...] = jnp.concatenate([tail_q[...], tail_c[...], pad], axis=1)
    down[...] = jnp.concatenate([head_q[...], head_c[...], pad], axis=1)


def pack(spectra, courant, tail_start):
    def tail(i, scal):
        return (scal[0] + i, 0, 0)

    def head(i, scal):
        return (i, 0, 0)

    return pl.pallas_call(
        pack_kernel,
        grid_spec=pltpu.PrefetchScalarGridSpec(
            num_scalar_prefetch=1,
            grid=(RUN,),
            in_specs=[
                pl.BlockSpec((1, BINS, CELLS), tail),
                pl.BlockSpec((1, 3, CELLS), tail),
                pl.BlockSpec((1, BINS, CELLS), head),
                pl.BlockSpec((1, 3, CELLS), head),
            ],
            out_specs=[pl.BlockSpec((1, PACKED, CELLS), head)] * 2,
        ),
        out_shape=[jax.ShapeDtypeStruct((RUN, PACKED, CELLS), F32)] * 2,
        compiler_params=params(24),
    )(tail_start, spectra, courant, spectra, courant)


def face_kernel(scal, table, spectra, courant, low, high, up, down, q0, cs):
    count = scal[MID1] - scal[MID0]

    def gather(j, _):
        first = scal[MID0] + jnp.where(j < RUN, j, count - 2 * RUN + j)
        fetch(first, scal, spectra, courant, low, high, q0, cs, j)
        return 0

    lax.fori_loop(0, 2 * RUN, gather, 0)

    def face(j, position):
        _, y, z = upwind_of(table, position)
        uy, uz = y + (j - position), z + (j - position)
        q1 = donor(q0, cs, j, 1, read(q0, j, 0), speed(cs, j, 0, 0), uy, uz)
        other = swap(q1)
        c = speed(cs, j, 0, 1)
        return jnp.where(upper(), limited(q1, c, other), other), c * read(q0, j, 1)

    for base, out in ((0, down), (RUN, up)):

        def pair(i, _, base=base, out=out):
            a0, b0 = face(base + 2 * i, 2 * i)
            a1, b1 = face(base + 2 * i + 1, 2 * i + 1)
            out[2 * i] = flat(a0)
            out[2 * i + 1] = flat(a1)
            out[RUN + i] = flat(jnp.where(upper(), b1, swap(b0)))
            return 0

        lax.fori_loop(0, RUN // 2, pair, 0)


def faces(scal, table, spectra, courant, low, high):
    capacity = spectra.shape[0]

    def half(*dims):
        return pl.BlockSpec(dims + (HALF,), lambda i: (0, 0, 1))

    return pl.pallas_call(
        face_kernel,
        grid=(1,),
        in_specs=[
            SMEM,
            SMEM,
            half(capacity, BINS),
            half(capacity, 3),
            half(RUN, PACKED),
            half(RUN, PACKED),
        ],
        out_specs=[VMEM] * 2,
        out_shape=[jax.ShapeDtypeStruct((FACES, PACKED, LANES), F32)] * 2,
        scratch_shapes=[pltpu.VMEM((2 * RUN, PACKED, HALF), F32), pltpu.VMEM((2 * RUN, 24, HALF), F32)],
        compiler_params=params(24),
    )(scal, table, spectra, courant, low, high)


def pair_terms(q):
    wide = q.shape[1]
    group = [q[8 * g : 8 * g + 8, :] for g in range(8)]
    row = [jnp.broadcast_to(q[i : i + 1, :], (8, wide)) for i in range(BINS)]
    out = [row[i] * group[g] for i in range(56) for g in range(i // 8 + 1, 8)]
    out += [row[i] * group[g] for i in (64, 65) for g in range(8)]
    for s in range(5):
        out += [x * (pltpu.roll(x, s, 0) if s else x) for x in group]
    at = lax.broadcasted_iota(jnp.int32, (8, wide), 0)
    rest = jnp.where(at < 2, row[64], row[65]) * jnp.where(at < 1, row[64], row[65])
    out.append(jnp.where(at < 3, rest, 0.0))
    return out + [jnp.zeros((8, wide), F32)] * (TERMS // 8 - len(out))


def pair_columns():
    pairs = [(i, j) for i in range(56) for j in range(i // 8 * 8 + 8, FULL)]
    pairs += [(i, j) for i in (64, 65) for j in range(FULL)]
    for s in range(5):
        for g in range(0, FULL, 8):
            pairs += [(g + r, g + (r - s) % 8) if s < 4 or r < 4 else None for r in range(8)]
    pairs += [(64, 64), (64, 65), (65, 65)]
    pairs += [None] * (TERMS - len(pairs))
    one = [p[0] * BINS + p[1] if p else -1 for p in pairs]
    two = [p[1] * BINS + p[0] if p and p[0] != p[1] else -1 for p in pairs]
    return np.array([one, two], np.int32)


def symmetric_kernel_body(columns, kernel, out):
    width = out.shape[1]
    one, two = columns[0:1], columns[1:2]

    def chunk(i, total):
        base = pl.multiple_of(i * 256, 256)
        row = lax.broadcasted_iota(jnp.int32, (256, width), 0) + base
        pick = jnp.where((row == one) | (row == two), 1.0, 0.0).astype(jnp.bfloat16)
        return total + jnp.dot(kernel[:, pl.ds(base, 256)], pick, preferred_element_type=F32)

    total = lax.fori_loop(0, kernel.shape[1] // 256, chunk, jnp.zeros((80, width), F32))
    out[...] = total.astype(jnp.bfloat16)


def symmetric_kernel(kernel):
    wide = -(-kernel.shape[1] // 256) * 256
    padded = jnp.pad(kernel, ((0, 80 - BINS), (0, wide - kernel.shape[1])))
    return pl.pallas_call(
        symmetric_kernel_body,
        grid=(TERMS // 256,),
        in_specs=[
            pl.BlockSpec((2, 256), lambda i: (0, i)),
            pl.BlockSpec((80, wide), lambda i: (0, 0)),
        ],
        out_specs=pl.BlockSpec((80, 256), lambda i: (0, i)),
        out_shape=jax.ShapeDtypeStruct((80, TERMS), jnp.bfloat16),
        compiler_params=params(16),
        cost_estimate=pl.CostEstimate(flops=2 * 10**9, bytes_accessed=10**6, transcendentals=0),
    )(jnp.asarray(pair_columns()), padded)


def coalesce(q, sym):
    terms = pair_terms(q)
    packed = [
        jnp.concatenate(terms[2 * r : 2 * r + 2], axis=0).astype(jnp.bfloat16) for r in range(TERMS // 16)
    ]
    gained = jnp.dot(sym[...], jnp.concatenate(packed, axis=0), preferred_element_type=F32)
    return q + gained[0:PACKED]


def neighbours(table, l):
    position = lax.rem(l, RUN)
    back, y, z = upwind_of(table, position)
    return jnp.where(back, l - RUN, l + RUN), y + (l - position), z + (l - position)


def cross_flux(count, table, q1, cs, fy, fz, v0, vf):
    def cross_body(l, _):
        _, uy, uz = neighbours(table, l)
        for w in range(2):
            q = read(q1, l, v0 + w)
            before_y = step_y(jnp.where(last_y(), read(q1, uy, v0 + w), q))
            before_z = step_z(jnp.where(last_z(), read(q1, uz, v0 + w), q))
            fy[l, :, span(w)] = flat(limited(q, speed(cs, l, 1, vf + w), before_y))
            fz[l, :, span(w)] = flat(limited(q, speed(cs, l, 2, vf + w), before_z))
        return 0

    lax.fori_loop(0, count, cross_body, 0)


def cross(table, l, fy, fz, w):
    _, uy, uz = neighbours(table, l)
    y_own, z_own = read(fy, l, w), read(fz, l, w)
    y_in = step_y(jnp.where(last_y(), read(fy, uy, w), y_own))
    z_in = step_z(jnp.where(last_z(), read(fz, uz, w), z_own))
    return (y_in - y_own) + (z_in - z_own)


def finish(count, second, q2, sym, out, up, down):
    second(0)

    def third(l, _):
        out[l] = coalesce(q2[l], sym)[0:BINS]
        second(jnp.minimum(l + 1, count - 1))
        return 0

    lax.fori_loop(0, count, third, 0)

    def hand_on(k, _):
        down[k] = out[k]
        up[k] = out[count - RUN + k]
        return 0

    lax.fori_loop(0, RUN, hand_on, 0)


def upper_kernel(scal, table, spectra, courant, low, high, sym, low_q1, low_c, side, out, up, down, q0, cs, q1, fy, fz, q2):
    count = scal[MID1] - scal[MID0]

    def gather(l, _):
        fetch(scal[MID0] + l, scal, spectra, courant, low, high, q0, cs, l)
        low_c[l] = cs[l, :, 0:HALF]
        return 0

    lax.fori_loop(0, count, gather, 0)

    def first(l, _):
        ux, uy, uz = neighbours(table, l)
        here = ((ux >= 0) & (ux < count)).astype(F32)
        ux = jnp.clip(ux, 0, count - 1)
        q_prev, cx_prev = read(q0, ux, 3), speed(cs, ux, 0, 3) * here
        for v in range(4):
            new = donor(q0, cs, l, v, q_prev, cx_prev, uy, uz)
            q_prev, cx_prev = read(q0, l, v), speed(cs, l, 0, v)
            if v < 2:
                low_q1[l, :, span(v)] = flat(new)
            else:
                q1[l, :, span(v - 2)] = flat(new)
        other = swap(new)
        side[l] = flat(jnp.where(upper(), limited(new, cx_prev, other), other))
        return 0

    lax.fori_loop(0, count, first, 0)
    cross_flux(count, table, q1, cs, fy, fz, 0, 2)

    def second(l):
        q_prev = read(low_q1, l, 1)
        f_prev = limited(q_prev, speed(cs, l, 0, 1), swap(q_prev))
        for w in range(2):
            q = read(q1, l, w)
            f = limited(q, speed(cs, l, 0, w + 2), swap(jnp.where(upper(), q_prev, q)))
            new = q - f + swap(jnp.where(upper(), f_prev, f)) + cross(table, l, fy, fz, w)
            q2[l, :, span(w)] = flat(new)
            q_prev, f_prev = q, f

    finish(count, second, q2, sym, out, up, down)


def upper_half(scal, table, spectra, courant, low, high, sym):
    capacity = spectra.shape[0]
    held = pltpu.VMEM((capacity, PACKED, HALF), F32)
    return pl.pallas_call(
        upper_kernel,
        in_specs=[SMEM, SMEM] + [VMEM] * 5,
        out_specs=[VMEM] * 6,
        out_shape=[
            jax.ShapeDtypeStruct((capacity, PACKED, HALF), F32),
            jax.ShapeDtypeStruct((capacity, 24, HALF), F32),
            jax.ShapeDtypeStruct((capacity, PACKED, LANES), F32),
            jax.ShapeDtypeStruct((capacity, BINS, HALF), F32),
            jax.ShapeDtypeStruct((RUN, BINS, HALF), F32),
            jax.ShapeDtypeStruct((RUN, BINS, HALF), F32),
        ],
        scratch_shapes=[
            pltpu.VMEM((capacity, PACKED, CELLS), F32),
            pltpu.VMEM((capacity, 24, CELLS), F32),
            held,
            held,
            held,
            held,
        ],
        compiler_params=params(48),
        cost_estimate=pl.CostEstimate(flops=8 * 10**9, bytes_accessed=20 * 10**6, transcendentals=0),
    )(scal, table, spectra, courant, low, high, sym)


def lower_kernel(scal, table, q1_in, cs, side, below, above, sym, out, up, down, q1, fy, fz, fx, q2):
    count = scal[MID1] - scal[MID0]

    def fix(l, _):
        position = lax.rem(l, RUN)
        ux, _, _ = neighbours(table, l)
        q1[l] = q1_in[l]

        def remote(face):
            fx[l] = face[position]
            flux = view(face[RUN + position // 2])
            flux = jnp.where(upper(), 0.0, jnp.where(lax.rem(position, 2) == 0, flux, swap(flux)))
            q1[l, :, span(0)] += flat(flux)

        @pl.when(ux < 0)
        def _():
            remote(below)

        @pl.when(ux >= count)
        def _():
            remote(above)

        @pl.when((ux >= 0) & (ux < count))
        def _():
            fx[l] = side[ux]

        return 0

    lax.fori_loop(0, count, fix, 0)
    cross_flux(count, table, q1, cs, fy, fz, 0, 0)

    def second(l):
        face = view(fx[l])
        q = read(q1, l, 0)
        f = limited(q, speed(cs, l, 0, 0), jnp.where(upper(), swap(q), face))
        q2[l, :, span(0)] = flat(q - f + swap(jnp.where(upper(), face, f)) + cross(table, l, fy, fz, 0))
        q_prev, f_prev = q, f
        q = read(q1, l, 1)
        f = limited(q, speed(cs, l, 0, 1), swap(jnp.where(upper(), q_prev, q)))
        q2[l, :, span(1)] = flat(q - f + swap(jnp.where(upper(), f_prev, f)) + cross(table, l, fy, fz, 1))

    finish(count, second, q2, sym, out, up, down)


def lower_half(scal, table, q1, cs, side, below, above, sym):
    capacity = q1.shape[0]
    sent = jax.ShapeDtypeStruct((RUN, BINS, HALF), F32)
    held = pltpu.VMEM((capacity, PACKED, HALF), F32)
    return pl.pallas_call(
        lower_kernel,
        in_specs=[SMEM, SMEM] + [VMEM] * 6,
        out_specs=[VMEM] * 3,
        out_shape=[jax.ShapeDtypeStruct((capacity, BINS, HALF), F32), sent, sent],
        scratch_shapes=[held, held, held, pltpu.VMEM((capacity, PACKED, LANES), F32), held],
        compiler_params=params(48),
        cost_estimate=pl.CostEstimate(flops=8 * 10**9, bytes_accessed=20 * 10**6, transcendentals=0),
    )(scal, table, q1, cs, side, below, above, sym)


def place_kernel(scal, own_u, low_u, high_u, own_l, low_l, high_l, out):
    start, end = scal[MID0], scal[MID1]
    count = scal[NEW1] - scal[NEW0]

    def body(s, _):
        block = scal[NEW0] + s
        live = s < count

        def put(lower, upper_, i):
            out[s, :, 0:HALF] = lower[i]
            out[s, :, HALF:CELLS] = upper_[i]

        @pl.when(live & (block >= start) & (block < end))
        def _():
            put(own_l, own_u, block - start)

        @pl.when(live & (block < start))
        def _():
            put(low_l, low_u, block - start + RUN)

        @pl.when(live & (block >= end))
        def _():
            put(high_l, high_u, block - end)

        @pl.when(jnp.logical_not(live))
        def _():
            out[s] = jnp.zeros((BINS, CELLS), F32)

        return 0

    lax.fori_loop(0, out.shape[0], body, 0)


def place(scal, *pieces):
    capacity = pieces[0].shape[0]
    return pl.pallas_call(
        place_kernel,
        in_specs=[SMEM] + [VMEM] * 6,
        out_specs=VMEM,
        out_shape=jax.ShapeDtypeStruct((capacity, BINS, CELLS), F32),
        compiler_params=params(32),
    )(scal, *pieces)


def bounds(device, devices, old_count, new_count):
    ids = jnp.arange(devices, dtype=jnp.int32)
    counts = jnp.stack([old_count, new_count])

    def start(p):
        old, new = jnp.sum(jnp.where(ids < p, counts, 0), axis=1)
        least = (jnp.maximum(old, new) - RUN + RUN - 1 + RUN) // RUN * RUN - RUN
        most = (jnp.minimum(old, new) + RUN) // RUN * RUN
        return old, jnp.clip(2 * RUN * p, least, most), new

    old0, mid0, new0 = start(device)
    old1, mid1, new1 = start(device + 1)
    return jnp.stack([old0, old1, mid0, mid1, new0, new1]).astype(jnp.int32)


def on_device(devices, spectra, courant, kernel, old_count, new_count, upwind):
    device = lax.axis_index("blocks").astype(jnp.int32)
    rise = [(i, i + 1) for i in range(devices - 1)]
    fall = [(i + 1, i) for i in range(devices - 1)]
    around = [(i, (i + 1) % devices) for i in range(devices)]
    reverse = [(j, i) for i, j in around]

    def move(block, route):
        return lax.ppermute(block, "blocks", route)

    tail_start = lax.dynamic_slice(old_count, (device,), (1,)) - RUN
    tail, head = pack(spectra, courant, tail_start)
    low, high = move(tail, rise), move(head, fall)
    scal = bounds(device, devices, old_count, new_count)
    table = upwind[RUN : 2 * RUN].reshape(-1)
    sym = symmetric_kernel(kernel)
    up, down = faces(scal, table, spectra, courant, low, high)
    below, above = move(up, around), move(down, reverse)
    q1, cs, side, own_u, up_u, down_u = upper_half(scal, table, spectra, courant, low, high, sym)
    low_u, high_u = move(up_u, rise), move(down_u, fall)
    own_l, up_l, down_l = lower_half(scal, table, q1, cs, side, below, above, sym)
    low_l, high_l = move(up_l, rise), move(down_l, fall)
    return place(scal, own_u, low_u, high_u, own_l, low_l, high_l)


def solution(mesh):
    in_specs = (P("blocks", None, None), P("blocks", None, None), P(), P(), P(), P())
    out_specs = P("blocks", None, None)
    return jax.shard_map(
        functools.partial(on_device, mesh.shape["blocks"]),
        mesh=mesh,
        in_specs=in_specs,
        out_specs=out_specs,
        check_vma=False,
    )
```

time: 218 us -> 151 us (0.69)
  local copies, waits for them, and re-layouts: 81.3 us -> 10.8 us
  Pallas kernels: 70.4 us -> 87 us
  other arithmetic: 12.2 us -> 0.16 us
    pallas_call x1 -> x2, Pallas kernels: 23 us -> 47 us  [the longest x1 29.4 us: symmetric_kernel(): pl.pallas_call(symmetric_kernel_body, grid=(TERMS // 256,), in_specs=[pl....]
    slice x15 -> x0, local copies, waits for them, and re-layouts: 20.2 us -> none  [the longest x12 16.9 us: symmetric_kernel(): both[:, 8 * g:8 * g + 8, 8 * g + 8:FULL].reshape(BINS, -1)]
    reshape x15 -> x0, local copies, waits for them, and re-layouts: 16.6 us -> none  [the longest x5 7.07 us: symmetric_kernel(): parts.append((diag * at).sum(axis=3).reshape(BINS, -1))]
    another operation x10 -> x0, local copies, waits for them, and re-layouts: 15.8 us -> none  [symmetric_kernel(): jnp.stack([both[:, 8 * g:8 * g + 8, 8 * g:8 * g + 8] for g in range(8)],...]
    unnamed x24 -> x19, local copies, waits for them, and re-layouts: 21.1 us -> 5.38 us
    pallas_call x1, Pallas kernels: 33.5 us -> 26 us  [upper_half(): pl.pallas_call(upper_kernel, in_specs=[SMEM, SMEM] + [VMEM] * 5, out_spec...]
    another operation x1 -> x0, other arithmetic: 3.04 us -> none
    select_n x5 -> x0, other arithmetic: 2.7 us -> none  [symmetric_kernel(): at = (r[None, :] == (r[:, None] - s) % 8).astype(F32)]
  transfers between devices with their start and end apart: 8 -> 8, of which waited for: 2 -> 2; matrix products, arithmetic and copies ran while one was open for 38% -> 3% of each run, Pallas kernels for 26% -> 49%
where the time goes in v2:
time: 151 us; the launch traced here: 150 us
  Pallas kernels  87 us (58%)
  starting transfers between devices  29.8 us (20%)
  waiting for transfers between devices  16.6 us (11%)
  local copies, waits for them, and re-layouts  10.8 us (7%)
  between operations  5.94 us (4%)
    ppermute x8, starting transfers between devices, move(): return lax.ppermute(block, 'blocks', route)  29.8 us
    pallas_call x1, Pallas kernels, symmetric_kernel(): pl.pallas_call(symmetric_kernel_body, grid=(TERMS // 256,), in_specs=[pl....  29.4 us
    pallas_call x1, Pallas kernels, upper_half(): pl.pallas_call(upper_kernel, in_specs=[SMEM, SMEM] + [VMEM] * 5, out_spec...  26 us
    pallas_call x1, Pallas kernels, lower_half(): pl.pallas_call(lower_kernel, in_specs=[SMEM, SMEM] + [VMEM] * 6, out_spec...  17.6 us
    ppermute x8, waiting for transfers between devices, move(): return lax.ppermute(block, 'blocks', route)  16.6 us
    unnamed x19, local copies, waits for them, and re-layouts  5.38 us
    pallas_call x1, Pallas kernels, faces(): pl.pallas_call(face_kernel, grid=(1,), in_specs=[SMEM, SMEM, half(capacit...  5.13 us
    pallas_call x1, Pallas kernels, pack(): pl.pallas_call(pack_kernel, grid_spec=pltpu.PrefetchScalarGridSpec(num_sc...  4.5 us
  transfers between devices with their start and end apart: 8, of which 2 were waited for; matrix products, arithmetic and copies ran while one was open for 3% of the time, Pallas kernels for 49%

profile of v2, /device:TPU:111, one launch (start us, length us, event | category | flops | bytes accessed | tf_op | source)
XLA Modules:
  0.0 150.4 jit_solution(11903687796547657529)
XLA Ops:
  0.0 1.1 copy.16.tail_c.head_c.courant
  1.1 1.2 dynamic_slice.3
  3.0 2.5 %copy-done = f32[36,66,512]{2,1,0:T(8,128)S(1)} copy-done((f32[36,66,512]{2,1,0:T(8,128)S(1)}, f32[36,66,512]{2,1,0:T(8,128)}, u32[]{:S(2)}) %copy-start) | copy-done | bytes 4866072
  5.5 4.5 %shard_map.73 = (f32[12,72,512]{2,1,0:T(8,128)}, f32[12,72,512]{2,1,0:T(8,128)}) custom-call(s32[1]{0:T(128)S(6)} %sub.32.scal, f32[36,66,512]{2,1,0:T(8,128)S(1)} %copy-done, f32[36,3,512]{2,1,0:T(4,128)S(1)} %copy.16.tail_c.head_c.courant, f32[36,66,512]{2,1,0:T(8,128)S(1)} %copy-done, f32[36,3,512]{2,1,0:T(4,128)S(1)} %copy.16.tail_c.head_c.courant), custom_call_target="tpu_custom_call" | custom-call | tf_op jit(solution)/shard_map/pallas_call | solution.py:151
  10.0 2.3 %collective-permute-start = (f32[12,72,512]{2,1,0:T(8,128)}, f32[12,72,512]{2,1,0:T(8,128)S(1)}, u32[]{:S(2)}, u32[]{:S(2)}) collective-permute-start(f32[12,72,512]{2,1,0:T(8,128)} %get-tuple-element.18), channel_id=1, source_target_pairs={{0,1},{1,2},{2,3},{3,4},{4,5},{5,6},{6,7},{7,8},{8,9},{9,10},{10,1... | collective-permute-start | bytes 5308424 | tf_op jit(solution)/shard_map/ppermute | solution.py:533
  12.3 2.2 %collective-permute-start.1 = (f32[12,72,512]{2,1,0:T(8,128)}, f32[12,72,512]{2,1,0:T(8,128)}, u32[]{:S(2)}, u32[]{:S(2)}) collective-permute-start(f32[12,72,512]{2,1,0:T(8,128)} %get-tuple-element.19), channel_id=1, source_target_pairs={{1,0},{2,1},{3,2},{4,3},{5,4},{6,5},{7,6},{8,7},{9,8},{10,9},{11,1... | collective-permute-start | bytes 5308424 | tf_op jit(solution)/shard_map/ppermute | solution.py:533
  14.6 0.1 select_reduce_fusion
  14.7 0.7 fusion
  20.4 0.8 slice.3
  21.2 0.1 copy.13
  21.4 2.6 %stack.23.scal = s32[6]{0:T(128)S(1)} concatenate(s32[1]{0:T(128)} %get-tuple-element.37, s32[1]{0:T(128)} %get-tuple-element.34, s32[1]{0:T(128)} %bitcast.6, s32[1]{0:T(128)} %bitcast.11, s32[1]{0:T(128)} %get-tuple-element.38, s32[1]{0:T(128)} %get-tuple-element.33), dimensions={0} | concatenate | bytes 48 | tf_op jit(solution)/shard_map/stack | solution.py:522
  24.0 29.4 %shard_map.74.sym = bf16[80,2304]{1,0:T(8,128)(2,1)S(1)} custom-call(s32[2,2304]{1,0:T(2,128)S(1)} %copy-done.5, bf16[80,4608]{1,0:T(8,128)(2,1)S(1)} %pad.4.kernel), custom_call_target="tpu_custom_call" | custom-call | flops 2000000000 | bytes 1000000 | tf_op jit(solution)/shard_map/pallas_call | solution.py:268
  53.5 5.1 %shard_map.76 = (f32[18,72,128]{2,1,0:T(8,128)S(1)}, f32[18,72,128]{2,1,0:T(8,128)S(1)}) custom-call(s32[6]{0:T(128)S(1)} %stack.23.scal, s32[36]{0:T(128)S(1)} %reshape.51.table, f32[36,66,512]{2,1,0:T(8,128)S(1)} %copy-done.1, f32[36,3,512]{2,1,0:T(4,128)S(1)} %copy.16.tail_c.head_c.courant, f32[12,72,512]{2,1,0:T(8,128)S(1)} %collective-permute-done.low, ...), custom_call_target="tpu_custom_call" | custom-call | tf_op jit(solution)/shard_map/pallas_call | solution.py:206
  58.6 5.8 %collective-permute-start.4 = (f32[18,72,128]{2,1,0:T(8,128)S(1)}, f32[18,72,128]{2,1,0:T(8,128)S(1)}, u32[]{:S(2)}, u32[]{:S(2)}) collective-permute-start(f32[18,72,128]{2,1,0:T(8,128)S(1)} %get-tuple-element.26), channel_id=1, source_target_pairs={{0,1},{1,2},{2,3},{3,4},{4,5},{5,6},{6,7},{7,8},{8,9},{9,10},{10,1... | collective-permute-start | bytes 1990664 | tf_op jit(solution)/shard_map/ppermute | solution.py:533
  64.4 26.0 %shard_map.75 = (f32[36,72,256]{2,1,0:T(8,128)}, f32[36,24,256]{2,1,0:T(8,128)S(1)}, f32[36,72,128]{2,1,0:T(8,128)S(1)}, f32[36,66,256]{2,1,0:T(8,128)}, f32[12,...) custom-call(s32[6]{0:T(128)S(1)} %stack.23.scal, s32[36]{0:T(128)S(1)} %reshape.51.table, f32[36,66,512]{2,1,0:T(8,128)} %spectra.3, ...), custom_call_target="tpu_custom_call" | custom-call | flops 8000000000 | bytes 20000000 | tf_op jit(solution)/shard_map/pallas_call | solution.py:382
  90.4 7.9 %collective-permute-start.2 = (f32[12,66,256]{2,1,0:T(8,128)S(1)}, f32[12,66,256]{2,1,0:T(8,128)S(1)}, u32[]{:S(2)}, u32[]{:S(2)}) collective-permute-start(f32[12,66,256]{2,1,0:T(8,128)S(1)} %get-tuple-element.21), channel_id=1, source_target_pairs={{0,1},{1,2},{2,3},{3,4},{4,5},{5,6},{6,7},{7,8},{8,9},{9,10},{10,1... | collective-permute-start | bytes 2433032 | tf_op jit(solution)/shard_map/ppermute | solution.py:533
  98.2 1.9 %collective-permute-start.3 = (f32[12,66,256]{2,1,0:T(8,128)S(1)}, f32[12,66,256]{2,1,0:T(8,128)S(1)}, u32[]{:S(2)}, u32[]{:S(2)}) collective-permute-start(f32[12,66,256]{2,1,0:T(8,128)S(1)} %get-tuple-element.22), channel_id=1, source_target_pairs={{1,0},{2,1},{3,2},{4,3},{5,4},{6,5},{7,6},{8,7},{9,8},{10,9},{11,1... | collective-permute-start | bytes 2433032 | tf_op jit(solution)/shard_map/ppermute | solution.py:533
  100.2 17.6 %shard_map.77 = (f32[36,66,256]{2,1,0:T(8,128)}, f32[12,66,256]{2,1,0:T(8,128)S(1)}, f32[12,66,256]{2,1,0:T(8,128)S(1)}) custom-call(s32[6]{0:T(128)S(1)} %stack.23.scal, s32[36]{0:T(128)S(1)} %reshape.51.table, f32[36,72,256]{2,1,0:T(8,128)} %get-tuple-element.23.q1_in, f32[36,24,256]{2,1,0:T(8,128)S(1)} %get-tuple-element.24.cs, ...), custom_call_target="tpu_custom_call" | custom-call | flops 8000000000 | bytes 20000000 | tf_op jit(solution)/shard_map/pallas_call | solution.py:455
  117.8 7.8 %collective-permute-start.6 = (f32[12,66,256]{2,1,0:T(8,128)S(1)}, f32[12,66,256]{2,1,0:T(8,128)S(1)}, u32[]{:S(2)}, u32[]{:S(2)}) collective-permute-start(f32[12,66,256]{2,1,0:T(8,128)S(1)} %get-tuple-element.29), channel_id=1, source_target_pairs={{0,1},{1,2},{2,3},{3,4},{4,5},{5,6},{6,7},{7,8},{8,9},{9,10},{10,1... | collective-permute-start | bytes 2433032 | tf_op jit(solution)/shard_map/ppermute | solution.py:533
  125.7 1.9 %collective-permute-start.7 = (f32[12,66,256]{2,1,0:T(8,128)S(1)}, f32[12,66,256]{2,1,0:T(8,128)S(1)}, u32[]{:S(2)}, u32[]{:S(2)}) collective-permute-start(f32[12,66,256]{2,1,0:T(8,128)S(1)} %get-tuple-element.30), channel_id=1, source_target_pairs={{1,0},{2,1},{3,2},{4,3},{5,4},{6,5},{7,6},{8,7},{9,8},{10,9},{11,1... | collective-permute-start | bytes 2433032 | tf_op jit(solution)/shard_map/ppermute | solution.py:533
  127.6 8.0 %collective-permute-done.6.low_l = f32[12,66,256]{2,1,0:T(8,128)S(1)} collective-permute-done((f32[12,66,256]{2,1,0:T(8,128)S(1)}, f32[12,66,256]{2,1,0:T(8,128)S(1)}, u32[]{:S(2)}, u32[]{:S(2)}) %collective-permute-start.6) | collective-permute-done | bytes 811040 | tf_op jit(solution)/shard_map/ppermute | solution.py:533
  135.6 8.6 %collective-permute-done.7.high_l = f32[12,66,256]{2,1,0:T(8,128)S(1)} collective-permute-done((f32[12,66,256]{2,1,0:T(8,128)S(1)}, f32[12,66,256]{2,1,0:T(8,128)S(1)}, u32[]{:S(2)}, u32[]{:S(2)}) %collective-permute-start.7) | collective-permute-done | bytes 811040 | tf_op jit(solution)/shard_map/ppermute | solution.py:533
  144.3 1.7 %copy-done.3 = f32[36,66,256]{2,1,0:T(8,128)S(1)} copy-done((f32[36,66,256]{2,1,0:T(8,128)S(1)}, f32[36,66,256]{2,1,0:T(8,128)}, u32[]{:S(2)}) %copy-start.3) | copy-done | bytes 2433048
  146.0 4.4 %shard_map.78 = f32[36,66,512]{2,1,0:T(8,128)} custom-call(s32[6]{0:T(128)S(1)} %stack.23.scal, f32[36,66,256]{2,1,0:T(8,128)S(1)} %copy-done.2, f32[12,66,256]{2,1,0:T(8,128)S(1)} %collective-permute-done.2.low_u, f32[12,66,256]{2,1,0:T(8,128)S(1)} %collective-permute-done.3.high_u, f32[36,66,256]{2,1,0:T(8,128)S(1)} %copy-done.3, ...), custom_call_target="tpu_custom_call" | custom-call | tf_op jit(solution)/shard_map/pallas_call | solution.py:501
  (27 shorter events, 0.2 us)
Async XLA Ops:
  3.0 2.5 %copy-start = (f32[36,66,512]{2,1,0:T(8,128)S(1)}, f32[36,66,512]{2,1,0:T(8,128)}, u32[]{:S(2)}) copy-start(f32[36,66,512]{2,1,0:T(8,128)} %spectra.3) | copy-start | bytes 14598148
  5.5 9.1 %copy-start.7 = (s32[128]{0:T(128)S(1)}, s32[128]{0:T(128)}, u32[]{:S(2)}) copy-start(s32[128]{0:T(128)} %param.11) | copy-start | bytes 1540
  5.5 9.1 %copy-start.8 = (s32[128]{0:T(128)S(1)}, s32[128]{0:T(128)}, u32[]{:S(2)}) copy-start(s32[128]{0:T(128)} %param.10) | copy-start | bytes 1540
  5.5 18.4 %copy-start.6 = (bf16[66,4356]{1,0:T(8,128)(2,1)S(1)}, bf16[66,4356]{1,0:T(8,128)(2,1)}, u32[]{:S(2)}) copy-start(bf16[66,4356]{1,0:T(8,128)(2,1)} %param.9) | copy-start | bytes 1724980
  5.5 18.5 %copy-start.5 = (s32[2,2304]{1,0:T(2,128)S(1)}, s32[2,2304]{1,0:T(2,128)}, u32[]{:S(2)}) copy-start(s32[2,2304]{1,0:T(2,128)} %constant.72.clone.columns) | copy-start | bytes 55300
  10.0 43.4 %collective-permute-start = (f32[12,72,512]{2,1,0:T(8,128)}, f32[12,72,512]{2,1,0:T(8,128)S(1)}, u32[]{:S(2)}, u32[]{:S(2)}) collective-permute-start(f32[12,72,512]{2,1,0:T(8,128)} %get-tuple-element.18), channel_id=1, source_target_pairs={{0,1},{1,2},{2,3},{3,4},{4,5},{5,6},{6,7},{7,8},{8,9},{9,10},{10,1... | collective-permute-start | bytes 5308424 | tf_op jit(solution)/shard_map/ppermute | solution.py:533
  12.3 41.1 %collective-permute-start.1 = (f32[12,72,512]{2,1,0:T(8,128)}, f32[12,72,512]{2,1,0:T(8,128)}, u32[]{:S(2)}, u32[]{:S(2)}) collective-permute-start(f32[12,72,512]{2,1,0:T(8,128)} %get-tuple-element.19), channel_id=1, source_target_pairs={{1,0},{2,1},{3,2},{4,3},{5,4},{6,5},{7,6},{8,7},{9,8},{10,9},{11,1... | collective-permute-start | bytes 5308424 | tf_op jit(solution)/shard_map/ppermute | solution.py:533
  24.0 29.5 %copy-start.1 = (f32[36,66,512]{2,1,0:T(8,128)S(1)}, f32[36,66,512]{2,1,0:T(8,128)}, u32[]{:S(2)}) copy-start(f32[36,66,512]{2,1,0:T(8,128)} %spectra.3) | copy-start | bytes 14598148
  53.5 5.2 %copy-start.4 = (f32[12,72,512]{2,1,0:T(8,128)}, f32[12,72,512]{2,1,0:T(8,128)S(1)}, u32[]{:S(2)}) copy-start(f32[12,72,512]{2,1,0:T(8,128)S(1)} %collective-permute-done.low) | copy-start | bytes 5308420
  58.6 41.5 %collective-permute-start.4 = (f32[18,72,128]{2,1,0:T(8,128)S(1)}, f32[18,72,128]{2,1,0:T(8,128)S(1)}, u32[]{:S(2)}, u32[]{:S(2)}) collective-permute-start(f32[18,72,128]{2,1,0:T(8,128)S(1)} %get-tuple-element.26), channel_id=1, source_target_pairs={{0,1},{1,2},{2,3},{3,4},{4,5},{5,6},{6,7},{7,8},{8,9},{9,10},{10,1... | collective-permute-start | bytes 1990664 | tf_op jit(solution)/shard_map/ppermute | solution.py:533
  64.4 35.8 %collective-permute-start.5 = (f32[18,72,128]{2,1,0:T(8,128)S(1)}, f32[18,72,128]{2,1,0:T(8,128)S(1)}, u32[]{:S(2)}, u32[]{:S(2)}) collective-permute-start(f32[18,72,128]{2,1,0:T(8,128)S(1)} %get-tuple-element.27), channel_id=1, source_target_pairs={{1,0},{2,1},{3,2},{4,3},{5,4},{6,5},{7,6},{8,7},{9,8},{10,9},{11,1... | collective-permute-start | bytes 1990664 | tf_op jit(solution)/shard_map/ppermute | solution.py:533
  90.4 37.2 %collective-permute-start.2 = (f32[12,66,256]{2,1,0:T(8,128)S(1)}, f32[12,66,256]{2,1,0:T(8,128)S(1)}, u32[]{:S(2)}, u32[]{:S(2)}) collective-permute-start(f32[12,66,256]{2,1,0:T(8,128)S(1)} %get-tuple-element.21), channel_id=1, source_target_pairs={{0,1},{1,2},{2,3},{3,4},{4,5},{5,6},{6,7},{7,8},{8,9},{9,10},{10,1... | collective-permute-start | bytes 2433032 | tf_op jit(solution)/shard_map/ppermute | solution.py:533
  98.2 29.4 %collective-permute-start.3 = (f32[12,66,256]{2,1,0:T(8,128)S(1)}, f32[12,66,256]{2,1,0:T(8,128)S(1)}, u32[]{:S(2)}, u32[]{:S(2)}) collective-permute-start(f32[12,66,256]{2,1,0:T(8,128)S(1)} %get-tuple-element.22), channel_id=1, source_target_pairs={{1,0},{2,1},{3,2},{4,3},{5,4},{6,5},{7,6},{8,7},{9,8},{10,9},{11,1... | collective-permute-start | bytes 2433032 | tf_op jit(solution)/shard_map/ppermute | solution.py:533
  100.2 44.1 %copy-start.2 = (f32[36,66,256]{2,1,0:T(8,128)S(1)}, f32[36,66,256]{2,1,0:T(8,128)}, u32[]{:S(2)}) copy-start(f32[36,66,256]{2,1,0:T(8,128)} %get-tuple-element.20.own_u) | copy-start | bytes 7299076
  117.8 17.8 %collective-permute-start.6 = (f32[12,66,256]{2,1,0:T(8,128)S(1)}, f32[12,66,256]{2,1,0:T(8,128)S(1)}, u32[]{:S(2)}, u32[]{:S(2)}) collective-permute-start(f32[12,66,256]{2,1,0:T(8,128)S(1)} %get-tuple-element.29), channel_id=1, source_target_pairs={{0,1},{1,2},{2,3},{3,4},{4,5},{5,6},{6,7},{7,8},{8,9},{9,10},{10,1... | collective-permute-start | bytes 2433032 | tf_op jit(solution)/shard_map/ppermute | solution.py:533
  125.7 18.6 %collective-permute-start.7 = (f32[12,66,256]{2,1,0:T(8,128)S(1)}, f32[12,66,256]{2,1,0:T(8,128)S(1)}, u32[]{:S(2)}, u32[]{:S(2)}) collective-permute-start(f32[12,66,256]{2,1,0:T(8,128)S(1)} %get-tuple-element.30), channel_id=1, source_target_pairs={{1,0},{2,1},{3,2},{4,3},{5,4},{6,5},{7,6},{8,7},{9,8},{10,9},{11,1... | collective-permute-start | bytes 2433032 | tf_op jit(solution)/shard_map/ppermute | solution.py:533
  144.2 1.8 %copy-start.3 = (f32[36,66,256]{2,1,0:T(8,128)S(1)}, f32[36,66,256]{2,1,0:T(8,128)}, u32[]{:S(2)}) copy-start(f32[36,66,256]{2,1,0:T(8,128)} %get-tuple-element.28.own_l) | copy-start | bytes 7299076

commit v3 on v2

--- a/solution.py
+++ b/solution.py
@@ -21,7 +21,8 @@
 F32 = jnp.float32
 VMEM = pl.BlockSpec(memory_space=pltpu.VMEM)
 SMEM = pl.BlockSpec(memory_space=pltpu.SMEM)
-OLD0, OLD1, MID0, MID1, NEW0, NEW1 = range(6)
+OLD0, OLD1, MID0, MID1, NEW0, NEW1, HERE0, HERE1 = range(8)
+ANY = pl.BlockSpec(memory_space=pl.ANY)
 
 
 def params(mib):
@@ -102,7 +103,7 @@
 def donor(q0, cs, l, v, q_prev, cx_prev, uy, uz):
     q, cx, cy, cz = read(q0, l, v), speed(cs, l, 0, v), speed(cs, l, 1, v), speed(cs, l, 2, v)
     up, ly, lz = upper(), last_y(), last_z()
-    in_x = swap(jnp.where(up, cx_prev, cx) * jnp.where(up, q_prev, q))
+    in_x = swap(jnp.where(up, 0.0 if q_prev is None else cx_prev * q_prev, cx * q))
     in_y = step_y(jnp.where(ly, speed(cs, uy, 1, v), cy) * jnp.where(ly, read(q0, uy, v), q))
     in_z = step_z(jnp.where(lz, speed(cs, uz, 2, v), cz) * jnp.where(lz, read(q0, uz, v), q))
     return (1.0 - (cx + cy + cz)) * q + in_x + in_y + in_z
@@ -117,10 +118,14 @@
                 ref[i, row + d : row + d + 1], (8,) + ref.shape[2:]
             )
 
-    @pl.when((block >= own0) & (block < own1))
-    def _():
+    def owned():
         q_dst[at, 0:BINS] = spectra[block - own0]
         spread(courant, block - own0, 0)
+
+    if low is None:
+        owned()
+        return
+    pl.when((block >= own0) & (block < own1))(owned)
 
     def received(ref, i):
         q_dst[at] = ref[i]
@@ -135,35 +140,48 @@
         received(high, block - own1)
 
 
-def pack_kernel(scal, tail_q, tail_c, head_q, head_c, up, down):
-    pad = jnp.zeros((1, PACKED - BINS - 3, CELLS), F32)
-    up[...] = jnp.concatenate([tail_q[...], tail_c[...], pad], axis=1)
-    down[...] = jnp.concatenate([head_q[...], head_c[...], pad], axis=1)
-
-
-def pack(spectra, courant, tail_start):
-    def tail(i, scal):
-        return (scal[0] + i, 0, 0)
-
-    def head(i, scal):
-        return (i, 0, 0)
-
+def pack_kernel(old_count, device, spectra, courant, up, down, raw, speeds, joined, in_sems, out_sems):
+    tail = old_count[device[0]] - RUN
+    copies = []
+    for side, start in ((0, tail), (1, 0)):
+        copies.append(pltpu.make_async_copy(courant.at[pl.ds(start, RUN)], speeds.at[side], in_sems.at[side, RUN]))
+        copies[-1].start()
+    waits, sends = [], []
+    for k in range(0, RUN, 2):
+        for side, start, out in ((0, tail, up), (1, 0, down)):
+            here = pl.ds(k, 2)
+            copy = pltpu.make_async_copy(spectra.at[pl.ds(start + k, 2)], raw.at[side, here], in_sems.at[side, k])
+            copy.start()
+            waits.append((side, k, copy))
+            sends.append(pltpu.make_async_copy(joined.at[side, here], out.at[here], out_sems.at[side, k]))
+    for copy in copies:
+        copy.wait()
+    for (side, k, copy), send in zip(waits, sends):
+        copy.wait()
+        for i in (k, k + 1):
+            joined[side, i, 0:BINS] = raw[side, i]
+            joined[side, i, BINS : BINS + 3] = speeds[side, i]
+        send.start()
+    for send in sends:
+        send.wait()
+
+
+def pack(old_count, device, spectra, courant):
+    sent = jax.ShapeDtypeStruct((RUN, PACKED, CELLS), F32)
     return pl.pallas_call(
         pack_kernel,
-        grid_spec=pltpu.PrefetchScalarGridSpec(
-            num_scalar_prefetch=1,
-            grid=(RUN,),
-            in_specs=[
-                pl.BlockSpec((1, BINS, CELLS), tail),
-                pl.BlockSpec((1, 3, CELLS), tail),
-                pl.BlockSpec((1, BINS, CELLS), head),
-                pl.BlockSpec((1, 3, CELLS), head),
-            ],
-            out_specs=[pl.BlockSpec((1, PACKED, CELLS), head)] * 2,
-        ),
-        out_shape=[jax.ShapeDtypeStruct((RUN, PACKED, CELLS), F32)] * 2,
-        compiler_params=params(24),
-    )(tail_start, spectra, courant, spectra, courant)
+        in_specs=[SMEM, SMEM, ANY, ANY],
+        out_specs=[ANY, ANY],
+        out_shape=[sent, sent],
+        scratch_shapes=[
+            pltpu.VMEM((2, RUN, BINS, CELLS), F32),
+            pltpu.VMEM((2, RUN, 3, CELLS), F32),
+            pltpu.VMEM((2, RUN, PACKED, CELLS), F32),
+            pltpu.SemaphoreType.DMA((2, RUN + 1)),
+            pltpu.SemaphoreType.DMA((2, RUN)),
+        ],
+        compiler_params=params(56),
+    )(old_count, device, spectra, courant)
 
 
 def face_kernel(scal, table, spectra, courant, low, high, up, down, q0, cs):
@@ -251,14 +269,11 @@
 def symmetric_kernel_body(columns, kernel, out):
     width = out.shape[1]
     one, two = columns[0:1], columns[1:2]
-
-    def chunk(i, total):
-        base = pl.multiple_of(i * 256, 256)
+    picks = []
+    for base in range(0, kernel.shape[1], 256):
         row = lax.broadcasted_iota(jnp.int32, (256, width), 0) + base
-        pick = jnp.where((row == one) | (row == two), 1.0, 0.0).astype(jnp.bfloat16)
-        return total + jnp.dot(kernel[:, pl.ds(base, 256)], pick, preferred_element_type=F32)
-
-    total = lax.fori_loop(0, kernel.shape[1] // 256, chunk, jnp.zeros((80, width), F32))
+        picks.append(jnp.where((row == one) | (row == two), 1.0, 0.0).astype(jnp.bfloat16))
+    total = jnp.dot(kernel[...], jnp.concatenate(picks, axis=0), preferred_element_type=F32)
     out[...] = total.astype(jnp.bfloat16)
 
 
@@ -294,8 +309,9 @@
     return jnp.where(back, l - RUN, l + RUN), y + (l - position), z + (l - position)
 
 
-def cross_flux(count, table, q1, cs, fy, fz, v0, vf):
-    def cross_body(l, _):
+def cross_flux(count, block_at, table, q1, cs, fy, fz, v0, vf):
+    def cross_body(i, _):
+        l = block_at(i)
         _, uy, uz = neighbours(table, l)
         for w in range(2):
             q = read(q1, l, v0 + w)
@@ -316,39 +332,41 @@
     return (y_in - y_own) + (z_in - z_own)
 
 
-def finish(count, second, q2, sym, out, up, down):
-    second(0)
-
-    def third(l, _):
-        out[l] = coalesce(q2[l], sym)[0:BINS]
-        second(jnp.minimum(l + 1, count - 1))
-        return 0
+def coalesce_all(count, block_at, second, q2, sym, out):
+    def third(i, _):
+        l = block_at(i)
+        out[l, :, 0:HALF] = coalesce(q2[l], sym)[0:BINS]
+        second(block_at(jnp.minimum(i + 1, count - 1)))
+        return 0
+
+    @pl.when(count > 0)
+    def _():
+        second(block_at(0))
 
     lax.fori_loop(0, count, third, 0)
 
-    def hand_on(k, _):
-        down[k] = out[k]
-        up[k] = out[count - RUN + k]
-        return 0
-
-    lax.fori_loop(0, RUN, hand_on, 0)
-
-
-def upper_kernel(scal, table, spectra, courant, low, high, sym, low_q1, low_c, side, out, up, down, q0, cs, q1, fy, fz, q2):
-    count = scal[MID1] - scal[MID0]
-
-    def gather(l, _):
+
+def upper_kernel(received, scal, table, spectra, courant, sym, *rest):
+    low, high = rest[:2] if received else (None, None)
+    low_q1, low_c, face, out, q0, cs, q1, fy, fz, q2 = rest[2 if received else 0 :]
+    here0, here = scal[HERE0], scal[HERE1] - scal[HERE0]
+    count = scal[MID1] - scal[MID0] - here if received else here
+
+    def block_at(i):
+        return i + jnp.where(i >= here0, here, 0) if received else i + here0
+
+    def gather(i, _):
+        l = block_at(i)
         fetch(scal[MID0] + l, scal, spectra, courant, low, high, q0, cs, l)
         low_c[l] = cs[l, :, 0:HALF]
         return 0
 
     lax.fori_loop(0, count, gather, 0)
 
-    def first(l, _):
-        ux, uy, uz = neighbours(table, l)
-        here = ((ux >= 0) & (ux < count)).astype(F32)
-        ux = jnp.clip(ux, 0, count - 1)
-        q_prev, cx_prev = read(q0, ux, 3), speed(cs, ux, 0, 3) * here
+    def first(i, _):
+        l = block_at(i)
+        _, uy, uz = neighbours(table, l)
+        q_prev = cx_prev = None
         for v in range(4):
             new = donor(q0, cs, l, v, q_prev, cx_prev, uy, uz)
             q_prev, cx_prev = read(q0, l, v), speed(cs, l, 0, v)
@@ -357,11 +375,12 @@
             else:
                 q1[l, :, span(v - 2)] = flat(new)
         other = swap(new)
-        side[l] = flat(jnp.where(upper(), limited(new, cx_prev, other), other))
+        face[l, 0:PACKED] = flat(jnp.where(upper(), limited(new, cx_prev, other), other))
+        face[l, PACKED : 2 * PACKED] = flat(cx_prev * q_prev)
         return 0
 
     lax.fori_loop(0, count, first, 0)
-    cross_flux(count, table, q1, cs, fy, fz, 0, 2)
+    cross_flux(count, block_at, table, q1, cs, fy, fz, 0, 2)
 
     def second(l):
         q_prev = read(low_q1, l, 1)
@@ -373,23 +392,21 @@
             q2[l, :, span(w)] = flat(new)
             q_prev, f_prev = q, f
 
-    finish(count, second, q2, sym, out, up, down)
-
-
-def upper_half(scal, table, spectra, courant, low, high, sym):
+    coalesce_all(count, block_at, second, q2, sym, out)
+
+
+def upper_half(scal, table, spectra, courant, sym, *moved):
     capacity = spectra.shape[0]
     held = pltpu.VMEM((capacity, PACKED, HALF), F32)
     return pl.pallas_call(
-        upper_kernel,
-        in_specs=[SMEM, SMEM] + [VMEM] * 5,
-        out_specs=[VMEM] * 6,
+        functools.partial(upper_kernel, bool(moved)),
+        in_specs=[SMEM, SMEM] + [VMEM] * (3 + len(moved)),
+        out_specs=[VMEM] * 4,
         out_shape=[
             jax.ShapeDtypeStruct((capacity, PACKED, HALF), F32),
             jax.ShapeDtypeStruct((capacity, 24, HALF), F32),
-            jax.ShapeDtypeStruct((capacity, PACKED, LANES), F32),
+            jax.ShapeDtypeStruct((capacity, 2 * PACKED, LANES), F32),
             jax.ShapeDtypeStruct((capacity, BINS, HALF), F32),
-            jax.ShapeDtypeStruct((RUN, BINS, HALF), F32),
-            jax.ShapeDtypeStruct((RUN, BINS, HALF), F32),
         ],
         scratch_shapes=[
             pltpu.VMEM((capacity, PACKED, CELLS), F32),
@@ -400,23 +417,38 @@
             held,
         ],
         compiler_params=params(48),
-        cost_estimate=pl.CostEstimate(flops=8 * 10**9, bytes_accessed=20 * 10**6, transcendentals=0),
-    )(scal, table, spectra, courant, low, high, sym)
-
-
-def lower_kernel(scal, table, q1_in, cs, side, below, above, sym, out, up, down, q1, fy, fz, fx, q2):
+        cost_estimate=pl.CostEstimate(flops=4 * 10**9, bytes_accessed=20 * 10**6, transcendentals=0),
+    )(scal, table, spectra, courant, sym, *moved)
+
+
+def lower_kernel(scal, table, *rest):
+    early, late = rest[0:4], rest[4:8]
+    below, above, sym, own, up, down, q1, cs, fy, fz, fx, q2 = rest[8:]
     count = scal[MID1] - scal[MID0]
+
+    def choose(l, take):
+        was_here = (l >= scal[HERE0]) & (l < scal[HERE1])
+        pl.when(was_here)(functools.partial(take, *early))
+        pl.when(jnp.logical_not(was_here))(functools.partial(take, *late))
 
     def fix(l, _):
         position = lax.rem(l, RUN)
         ux, _, _ = neighbours(table, l)
-        q1[l] = q1_in[l]
+
+        def take(low_q1, low_c, face, out):
+            q1[l] = low_q1[l]
+            cs[l] = low_c[l]
+            own[l, :, HALF:CELLS] = out[l]
+
+        choose(l, take)
+
+        def add_flux(flux):
+            q1[l, :, span(0)] += flat(jnp.where(upper(), 0.0, flux))
 
         def remote(face):
             fx[l] = face[position]
             flux = view(face[RUN + position // 2])
-            flux = jnp.where(upper(), 0.0, jnp.where(lax.rem(position, 2) == 0, flux, swap(flux)))
-            q1[l, :, span(0)] += flat(flux)
+            add_flux(jnp.where(lax.rem(position, 2) == 0, flux, swap(flux)))
 
         @pl.when(ux < 0)
         def _():
@@ -428,12 +460,16 @@
 
         @pl.when((ux >= 0) & (ux < count))
         def _():
-            fx[l] = side[ux]
+            def take_face(low_q1, low_c, face, out):
+                fx[l] = face[ux, 0:PACKED]
+                add_flux(swap(view(face[ux, PACKED : 2 * PACKED])))
+
+            choose(ux, take_face)
 
         return 0
 
     lax.fori_loop(0, count, fix, 0)
-    cross_flux(count, table, q1, cs, fy, fz, 0, 0)
+    cross_flux(count, lambda i: i, table, q1, cs, fy, fz, 0, 0)
 
     def second(l):
         face = view(fx[l])
@@ -445,49 +481,51 @@
         f = limited(q, speed(cs, l, 0, 1), swap(jnp.where(upper(), q_prev, q)))
         q2[l, :, span(1)] = flat(q - f + swap(jnp.where(upper(), f_prev, f)) + cross(table, l, fy, fz, 1))
 
-    finish(count, second, q2, sym, out, up, down)
-
-
-def lower_half(scal, table, q1, cs, side, below, above, sym):
-    capacity = q1.shape[0]
-    sent = jax.ShapeDtypeStruct((RUN, BINS, HALF), F32)
+    coalesce_all(count, lambda i: i, second, q2, sym, own)
+
+    def hand_on(k, _):
+        down[k] = own[k]
+        up[k] = own[count - RUN + k]
+        return 0
+
+    lax.fori_loop(0, RUN, hand_on, 0)
+
+
+def lower_half(scal, table, early, late, below, above, sym):
+    capacity = early[0].shape[0]
+    sent = jax.ShapeDtypeStruct((RUN, BINS, CELLS), F32)
     held = pltpu.VMEM((capacity, PACKED, HALF), F32)
     return pl.pallas_call(
         lower_kernel,
-        in_specs=[SMEM, SMEM] + [VMEM] * 6,
+        in_specs=[SMEM, SMEM] + [VMEM] * 11,
         out_specs=[VMEM] * 3,
-        out_shape=[jax.ShapeDtypeStruct((capacity, BINS, HALF), F32), sent, sent],
-        scratch_shapes=[held, held, held, pltpu.VMEM((capacity, PACKED, LANES), F32), held],
-        compiler_params=params(48),
+        out_shape=[jax.ShapeDtypeStruct((capacity, BINS, CELLS), F32), sent, sent],
+        scratch_shapes=[
+            held,
+            pltpu.VMEM((capacity, 24, HALF), F32),
+            held,
+            held,
+            pltpu.VMEM((capacity, PACKED, LANES), F32),
+            held,
+        ],
+        compiler_params=params(52),
         cost_estimate=pl.CostEstimate(flops=8 * 10**9, bytes_accessed=20 * 10**6, transcendentals=0),
-    )(scal, table, q1, cs, side, below, above, sym)
-
-
-def place_kernel(scal, own_u, low_u, high_u, own_l, low_l, high_l, out):
+    )(scal, table, *early, *late, below, above, sym)
+
+
+def place_own_kernel(scal, own, out):
     start, end = scal[MID0], scal[MID1]
     count = scal[NEW1] - scal[NEW0]
 
     def body(s, _):
         block = scal[NEW0] + s
-        live = s < count
-
-        def put(lower, upper_, i):
-            out[s, :, 0:HALF] = lower[i]
-            out[s, :, HALF:CELLS] = upper_[i]
-
-        @pl.when(live & (block >= start) & (block < end))
+        mine = (s < count) & (block >= start) & (block < end)
+
+        @pl.when(mine)
         def _():
-            put(own_l, own_u, block - start)
-
-        @pl.when(live & (block < start))
-        def _():
-            put(low_l, low_u, block - start + RUN)
-
-        @pl.when(live & (block >= end))
-        def _():
-            put(high_l, high_u, block - end)
-
-        @pl.when(jnp.logical_not(live))
+            out[s] = own[block - start]
+
+        @pl.when(jnp.logical_not(mine))
         def _():
             out[s] = jnp.zeros((BINS, CELLS), F32)
 
@@ -496,34 +534,81 @@
     lax.fori_loop(0, out.shape[0], body, 0)
 
 
-def place(scal, *pieces):
-    capacity = pieces[0].shape[0]
-    return pl.pallas_call(
-        place_kernel,
-        in_specs=[SMEM] + [VMEM] * 6,
+def place_own(scal, own):
+    return pl.pallas_call(
+        place_own_kernel,
+        in_specs=[SMEM, VMEM],
         out_specs=VMEM,
-        out_shape=jax.ShapeDtypeStruct((capacity, BINS, CELLS), F32),
-        compiler_params=params(32),
-    )(scal, *pieces)
-
-
-def bounds(device, devices, old_count, new_count):
-    ids = jnp.arange(devices, dtype=jnp.int32)
-    counts = jnp.stack([old_count, new_count])
+        out_shape=own,
+        compiler_params=params(24),
+        cost_estimate=pl.CostEstimate(flops=10**6, bytes_accessed=11 * 10**6, transcendentals=0),
+    )(scal, own)
+
+
+def place_moved_kernel(scal, low, high, _, out, sems):
+    first, end = scal[NEW0], scal[NEW1]
+
+    def copies(act):
+        for k in range(RUN):
+            block = scal[MID0] - RUN + k
+
+            @pl.when((block >= first) & (block < end))
+            def _(k=k, block=block):
+                act(pltpu.make_async_copy(low.at[k], out.at[block - first], sems.at[0, k]))
+
+            above = scal[MID1] + k
+
+            @pl.when((above >= first) & (above < end))
+            def _(k=k, above=above):
+                act(pltpu.make_async_copy(high.at[k], out.at[above - first], sems.at[1, k]))
+
+    copies(lambda copy: copy.start())
+    copies(lambda copy: copy.wait())
+
+
+def place_moved(scal, low, high, out):
+    return pl.pallas_call(
+        place_moved_kernel,
+        in_specs=[SMEM, ANY, ANY, ANY],
+        out_specs=ANY,
+        out_shape=jax.ShapeDtypeStruct(out.shape, F32),
+        scratch_shapes=[pltpu.SemaphoreType.DMA((2, RUN))],
+        input_output_aliases={3: 0},
+        compiler_params=params(56),
+    )(scal, low, high, out)
+
+
+def bounds_kernel(device, old_count, new_count, out):
+    ids = lax.broadcasted_iota(jnp.int32, old_count.shape, 1)
+
+    def total(counts, p):
+        return jnp.sum(jnp.where(ids < p, counts[...], 0).astype(F32)).astype(jnp.int32)
 
     def start(p):
-        old, new = jnp.sum(jnp.where(ids < p, counts, 0), axis=1)
-        least = (jnp.maximum(old, new) - RUN + RUN - 1 + RUN) // RUN * RUN - RUN
-        most = (jnp.minimum(old, new) + RUN) // RUN * RUN
+        old, new = total(old_count, p), total(new_count, p)
+        least = lax.div(jnp.maximum(old, new) + RUN - 1, RUN) * RUN - RUN
+        most = lax.div(jnp.minimum(old, new), RUN) * RUN + RUN
         return old, jnp.clip(2 * RUN * p, least, most), new
 
-    old0, mid0, new0 = start(device)
-    old1, mid1, new1 = start(device + 1)
-    return jnp.stack([old0, old1, mid0, mid1, new0, new1]).astype(jnp.int32)
+    old0, mid0, new0 = start(device[0])
+    old1, mid1, new1 = start(device[0] + 1)
+    out[OLD0], out[OLD1], out[MID0], out[MID1], out[NEW0], out[NEW1] = old0, old1, mid0, mid1, new0, new1
+    here0 = lax.div(jnp.maximum(old0 - mid0, 0) + RUN - 1, RUN) * RUN
+    here1 = lax.div(jnp.minimum(old1, mid1) - mid0, RUN) * RUN
+    out[HERE0], out[HERE1] = here0, jnp.maximum(here0, here1)
+
+
+def bounds(device, old_count, new_count):
+    return pl.pallas_call(
+        bounds_kernel,
+        in_specs=[SMEM, VMEM, VMEM],
+        out_specs=SMEM,
+        out_shape=jax.ShapeDtypeStruct((8,), jnp.int32),
+    )(device, old_count.reshape(1, -1), new_count.reshape(1, -1))
 
 
 def on_device(devices, spectra, courant, kernel, old_count, new_count, upwind):
-    device = lax.axis_index("blocks").astype(jnp.int32)
+    device = lax.axis_index("blocks").astype(jnp.int32).reshape(1)
     rise = [(i, i + 1) for i in range(devices - 1)]
     fall = [(i + 1, i) for i in range(devices - 1)]
     around = [(i, (i + 1) % devices) for i in range(devices)]
@@ -532,19 +617,18 @@
     def move(block, route):
         return lax.ppermute(block, "blocks", route)
 
-    tail_start = lax.dynamic_slice(old_count, (device,), (1,)) - RUN
-    tail, head = pack(spectra, courant, tail_start)
+    tail, head = pack(old_count, device, spectra, courant)
     low, high = move(tail, rise), move(head, fall)
-    scal = bounds(device, devices, old_count, new_count)
+    scal = bounds(device, old_count, new_count)
     table = upwind[RUN : 2 * RUN].reshape(-1)
     sym = symmetric_kernel(kernel)
+    early = upper_half(scal, table, spectra, courant, sym)
     up, down = faces(scal, table, spectra, courant, low, high)
     below, above = move(up, around), move(down, reverse)
-    q1, cs, side, own_u, up_u, down_u = upper_half(scal, table, spectra, courant, low, high, sym)
-    low_u, high_u = move(up_u, rise), move(down_u, fall)
-    own_l, up_l, down_l = lower_half(scal, table, q1, cs, side, below, above, sym)
-    low_l, high_l = move(up_l, rise), move(down_l, fall)
-    return place(scal, own_u, low_u, high_u, own_l, low_l, high_l)
+    late = upper_half(scal, table, spectra, courant, sym, low, high)
+    own, up, down = lower_half(scal, table, early, late, below, above, sym)
+    low, high = move(up, rise), move(down, fall)
+    return place_moved(scal, low, high, place_own(scal, own))
 
 
 def solution(mesh):

time: 151 us -> 192 us (1.27)
  the two profiles are of different devices: /device:TPU:111 before, /device:TPU:39 now
where the time goes in v3:
time: 192 us; the launch traced here: 189 us
  Pallas kernels  137 us (71%)
  waiting for transfers between devices  27.9 us (15%)
  starting transfers between devices  12.5 us (7%)
  local copies, waits for them, and re-layouts  11.3 us (6%)
    pallas_call x1, Pallas kernels, place_moved(): pl.pallas_call(place_moved_kernel, in_specs=[SMEM, ANY, ANY, ANY], out_sp...  55.6 us
    pallas_call x2, Pallas kernels, upper_half(): pl.pallas_call(functools.partial(upper_kernel, bool(moved)), in_specs=[SM...  30.9 us
    ppermute x6, waiting for transfers between devices, move(): return lax.ppermute(block, 'blocks', route)  27.9 us
    pallas_call x1, Pallas kernels, lower_half(): pl.pallas_call(lower_kernel, in_specs=[SMEM, SMEM] + [VMEM] * 11, out_spe...  24.7 us
    ppermute x6, starting transfers between devices, move(): return lax.ppermute(block, 'blocks', route)  12.5 us
    pallas_call x1, Pallas kernels, symmetric_kernel(): pl.pallas_call(symmetric_kernel_body, grid=(TERMS // 256,), in_specs=[pl....  10.5 us
    unnamed x25, local copies, waits for them, and re-layouts  9.02 us
    pallas_call x1, Pallas kernels, pack(): pl.pallas_call(pack_kernel, in_specs=[SMEM, SMEM, ANY, ANY], out_specs=[A...  4.95 us
  transfers between devices with their start and end apart: 6, of which 4 were waited for; matrix products, arithmetic and copies ran while one was open for 1% of the time, Pallas kernels for 25%

profile of v3, /device:TPU:39, one launch (start us, length us, event | category | flops | bytes accessed | tf_op | source)
XLA Modules:
  0.0 188.7 jit_solution(6353290375260764120)
XLA Ops:
  0.0 1.9 %copy.15.courant = f32[36,3,512]{2,1,0:T(4,128)} copy(f32[36,3,512]{2,0,1:T(8,128)} %param.8) | data formatting | bytes 442368 | tf_op args[1]
  1.9 4.9 %shard_map.76 = (f32[12,72,512]{2,1,0:T(8,128)}, f32[12,72,512]{2,1,0:T(8,128)}) custom-call(s32[128]{0:T(128)} %old_count.1, s32[1]{0:T(128)} %bitcast.device, f32[36,66,512]{2,1,0:T(8,128)} %spectra.7, f32[36,3,512]{2,1,0:T(4,128)} %copy.15.courant), custom_call_target="tpu_custom_call" | custom-call | tf_op jit(solution)/shard_map/pallas_call | solution.py:171
  6.9 3.2 %collective-permute-start = (f32[12,72,512]{2,1,0:T(8,128)}, f32[12,72,512]{2,1,0:T(8,128)S(1)}, u32[]{:S(2)}, u32[]{:S(2)}) collective-permute-start(f32[12,72,512]{2,1,0:T(8,128)} %get-tuple-element.24), channel_id=1, source_target_pairs={{0,1},{1,2},{2,3},{3,4},{4,5},{5,6},{6,7},{7,8},{8,9},{9,10},{10,1... | collective-permute-start | bytes 5308424 | tf_op jit(solution)/shard_map/ppermute | solution.py:618
  10.1 1.9 %collective-permute-start.1 = (f32[12,72,512]{2,1,0:T(8,128)}, f32[12,72,512]{2,1,0:T(8,128)}, u32[]{:S(2)}, u32[]{:S(2)}) collective-permute-start(f32[12,72,512]{2,1,0:T(8,128)} %get-tuple-element.25), channel_id=1, source_target_pairs={{1,0},{2,1},{3,2},{4,3},{5,4},{6,5},{7,6},{8,7},{9,8},{10,9},{11,1... | collective-permute-start | bytes 5308424 | tf_op jit(solution)/shard_map/ppermute | solution.py:618
  13.5 0.8 reshape.15.table
  14.3 1.3 shard_map.73.scal
  15.7 10.5 %shard_map.74.sym.rest_10_ = bf16[80,2304]{1,0:T(8,128)(2,1)S(1)} custom-call(s32[2,2304]{1,0:T(2,128)S(1)} %copy-done.3, bf16[80,4608]{1,0:T(8,128)(2,1)S(1)} %pad.4.kernel), custom_call_target="tpu_custom_call" | custom-call | flops 2000000000 | bytes 1000000 | tf_op jit(solution)/shard_map/pallas_call | solution.py:283
  26.2 3.6 %collective-permute-done.rest_0_.low = f32[12,72,512]{2,1,0:T(8,128)S(1)} collective-permute-done((f32[12,72,512]{2,1,0:T(8,128)}, f32[12,72,512]{2,1,0:T(8,128)S(1)}, u32[]{:S(2)}, u32[]{:S(2)}) %collective-permute-start) | collective-permute-done | bytes 1769504 | tf_op jit(solution)/shard_map/ppermute | solution.py:618
  29.9 6.5 %collective-permute-done.1.rest_1_.high = f32[12,72,512]{2,1,0:T(8,128)} collective-permute-done((f32[12,72,512]{2,1,0:T(8,128)}, f32[12,72,512]{2,1,0:T(8,128)}, u32[]{:S(2)}, u32[]{:S(2)}) %collective-permute-start.1) | collective-permute-done | bytes 1769504 | tf_op jit(solution)/shard_map/ppermute | solution.py:618
  36.4 4.8 %shard_map.78 = (f32[18,72,128]{2,1,0:T(8,128)S(1)}, f32[18,72,128]{2,1,0:T(8,128)S(1)}) custom-call(s32[8]{0:T(128)S(1)} %copy-done.2, s32[36]{0:T(128)S(1)} %reshape.15.table, f32[36,66,512]{2,1,0:T(8,128)S(1)} %bitcast.4, f32[36,3,512]{2,1,0:T(4,128)S(1)} %copy-done.1, f32[12,72,512]{2,1,0:T(8,128)S(1)} %collective-permute-done.rest_0_.low, ...), custom_call_target="tpu_custom_call" | custom-call | tf_op jit(solution)/shard_map/pallas_call | solution.py:224
  41.7 14.7 %shard_map.75 = (f32[36,72,256]{2,1,0:T(8,128)S(1)}, f32[36,24,256]{2,1,0:T(8,128)S(1)}, f32[36,144,128]{2,1,0:T(8,128)}, f32[36,66,256]{2,1,0:T(8,128)}) custom-call(s32[8]{0:T(128)S(1)} %copy-done.2, s32[36]{0:T(128)S(1)} %reshape.15.table, f32[36,66,512]{2,1,0:T(8,128)} %spectra.7, f32[36,3,512]{2,1,0:T(4,128)S(1)} %copy-done.1, ...), custom_call_target="tpu_custom_call" | custom-call | flops 4000000000 | bytes 20000000 | tf_op jit(solution)/shard_map/pallas_call | solution.py:401
  56.5 1.5 copy-done.4
  58.0 0.9 copy-done.6
  58.9 16.2 %shard_map.77 = (f32[36,72,256]{2,1,0:T(8,128)}, f32[36,24,256]{2,1,0:T(8,128)S(1)}, f32[36,144,128]{2,1,0:T(8,128)}, f32[36,66,256]{2,1,0:T(8,128)}) custom-call(s32[8]{0:T(128)S(1)} %copy-done.2, s32[36]{0:T(128)S(1)} %reshape.15.table, f32[36,66,512]{2,1,0:T(8,128)} %spectra.7, f32[36,3,512]{2,1,0:T(4,128)S(1)} %copy-done.1, ...), custom_call_target="tpu_custom_call" | custom-call | flops 4000000000 | bytes 20000000 | tf_op jit(solution)/shard_map/pallas_call | solution.py:401
  75.1 0.9 copy-done.5
  76.1 24.7 %shard_map.79 = (f32[36,66,512]{2,1,0:T(8,128)}, f32[12,66,512]{2,1,0:T(8,128)}, f32[12,66,512]{2,1,0:T(8,128)}) custom-call(s32[8]{0:T(128)S(1)} %copy-done.2, s32[36]{0:T(128)S(1)} %reshape.15.table, f32[36,72,256]{2,1,0:T(8,128)} %copy-done.4, f32[36,24,256]{2,1,0:T(8,128)} %copy-done.6, f32[36,144,128]{2,1,0:T(8,128)} %get-tuple-element.22.rest_2_, ...), custom_call_target="tpu_custom_call" | custom-call | flops 8000000000 | bytes 20000000 | tf_op jit(solution)/shard_map/pallas_call | solution.py:498
  100.8 4.9 %collective-permute-start.4 = (f32[12,66,512]{2,1,0:T(8,128)}, f32[12,66,512]{2,1,0:T(8,128)S(1)}, u32[]{:S(2)}, u32[]{:S(2)}) collective-permute-start(f32[12,66,512]{2,1,0:T(8,128)} %get-tuple-element.32), channel_id=1, source_target_pairs={{0,1},{1,2},{2,3},{3,4},{4,5},{5,6},{6,7},{7,8},{8,9},{9,10},{10,1... | collective-permute-start | bytes 4866056 | tf_op jit(solution)/shard_map/ppermute | solution.py:618
  105.7 1.9 %collective-permute-start.5 = (f32[12,66,512]{2,1,0:T(8,128)}, f32[12,66,512]{2,1,0:T(8,128)S(1)}, u32[]{:S(2)}, u32[]{:S(2)}) collective-permute-start(f32[12,66,512]{2,1,0:T(8,128)} %get-tuple-element.33), channel_id=1, source_target_pairs={{1,0},{2,1},{3,2},{4,3},{5,4},{6,5},{7,6},{8,7},{9,8},{10,9},{11,1... | collective-permute-start | bytes 4866056 | tf_op jit(solution)/shard_map/ppermute | solution.py:618
  107.6 2.5 %copy-done = f32[36,66,512]{2,1,0:T(8,128)S(1)} copy-done((f32[36,66,512]{2,1,0:T(8,128)S(1)}, f32[36,66,512]{2,1,0:T(8,128)}, u32[]{:S(2)}) %copy-start) | copy-done | bytes 4866072
  110.1 3.9 %shard_map.80._ = f32[36,66,512]{2,1,0:T(8,128)} custom-call(s32[8]{0:T(128)S(1)} %copy-done.2, f32[36,66,512]{2,1,0:T(8,128)S(1)} %copy-done), custom_call_target="tpu_custom_call" | custom-call | flops 1000000 | bytes 11000000 | tf_op jit(solution)/shard_map/pallas_call | solution.py:538
  114.1 11.4 %collective-permute-done.4.low = f32[12,66,512]{2,1,0:T(8,128)S(1)} collective-permute-done((f32[12,66,512]{2,1,0:T(8,128)}, f32[12,66,512]{2,1,0:T(8,128)S(1)}, u32[]{:S(2)}, u32[]{:S(2)}) %collective-permute-start.4) | collective-permute-done | bytes 1622048 | tf_op jit(solution)/shard_map/ppermute | solution.py:618
  125.5 6.4 %collective-permute-done.5.high = f32[12,66,512]{2,1,0:T(8,128)S(1)} collective-permute-done((f32[12,66,512]{2,1,0:T(8,128)}, f32[12,66,512]{2,1,0:T(8,128)S(1)}, u32[]{:S(2)}, u32[]{:S(2)}) %collective-permute-start.5) | collective-permute-done | bytes 1622048 | tf_op jit(solution)/shard_map/ppermute | solution.py:618
  131.9 1.2 copy-done.8
  133.1 55.6 %shard_map.81 = f32[36,66,512]{2,1,0:T(8,128)} custom-call(s32[8]{0:T(128)} %shard_map.73.scal, f32[12,66,512]{2,1,0:T(8,128)} %copy-done.7, f32[12,66,512]{2,1,0:T(8,128)} %copy-done.8, f32[36,66,512]{2,1,0:T(8,128)} %shard_map.80._), custom_call_target="tpu_custom_call", output_to_operand_aliasing={{}: (3, {})} | custom-call | tf_op jit(solution)/shard_map/pallas_call | solution.py:570
  (27 shorter events, 2.1 us)
Async XLA Ops:
  0.0 36.4 %slice-start = ((s8[5308416]{0:T(1024)(128)(4,1)}), s8[1114112]{0:T(1024)(128)(4,1)S(1)}, s32[]{:S(2)}) async-start(s8[5308416]{0:T(1024)(128)(4,1)} %bitcast.3), calls=%async_computation | async-start | bytes 2228224
  1.9 13.7 %copy-start.9 = (bf16[66,4356]{1,0:T(8,128)(2,1)S(1)}, bf16[66,4356]{1,0:T(8,128)(2,1)}, u32[]{:S(2)}) copy-start(bf16[66,4356]{1,0:T(8,128)(2,1)} %param.9) | copy-start | bytes 1724980
  1.9 13.8 %copy-start.3 = (s32[2,2304]{1,0:T(2,128)S(1)}, s32[2,2304]{1,0:T(2,128)}, u32[]{:S(2)}) copy-start(s32[2,2304]{1,0:T(2,128)} %constant.9.clone.columns) | copy-start | bytes 55300
  6.9 23.0 %collective-permute-start = (f32[12,72,512]{2,1,0:T(8,128)}, f32[12,72,512]{2,1,0:T(8,128)S(1)}, u32[]{:S(2)}, u32[]{:S(2)}) collective-permute-start(f32[12,72,512]{2,1,0:T(8,128)} %get-tuple-element.24), channel_id=1, source_target_pairs={{0,1},{1,2},{2,3},{3,4},{4,5},{5,6},{6,7},{7,8},{8,9},{9,10},{10,1... | collective-permute-start | bytes 5308424 | tf_op jit(solution)/shard_map/ppermute | solution.py:618
  10.1 26.3 %collective-permute-start.1 = (f32[12,72,512]{2,1,0:T(8,128)}, f32[12,72,512]{2,1,0:T(8,128)}, u32[]{:S(2)}, u32[]{:S(2)}) collective-permute-start(f32[12,72,512]{2,1,0:T(8,128)} %get-tuple-element.25), channel_id=1, source_target_pairs={{1,0},{2,1},{3,2},{4,3},{5,4},{6,5},{7,6},{8,7},{9,8},{10,9},{11,1... | collective-permute-start | bytes 5308424 | tf_op jit(solution)/shard_map/ppermute | solution.py:618
  15.6 20.8 %slice-start.1 = ((s8[5308416]{0:T(1024)(128)(4,1)}), s8[4194304]{0:T(1024)(128)(4,1)S(1)}, s32[]{:S(2)}) async-start(s8[5308416]{0:T(1024)(128)(4,1)} %bitcast.3), calls=%async_computation.1 | async-start | bytes 8388608
  15.7 20.7 %copy-start.1 = (f32[36,3,512]{2,1,0:T(4,128)S(1)}, f32[36,3,512]{2,1,0:T(4,128)}, u32[]{:S(2)}) copy-start(f32[36,3,512]{2,1,0:T(4,128)} %copy.15.courant) | copy-start | bytes 663556
  15.7 20.7 %copy-start.2 = (s32[8]{0:T(128)S(1)}, s32[8]{0:T(128)}, u32[]{:S(2)}) copy-start(s32[8]{0:T(128)} %shard_map.73.scal) | copy-start | bytes 100
  41.2 34.9 %collective-permute-start.2 = (f32[18,72,128]{2,1,0:T(8,128)S(1)}, f32[18,72,128]{2,1,0:T(8,128)S(1)}, u32[]{:S(2)}, u32[]{:S(2)}) collective-permute-start(f32[18,72,128]{2,1,0:T(8,128)S(1)} %get-tuple-element.30), channel_id=1, source_target_pairs={{0,1},{1,2},{2,3},{3,4},{4,5},{5,6},{6,7},{7,8},{8,9},{9,10},{10,1... | collective-permute-start | bytes 1990664 | tf_op jit(solution)/shard_map/ppermute | solution.py:618
  41.3 34.8 %collective-permute-start.3 = (f32[18,72,128]{2,1,0:T(8,128)S(1)}, f32[18,72,128]{2,1,0:T(8,128)S(1)}, u32[]{:S(2)}, u32[]{:S(2)}) collective-permute-start(f32[18,72,128]{2,1,0:T(8,128)S(1)} %get-tuple-element.31), channel_id=1, source_target_pairs={{1,0},{2,1},{3,2},{4,3},{5,4},{6,5},{7,6},{8,7},{9,8},{10,9},{11,1... | collective-permute-start | bytes 1990664 | tf_op jit(solution)/shard_map/ppermute | solution.py:618
  56.5 1.5 copy-start.4
  58.0 0.9 copy-start.6
  75.1 0.9 copy-start.5
  100.8 24.7 %collective-permute-start.4 = (f32[12,66,512]{2,1,0:T(8,128)}, f32[12,66,512]{2,1,0:T(8,128)S(1)}, u32[]{:S(2)}, u32[]{:S(2)}) collective-permute-start(f32[12,66,512]{2,1,0:T(8,128)} %get-tuple-element.32), channel_id=1, source_target_pairs={{0,1},{1,2},{2,3},{3,4},{4,5},{5,6},{6,7},{7,8},{8,9},{9,10},{10,1... | collective-permute-start | bytes 4866056 | tf_op jit(solution)/shard_map/ppermute | solution.py:618
  105.7 26.2 %collective-permute-start.5 = (f32[12,66,512]{2,1,0:T(8,128)}, f32[12,66,512]{2,1,0:T(8,128)S(1)}, u32[]{:S(2)}, u32[]{:S(2)}) collective-permute-start(f32[12,66,512]{2,1,0:T(8,128)} %get-tuple-element.33), channel_id=1, source_target_pairs={{1,0},{2,1},{3,2},{4,3},{5,4},{6,5},{7,6},{8,7},{9,8},{10,9},{11,1... | collective-permute-start | bytes 4866056 | tf_op jit(solution)/shard_map/ppermute | solution.py:618
  107.6 2.5 %copy-start = (f32[36,66,512]{2,1,0:T(8,128)S(1)}, f32[36,66,512]{2,1,0:T(8,128)}, u32[]{:S(2)}) copy-start(f32[36,66,512]{2,1,0:T(8,128)} %get-tuple-element.34.own) | copy-start | bytes 14598148
  125.4 6.4 %copy-start.7 = (f32[12,66,512]{2,1,0:T(8,128)}, f32[12,66,512]{2,1,0:T(8,128)S(1)}, u32[]{:S(2)}) copy-start(f32[12,66,512]{2,1,0:T(8,128)S(1)} %collective-permute-done.4.low) | copy-start | bytes 4866052
  131.9 1.2 copy-start.8

commit v4 on v3

--- a/solution.py
+++ b/solution.py
@@ -268,11 +268,12 @@
 
 def symmetric_kernel_body(columns, kernel, out):
     width = out.shape[1]
-    one, two = columns[0:1], columns[1:2]
+    row = lax.broadcasted_iota(jnp.int32, (256, width), 0).astype(F32).astype(jnp.bfloat16)
     picks = []
     for base in range(0, kernel.shape[1], 256):
-        row = lax.broadcasted_iota(jnp.int32, (256, width), 0) + base
-        picks.append(jnp.where((row == one) | (row == two), 1.0, 0.0).astype(jnp.bfloat16))
+        near = jnp.clip(columns[...] - base, -1, 256).astype(F32).astype(jnp.bfloat16)
+        hit = (row == near[0:1]) | (row == near[1:2])
+        picks.append(jnp.where(hit, jnp.bfloat16(1), jnp.bfloat16(0)))
     total = jnp.dot(kernel[...], jnp.concatenate(picks, axis=0), preferred_element_type=F32)
     out[...] = total.astype(jnp.bfloat16)
 
@@ -332,33 +333,26 @@
     return (y_in - y_own) + (z_in - z_own)
 
 
-def coalesce_all(count, block_at, second, q2, sym, out):
-    def third(i, _):
-        l = block_at(i)
-        out[l, :, 0:HALF] = coalesce(q2[l], sym)[0:BINS]
-        second(block_at(jnp.minimum(i + 1, count - 1)))
-        return 0
-
-    @pl.when(count > 0)
-    def _():
-        second(block_at(0))
-
-    lax.fori_loop(0, count, third, 0)
-
-
-def upper_kernel(received, scal, table, spectra, courant, sym, *rest):
-    low, high = rest[:2] if received else (None, None)
-    low_q1, low_c, face, out, q0, cs, q1, fy, fz, q2 = rest[2 if received else 0 :]
+def upper_kernel(moved, scal, table, spectra, courant, sym, *rest):
+    low, high = rest[:2] if moved else (None, None)
+    to_q1, to_c, to_face, to_out, scal_out, low_q1, low_c, face, out, q0, cs, q1, fy, fz, q2, sems = rest[6 if moved else 0 :]
+    for k in range(8):
+        scal_out[k] = scal[k]
     here0, here = scal[HERE0], scal[HERE1] - scal[HERE0]
-    count = scal[MID1] - scal[MID0] - here if received else here
+    count = scal[MID1] - scal[MID0] - here if moved else here
 
     def block_at(i):
-        return i + jnp.where(i >= here0, here, 0) if received else i + here0
+        return i + jnp.where(i >= here0, here, 0) if moved else i + here0
+
+    def copy(k, l):
+        source, target = ((low_q1, to_q1), (low_c, to_c), (face, to_face), (out, to_out))[k]
+        return pltpu.make_async_copy(source.at[l], target.at[l], sems.at[k, l])
 
     def gather(i, _):
         l = block_at(i)
         fetch(scal[MID0] + l, scal, spectra, courant, low, high, q0, cs, l)
         low_c[l] = cs[l, :, 0:HALF]
+        copy(1, l).start()
         return 0
 
     lax.fori_loop(0, count, gather, 0)
@@ -377,6 +371,8 @@
         other = swap(new)
         face[l, 0:PACKED] = flat(jnp.where(upper(), limited(new, cx_prev, other), other))
         face[l, PACKED : 2 * PACKED] = flat(cx_prev * q_prev)
+        copy(0, l).start()
+        copy(2, l).start()
         return 0
 
     lax.fori_loop(0, count, first, 0)
@@ -392,62 +388,94 @@
             q2[l, :, span(w)] = flat(new)
             q_prev, f_prev = q, f
 
-    coalesce_all(count, block_at, second, q2, sym, out)
+    @pl.when(count > 0)
+    def _():
+        second(block_at(0))
+
+    def third(i, _):
+        l = block_at(i)
+        out[l] = coalesce(q2[l], sym)[0:BINS]
+        second(block_at(jnp.minimum(i + 1, count - 1)))
+        copy(3, l).start()
+        return 0
+
+    lax.fori_loop(0, count, third, 0)
+
+    def drain(i, _):
+        for k in range(4):
+            copy(k, block_at(i)).wait()
+        return 0
+
+    lax.fori_loop(0, count, drain, 0)
 
 
 def upper_half(scal, table, spectra, courant, sym, *moved):
     capacity = spectra.shape[0]
-    held = pltpu.VMEM((capacity, PACKED, HALF), F32)
+    held = (capacity, PACKED, HALF)
+    shapes = [held, (capacity, 24, HALF), (capacity, 2 * PACKED, LANES), (capacity, BINS, HALF)]
     return pl.pallas_call(
         functools.partial(upper_kernel, bool(moved)),
-        in_specs=[SMEM, SMEM] + [VMEM] * (3 + len(moved)),
-        out_specs=[VMEM] * 4,
-        out_shape=[
-            jax.ShapeDtypeStruct((capacity, PACKED, HALF), F32),
-            jax.ShapeDtypeStruct((capacity, 24, HALF), F32),
-            jax.ShapeDtypeStruct((capacity, 2 * PACKED, LANES), F32),
-            jax.ShapeDtypeStruct((capacity, BINS, HALF), F32),
-        ],
-        scratch_shapes=[
-            pltpu.VMEM((capacity, PACKED, CELLS), F32),
-            pltpu.VMEM((capacity, 24, CELLS), F32),
-            held,
-            held,
-            held,
-            held,
-        ],
-        compiler_params=params(48),
+        in_specs=[SMEM, SMEM] + [VMEM] * 3 + ([VMEM] * 2 + [ANY] * 4 if moved else []),
+        out_specs=[ANY] * 4 + [SMEM],
+        out_shape=[jax.ShapeDtypeStruct(shape, F32) for shape in shapes] + [jax.ShapeDtypeStruct((8,), jnp.int32)],
+        scratch_shapes=[pltpu.VMEM(shape, F32) for shape in shapes]
+        + [pltpu.VMEM((capacity, PACKED, CELLS), F32), pltpu.VMEM((capacity, 24, CELLS), F32)]
+        + [pltpu.VMEM(held, F32)] * 4
+        + [pltpu.SemaphoreType.DMA((4, capacity))],
+        input_output_aliases={7: 0, 8: 1, 9: 2, 10: 3} if moved else {},
+        compiler_params=params(40),
         cost_estimate=pl.CostEstimate(flops=4 * 10**9, bytes_accessed=20 * 10**6, transcendentals=0),
     )(scal, table, spectra, courant, sym, *moved)
 
 
-def lower_kernel(scal, table, *rest):
-    early, late = rest[0:4], rest[4:8]
-    below, above, sym, own, up, down, q1, cs, fy, fz, fx, q2 = rest[8:]
+def lower_kernel(scal, table, from_q1, from_c, from_face, from_out, below, above, sym, result, up, down, q1, cs, face, own, fy, fz, fx, q2, blank, sems, out_sems, blank_sems):
     count = scal[MID1] - scal[MID0]
-
-    def choose(l, take):
-        was_here = (l >= scal[HERE0]) & (l < scal[HERE1])
-        pl.when(was_here)(functools.partial(take, *early))
-        pl.when(jnp.logical_not(was_here))(functools.partial(take, *late))
+    slots = scal[NEW1] - scal[NEW0]
+
+    def copy(k, l):
+        source, target = ((from_q1, q1), (from_c, cs), (from_face, face))[k]
+        return pltpu.make_async_copy(source.at[l], target.at[l], sems.at[k, l])
+
+    def copy_out(l):
+        return pltpu.make_async_copy(from_out.at[l], own.at[l, :, HALF:CELLS], sems.at[3, l])
+
+    def begin(l, _):
+        for k in range(3):
+            copy(k, l).start()
+        copy_out(l).start()
+        return 0
+
+    lax.fori_loop(0, count, begin, 0)
+
+    def clear(s):
+        return pltpu.make_async_copy(blank, result.at[s], blank_sems.at[s])
+
+    blank[...] = jnp.zeros(blank.shape, F32)
+
+    def clear_start(s, _):
+        clear(s).start()
+        return 0
+
+    lax.fori_loop(slots, result.shape[0], clear_start, 0)
+
+    def arrive(l, _):
+        for k in range(3):
+            copy(k, l).wait()
+        copy_out(l).wait()
+        return 0
+
+    lax.fori_loop(0, count, arrive, 0)
 
     def fix(l, _):
         position = lax.rem(l, RUN)
         ux, _, _ = neighbours(table, l)
 
-        def take(low_q1, low_c, face, out):
-            q1[l] = low_q1[l]
-            cs[l] = low_c[l]
-            own[l, :, HALF:CELLS] = out[l]
-
-        choose(l, take)
-
         def add_flux(flux):
             q1[l, :, span(0)] += flat(jnp.where(upper(), 0.0, flux))
 
-        def remote(face):
-            fx[l] = face[position]
-            flux = view(face[RUN + position // 2])
+        def remote(side):
+            fx[l] = side[position]
+            flux = view(side[RUN + position // 2])
             add_flux(jnp.where(lax.rem(position, 2) == 0, flux, swap(flux)))
 
         @pl.when(ux < 0)
@@ -460,11 +488,8 @@
 
         @pl.when((ux >= 0) & (ux < count))
         def _():
-            def take_face(low_q1, low_c, face, out):
-                fx[l] = face[ux, 0:PACKED]
-                add_flux(swap(view(face[ux, PACKED : 2 * PACKED])))
-
-            choose(ux, take_face)
+            fx[l] = face[ux, 0:PACKED]
+            add_flux(swap(view(face[ux, PACKED : 2 * PACKED])))
 
         return 0
 
@@ -472,77 +497,84 @@
     cross_flux(count, lambda i: i, table, q1, cs, fy, fz, 0, 0)
 
     def second(l):
-        face = view(fx[l])
+        side = view(fx[l])
         q = read(q1, l, 0)
-        f = limited(q, speed(cs, l, 0, 0), jnp.where(upper(), swap(q), face))
-        q2[l, :, span(0)] = flat(q - f + swap(jnp.where(upper(), face, f)) + cross(table, l, fy, fz, 0))
+        f = limited(q, speed(cs, l, 0, 0), jnp.where(upper(), swap(q), side))
+        q2[l, :, span(0)] = flat(q - f + swap(jnp.where(upper(), side, f)) + cross(table, l, fy, fz, 0))
         q_prev, f_prev = q, f
         q = read(q1, l, 1)
         f = limited(q, speed(cs, l, 0, 1), swap(jnp.where(upper(), q_prev, q)))
         q2[l, :, span(1)] = flat(q - f + swap(jnp.where(upper(), f_prev, f)) + cross(table, l, fy, fz, 1))
 
-    coalesce_all(count, lambda i: i, second, q2, sym, own)
-
-    def hand_on(k, _):
-        down[k] = own[k]
-        up[k] = own[count - RUN + k]
-        return 0
-
-    lax.fori_loop(0, RUN, hand_on, 0)
-
-
-def lower_half(scal, table, early, late, below, above, sym):
-    capacity = early[0].shape[0]
+    second(0)
+
+    def third(l, _):
+        own[l, :, 0:HALF] = coalesce(q2[l], sym)[0:BINS]
+        second(jnp.minimum(l + 1, count - 1))
+        return 0
+
+    def leave(act):
+        def body(l, _):
+            s = scal[MID0] + l - scal[NEW0]
+
+            @pl.when(l < RUN)
+            def _():
+                act(pltpu.make_async_copy(own.at[l], down.at[l], out_sems.at[0, l]))
+
+            @pl.when(l >= count - RUN)
+            def _():
+                act(pltpu.make_async_copy(own.at[l], up.at[l - (count - RUN)], out_sems.at[1, l]))
+
+            @pl.when((s >= 0) & (s < slots))
+            def _():
+                act(pltpu.make_async_copy(own.at[l], result.at[s], out_sems.at[2, l]))
+
+            return 0
+
+        return body
+
+    def one_run(r, _):
+        lax.fori_loop(r * RUN, r * RUN + RUN, third, 0)
+        lax.fori_loop(r * RUN, r * RUN + RUN, leave(lambda copy: copy.start()), 0)
+        return 0
+
+    lax.fori_loop(0, lax.div(count, RUN), one_run, 0)
+    lax.fori_loop(0, count, leave(lambda copy: copy.wait()), 0)
+
+    def clear_wait(s, _):
+        clear(s).wait()
+        return 0
+
+    lax.fori_loop(slots, result.shape[0], clear_wait, 0)
+
+
+def lower_half(scal, table, arrays, below, above, sym):
+    capacity = arrays[0].shape[0]
+    whole = jax.ShapeDtypeStruct((capacity, BINS, CELLS), F32)
     sent = jax.ShapeDtypeStruct((RUN, BINS, CELLS), F32)
     held = pltpu.VMEM((capacity, PACKED, HALF), F32)
     return pl.pallas_call(
         lower_kernel,
-        in_specs=[SMEM, SMEM] + [VMEM] * 11,
-        out_specs=[VMEM] * 3,
-        out_shape=[jax.ShapeDtypeStruct((capacity, BINS, CELLS), F32), sent, sent],
+        in_specs=[SMEM, SMEM] + [ANY] * 4 + [VMEM] * 3,
+        out_specs=[ANY] * 3,
+        out_shape=[whole, sent, sent],
         scratch_shapes=[
             held,
             pltpu.VMEM((capacity, 24, HALF), F32),
+            pltpu.VMEM((capacity, 2 * PACKED, LANES), F32),
+            pltpu.VMEM((capacity, BINS, CELLS), F32),
             held,
             held,
             pltpu.VMEM((capacity, PACKED, LANES), F32),
             held,
+            pltpu.VMEM((BINS, CELLS), F32),
+            pltpu.SemaphoreType.DMA((4, capacity)),
+            pltpu.SemaphoreType.DMA((3, capacity)),
+            pltpu.SemaphoreType.DMA((capacity,)),
         ],
-        compiler_params=params(52),
+        compiler_params=params(32),
         cost_estimate=pl.CostEstimate(flops=8 * 10**9, bytes_accessed=20 * 10**6, transcendentals=0),
-    )(scal, table, *early, *late, below, above, sym)
-
-
-def place_own_kernel(scal, own, out):
-    start, end = scal[MID0], scal[MID1]
-    count = scal[NEW1] - scal[NEW0]
-
-    def body(s, _):
-        block = scal[NEW0] + s
-        mine = (s < count) & (block >= start) & (block < end)
-
-        @pl.when(mine)
-        def _():
-            out[s] = own[block - start]
-
-        @pl.when(jnp.logical_not(mine))
-        def _():
-            out[s] = jnp.zeros((BINS, CELLS), F32)
-
-        return 0
-
-    lax.fori_loop(0, out.shape[0], body, 0)
-
-
-def place_own(scal, own):
-    return pl.pallas_call(
-        place_own_kernel,
-        in_specs=[SMEM, VMEM],
-        out_specs=VMEM,
-        out_shape=own,
-        compiler_params=params(24),
-        cost_estimate=pl.CostEstimate(flops=10**6, bytes_accessed=11 * 10**6, transcendentals=0),
-    )(scal, own)
+    )(scal, table, *arrays, below, above, sym)
 
 
 def place_moved_kernel(scal, low, high, _, out, sems):
@@ -569,12 +601,12 @@
 def place_moved(scal, low, high, out):
     return pl.pallas_call(
         place_moved_kernel,
-        in_specs=[SMEM, ANY, ANY, ANY],
+        in_specs=[SMEM, VMEM, VMEM, ANY],
         out_specs=ANY,
         out_shape=jax.ShapeDtypeStruct(out.shape, F32),
         scratch_shapes=[pltpu.SemaphoreType.DMA((2, RUN))],
         input_output_aliases={3: 0},
-        compiler_params=params(56),
+        compiler_params=params(8),
     )(scal, low, high, out)
 
 
@@ -622,13 +654,13 @@
     scal = bounds(device, old_count, new_count)
     table = upwind[RUN : 2 * RUN].reshape(-1)
     sym = symmetric_kernel(kernel)
-    early = upper_half(scal, table, spectra, courant, sym)
+    *early, scal = upper_half(scal, table, spectra, courant, sym)
     up, down = faces(scal, table, spectra, courant, low, high)
     below, above = move(up, around), move(down, reverse)
-    late = upper_half(scal, table, spectra, courant, sym, low, high)
-    own, up, down = lower_half(scal, table, early, late, below, above, sym)
+    *arrays, scal = upper_half(scal, table, spectra, courant, sym, low, high, *early)
+    result, up, down = lower_half(scal, table, arrays, below, above, sym)
     low, high = move(up, rise), move(down, fall)
-    return place_moved(scal, low, high, place_own(scal, own))
+    return place_moved(scal, low, high, result)
 
 
 def solution(mesh):

time: 192 us -> 141 us (0.73)
  the two profiles are of different devices: /device:TPU:39 before, /device:TPU:111 now
where the time goes in v4:
time: 141 us; the launch traced here: 142 us
  Pallas kernels  81.6 us (58%)
  waiting for transfers between devices  35.6 us (25%)
  starting transfers between devices  19.8 us (14%)
  local copies, waits for them, and re-layouts  4.65 us (3%)
    pallas_call x2, Pallas kernels, upper_half(): pl.pallas_call(functools.partial(upper_kernel, bool(moved)), in_specs=[SM...  36.3 us
    ppermute x6, waiting for transfers between devices, move(): return lax.ppermute(block, 'blocks', route)  35.6 us
    pallas_call x1, Pallas kernels, lower_half(): pl.pallas_call(lower_kernel, in_specs=[SMEM, SMEM] + [ANY] * 4 + [VMEM] *...  29.1 us
    ppermute x6, starting transfers between devices, move(): return lax.ppermute(block, 'blocks', route)  19.8 us
    pallas_call x1, Pallas kernels, symmetric_kernel(): pl.pallas_call(symmetric_kernel_body, grid=(TERMS // 256,), in_specs=[pl....  5.05 us
    pallas_call x1, Pallas kernels, pack(): pl.pallas_call(pack_kernel, in_specs=[SMEM, SMEM, ANY, ANY], out_specs=[A...  4.03 us
    pallas_call x1, Pallas kernels, faces(): pl.pallas_call(face_kernel, grid=(1,), in_specs=[SMEM, SMEM, half(capacit...  3.89 us
  transfers between devices with their start and end apart: 6, of which 4 were waited for; matrix products, arithmetic and copies ran while one was open for 1% of the time, Pallas kernels for 30%

profile of v4, /device:TPU:111, one launch (start us, length us, event | category | flops | bytes accessed | tf_op | source)
XLA Modules:
  0.0 141.8 jit_solution(5109111452744898200)
XLA Ops:
  0.0 1.8 %copy.19.courant = f32[36,3,512]{2,1,0:T(4,128)} copy(f32[36,3,512]{2,0,1:T(8,128)} %param.8) | data formatting | bytes 442368 | tf_op args[1]
  1.8 4.0 %shard_map.76 = (f32[12,72,512]{2,1,0:T(8,128)}, f32[12,72,512]{2,1,0:T(8,128)}) custom-call(s32[128]{0:T(128)} %old_count.1, s32[1]{0:T(128)} %bitcast.device, f32[36,66,512]{2,1,0:T(8,128)} %spectra.7, f32[36,3,512]{2,1,0:T(4,128)} %copy.19.courant), custom_call_target="tpu_custom_call" | custom-call | tf_op jit(solution)/shard_map/pallas_call | solution.py:171
  5.9 3.2 %collective-permute-start = (f32[12,72,512]{2,1,0:T(8,128)}, f32[12,72,512]{2,1,0:T(8,128)S(1)}, u32[]{:S(2)}, u32[]{:S(2)}) collective-permute-start(f32[12,72,512]{2,1,0:T(8,128)} %get-tuple-element.23), channel_id=1, source_target_pairs={{0,1},{1,2},{2,3},{3,4},{4,5},{5,6},{6,7},{7,8},{8,9},{9,10},{10,1... | collective-permute-start | bytes 5308424 | tf_op jit(solution)/shard_map/ppermute | solution.py:650
  9.1 1.9 %collective-permute-start.1 = (f32[12,72,512]{2,1,0:T(8,128)}, f32[12,72,512]{2,1,0:T(8,128)S(1)}, u32[]{:S(2)}, u32[]{:S(2)}) collective-permute-start(f32[12,72,512]{2,1,0:T(8,128)} %get-tuple-element.24), channel_id=1, source_target_pairs={{1,0},{2,1},{3,2},{4,3},{5,4},{6,5},{7,6},{8,7},{9,8},{10,9},{11,1... | collective-permute-start | bytes 5308424 | tf_op jit(solution)/shard_map/ppermute | solution.py:650
  11.0 0.8 slice.3
  11.8 0.1 copy.18
  11.9 0.1 reshape.15.table
  12.0 1.3 shard_map.73.scal
  13.3 1.1 pad.4.kernel
  14.5 0.7 copy-done.2
  15.2 5.0 %shard_map.74.sym = bf16[80,2304]{1,0:T(8,128)(2,1)S(1)} custom-call(s32[2,2304]{1,0:T(2,128)S(1)} %copy-done.2, bf16[80,4608]{1,0:T(8,128)(2,1)S(1)} %pad.4.kernel), custom_call_target="tpu_custom_call" | custom-call | flops 2000000000 | bytes 1000000 | tf_op jit(solution)/shard_map/pallas_call | solution.py:284
  20.3 31.9 %shard_map.75 = (f32[36,72,256]{2,1,0:T(8,128)S(1)}, f32[36,24,256]{2,1,0:T(8,128)S(1)}, f32[36,144,128]{2,1,0:T(8,128)S(1)}, f32[36,66,256]{2,1,0:T(8,128)S(1)}, s32[8]{0:T(128)S(1)}) custom-call(s32[8]{0:T(128)S(1)} %copy-done.1, s32[36]{0:T(128)S(1)} %reshape.15.table, f32[36,66,512]{2,1,0:T(8,128)} %spectra.7, f32[36,3,512]{2,1,0:T(4,128)S(1)} %copy-done, ...), custom_call_target="tpu_custom_call" | custom-call | flops 4000000000 | bytes 20000000 | tf_op jit(solution)/shard_map/pallas_call | solution.py:416
  52.2 3.9 %shard_map.78 = (f32[18,72,128]{2,1,0:T(8,128)S(1)}, f32[18,72,128]{2,1,0:T(8,128)S(1)}) custom-call(s32[8]{0:T(128)S(1)} %get-tuple-element.22.scal, s32[36]{0:T(128)S(1)} %reshape.15.table, f32[36,66,512]{2,1,0:T(8,128)S(1)} %bitcast.4, f32[36,3,512]{2,1,0:T(4,128)S(1)} %copy-done, f32[12,72,512]{2,1,0:T(8,128)S(1)} %collective-permute-done.rest_0_.low, ...), custom_call_target="tpu_custom_call" | custom-call | tf_op jit(solution)/shard_map/pallas_call | solution.py:224
  56.1 0.1 collective-permute-start.2
  56.2 0.5 collective-permute-start.3
  56.7 4.4 %shard_map.77 = (f32[36,72,256]{2,1,0:T(8,128)S(1)}, f32[36,24,256]{2,1,0:T(8,128)S(1)}, f32[36,144,128]{2,1,0:T(8,128)S(1)}, f32[36,66,256]{2,1,0:T(8,128)S(1)}, s32[8]{0:T(128)S(1)}) custom-call(s32[8]{0:T(128)S(1)} %get-tuple-element.22.scal, s32[36]{0:T(128)S(1)} %reshape.15.table, ...), custom_call_target="tpu_custom_call", output_to_operand_aliasing={{0}: (7, {}), {1}: (8, {}), {2}: (9, {}), {3}: (10, {})} | custom-call | flops 4000000000 | bytes 20000000 | tf_op jit(solution)/shard_map/pallas_call | solution.py:416
  61.1 2.7 %collective-permute-done.2.below = f32[18,72,128]{2,1,0:T(8,128)S(1)} collective-permute-done((f32[18,72,128]{2,1,0:T(8,128)S(1)}, f32[18,72,128]{2,1,0:T(8,128)S(1)}, u32[]{:S(2)}, u32[]{:S(2)}) %collective-permute-start.2) | collective-permute-done | bytes 663584 | tf_op jit(solution)/shard_map/ppermute | solution.py:650
  63.8 6.8 %collective-permute-done.3.above = f32[18,72,128]{2,1,0:T(8,128)S(1)} collective-permute-done((f32[18,72,128]{2,1,0:T(8,128)S(1)}, f32[18,72,128]{2,1,0:T(8,128)S(1)}, u32[]{:S(2)}, u32[]{:S(2)}) %collective-permute-start.3) | collective-permute-done | bytes 663584 | tf_op jit(solution)/shard_map/ppermute | solution.py:650
  70.6 29.1 %shard_map.79 = (f32[36,66,512]{2,1,0:T(8,128)}, f32[12,66,512]{2,1,0:T(8,128)S(1)}, f32[12,66,512]{2,1,0:T(8,128)S(1)}) custom-call(s32[8]{0:T(128)S(1)} %get-tuple-element.29.scal, s32[36]{0:T(128)S(1)} %reshape.15.table, f32[36,72,256]{2,1,0:T(8,128)S(1)} %get-tuple-element.30.from_q1, f32[36,24,256]{2,1,0:T(8,128)S(1)} %get-tuple-element.31.from_c, ...), custom_call_target="tpu_custom_call" | custom-call | flops 8000000000 | bytes 20000000 | tf_op jit(solution)/shard_map/pallas_call | solution.py:556
  99.7 12.2 %collective-permute-start.4 = (f32[12,66,512]{2,1,0:T(8,128)S(1)}, f32[12,66,512]{2,1,0:T(8,128)S(1)}, u32[]{:S(2)}, u32[]{:S(2)}) collective-permute-start(f32[12,66,512]{2,1,0:T(8,128)S(1)} %get-tuple-element.36), channel_id=1, source_target_pairs={{0,1},{1,2},{2,3},{3,4},{4,5},{5,6},{6,7},{7,8},{8,9},{9,10},{10,1... | collective-permute-start | bytes 4866056 | tf_op jit(solution)/shard_map/ppermute | solution.py:650
  111.9 1.9 %collective-permute-start.5 = (f32[12,66,512]{2,1,0:T(8,128)S(1)}, f32[12,66,512]{2,1,0:T(8,128)S(1)}, u32[]{:S(2)}, u32[]{:S(2)}) collective-permute-start(f32[12,66,512]{2,1,0:T(8,128)S(1)} %get-tuple-element.37), channel_id=1, source_target_pairs={{1,0},{2,1},{3,2},{4,3},{5,4},{6,5},{7,6},{8,7},{9,8},{10,9},{11,1... | collective-permute-start | bytes 4866056 | tf_op jit(solution)/shard_map/ppermute | solution.py:650
  113.9 17.5 %collective-permute-done.4.low = f32[12,66,512]{2,1,0:T(8,128)S(1)} collective-permute-done((f32[12,66,512]{2,1,0:T(8,128)S(1)}, f32[12,66,512]{2,1,0:T(8,128)S(1)}, u32[]{:S(2)}, u32[]{:S(2)}) %collective-permute-start.4) | collective-permute-done | bytes 1622048 | tf_op jit(solution)/shard_map/ppermute | solution.py:650
  131.4 8.6 %collective-permute-done.5.high = f32[12,66,512]{2,1,0:T(8,128)S(1)} collective-permute-done((f32[12,66,512]{2,1,0:T(8,128)S(1)}, f32[12,66,512]{2,1,0:T(8,128)S(1)}, u32[]{:S(2)}, u32[]{:S(2)}) %collective-permute-start.5) | collective-permute-done | bytes 1622048 | tf_op jit(solution)/shard_map/ppermute | solution.py:650
  140.0 1.8 %shard_map.80 = f32[36,66,512]{2,1,0:T(8,128)} custom-call(s32[8]{0:T(128)S(1)} %get-tuple-element.29.scal, f32[12,66,512]{2,1,0:T(8,128)S(1)} %collective-permute-done.4.low, f32[12,66,512]{2,1,0:T(8,128)S(1)} %collective-permute-done.5.high, f32[36,66,512]{2,1,0:T(8,128)} %get-tuple-element.38._), custom_call_target="tpu_custom_call", output_to_operand_aliasing={{}: (3, {})} | custom-call | tf_op jit(solution)/shard_map/pallas_call | solution.py:602
  (12 shorter events, 0.0 us)
Async XLA Ops:
  5.9 46.3 %collective-permute-start = (f32[12,72,512]{2,1,0:T(8,128)}, f32[12,72,512]{2,1,0:T(8,128)S(1)}, u32[]{:S(2)}, u32[]{:S(2)}) collective-permute-start(f32[12,72,512]{2,1,0:T(8,128)} %get-tuple-element.23), channel_id=1, source_target_pairs={{0,1},{1,2},{2,3},{3,4},{4,5},{5,6},{6,7},{7,8},{8,9},{9,10},{10,1... | collective-permute-start | bytes 5308424 | tf_op jit(solution)/shard_map/ppermute | solution.py:650
  9.1 43.1 %collective-permute-start.1 = (f32[12,72,512]{2,1,0:T(8,128)}, f32[12,72,512]{2,1,0:T(8,128)S(1)}, u32[]{:S(2)}, u32[]{:S(2)}) collective-permute-start(f32[12,72,512]{2,1,0:T(8,128)} %get-tuple-element.24), channel_id=1, source_target_pairs={{1,0},{2,1},{3,2},{4,3},{5,4},{6,5},{7,6},{8,7},{9,8},{10,9},{11,1... | collective-permute-start | bytes 5308424 | tf_op jit(solution)/shard_map/ppermute | solution.py:650
  14.4 0.7 copy-start.2
  15.2 5.1 %copy-start = (f32[36,3,512]{2,1,0:T(4,128)S(1)}, f32[36,3,512]{2,1,0:T(4,128)}, u32[]{:S(2)}) copy-start(f32[36,3,512]{2,1,0:T(4,128)} %copy.19.courant) | copy-start | bytes 663556
  15.2 5.1 %copy-start.1 = (s32[8]{0:T(128)S(1)}, s32[8]{0:T(128)}, u32[]{:S(2)}) copy-start(s32[8]{0:T(128)} %shard_map.73.scal) | copy-start | bytes 100
  15.2 37.0 %slice-start = ((s8[5308416]{0:T(1024)(128)(4,1)}), s8[4194304]{0:T(1024)(128)(4,1)S(1)}, s32[]{:S(2)}) async-start(s8[5308416]{0:T(1024)(128)(4,1)} %bitcast.3), calls=%async_computation | async-start | bytes 8388608
  20.3 32.0 %slice-start.1 = ((s8[5308416]{0:T(1024)(128)(4,1)}), s8[1114112]{0:T(1024)(128)(4,1)S(1)}, s32[]{:S(2)}) async-start(s8[5308416]{0:T(1024)(128)(4,1)} %bitcast.3), calls=%async_computation.1 | async-start | bytes 2228224
  56.1 7.7 %collective-permute-start.2 = (f32[18,72,128]{2,1,0:T(8,128)S(1)}, f32[18,72,128]{2,1,0:T(8,128)S(1)}, u32[]{:S(2)}, u32[]{:S(2)}) collective-permute-start(f32[18,72,128]{2,1,0:T(8,128)S(1)} %get-tuple-element.34), channel_id=1, source_target_pairs={{0,1},{1,2},{2,3},{3,4},{4,5},{5,6},{6,7},{7,8},{8,9},{9,10},{10,1... | collective-permute-start | bytes 1990664 | tf_op jit(solution)/shard_map/ppermute | solution.py:650
  56.2 14.4 %collective-permute-start.3 = (f32[18,72,128]{2,1,0:T(8,128)S(1)}, f32[18,72,128]{2,1,0:T(8,128)S(1)}, u32[]{:S(2)}, u32[]{:S(2)}) collective-permute-start(f32[18,72,128]{2,1,0:T(8,128)S(1)} %get-tuple-element.35), channel_id=1, source_target_pairs={{1,0},{2,1},{3,2},{4,3},{5,4},{6,5},{7,6},{8,7},{9,8},{10,9},{11,1... | collective-permute-start | bytes 1990664 | tf_op jit(solution)/shard_map/ppermute | solution.py:650
  99.7 31.7 %collective-permute-start.4 = (f32[12,66,512]{2,1,0:T(8,128)S(1)}, f32[12,66,512]{2,1,0:T(8,128)S(1)}, u32[]{:S(2)}, u32[]{:S(2)}) collective-permute-start(f32[12,66,512]{2,1,0:T(8,128)S(1)} %get-tuple-element.36), channel_id=1, source_target_pairs={{0,1},{1,2},{2,3},{3,4},{4,5},{5,6},{6,7},{7,8},{8,9},{9,10},{10,1... | collective-permute-start | bytes 4866056 | tf_op jit(solution)/shard_map/ppermute | solution.py:650
  111.9 28.1 %collective-permute-start.5 = (f32[12,66,512]{2,1,0:T(8,128)S(1)}, f32[12,66,512]{2,1,0:T(8,128)S(1)}, u32[]{:S(2)}, u32[]{:S(2)}) collective-permute-start(f32[12,66,512]{2,1,0:T(8,128)S(1)} %get-tuple-element.37), channel_id=1, source_target_pairs={{1,0},{2,1},{3,2},{4,3},{5,4},{6,5},{7,6},{8,7},{9,8},{10,9},{11,1... | collective-permute-start | bytes 4866056 | tf_op jit(solution)/shard_map/ppermute | solution.py:650

commit v5 on v4

--- a/solution.py
+++ b/solution.py
@@ -62,7 +62,7 @@
 
 
 def permuted(x, source):
-    return view(jnp.take_along_axis(flat(x), source, axis=1))
+    return view(jnp.take_along_axis(flat(x), source, axis=1, mode="promise_in_bounds"))
 
 
 def wide_lanes():
@@ -335,7 +335,7 @@
 
 def upper_kernel(moved, scal, table, spectra, courant, sym, *rest):
     low, high = rest[:2] if moved else (None, None)
-    to_q1, to_c, to_face, to_out, scal_out, low_q1, low_c, face, out, q0, cs, q1, fy, fz, q2, sems = rest[6 if moved else 0 :]
+    low_q1, low_c, face, out, scal_out, q0, cs, q1, fy, fz, q2 = rest[6 if moved else 0 :]
     for k in range(8):
         scal_out[k] = scal[k]
     here0, here = scal[HERE0], scal[HERE1] - scal[HERE0]
@@ -344,15 +344,10 @@
     def block_at(i):
         return i + jnp.where(i >= here0, here, 0) if moved else i + here0
 
-    def copy(k, l):
-        source, target = ((low_q1, to_q1), (low_c, to_c), (face, to_face), (out, to_out))[k]
-        return pltpu.make_async_copy(source.at[l], target.at[l], sems.at[k, l])
-
     def gather(i, _):
         l = block_at(i)
         fetch(scal[MID0] + l, scal, spectra, courant, low, high, q0, cs, l)
         low_c[l] = cs[l, :, 0:HALF]
-        copy(1, l).start()
         return 0
 
     lax.fori_loop(0, count, gather, 0)
@@ -371,8 +366,6 @@
         other = swap(new)
         face[l, 0:PACKED] = flat(jnp.where(upper(), limited(new, cx_prev, other), other))
         face[l, PACKED : 2 * PACKED] = flat(cx_prev * q_prev)
-        copy(0, l).start()
-        copy(2, l).start()
         return 0
 
     lax.fori_loop(0, count, first, 0)
@@ -396,17 +389,9 @@
         l = block_at(i)
         out[l] = coalesce(q2[l], sym)[0:BINS]
         second(block_at(jnp.minimum(i + 1, count - 1)))
-        copy(3, l).start()
         return 0
 
     lax.fori_loop(0, count, third, 0)
-
-    def drain(i, _):
-        for k in range(4):
-            copy(k, block_at(i)).wait()
-        return 0
-
-    lax.fori_loop(0, count, drain, 0)
 
 
 def upper_half(scal, table, spectra, courant, sym, *moved):
@@ -415,60 +400,92 @@
     shapes = [held, (capacity, 24, HALF), (capacity, 2 * PACKED, LANES), (capacity, BINS, HALF)]
     return pl.pallas_call(
         functools.partial(upper_kernel, bool(moved)),
-        in_specs=[SMEM, SMEM] + [VMEM] * 3 + ([VMEM] * 2 + [ANY] * 4 if moved else []),
-        out_specs=[ANY] * 4 + [SMEM],
+        in_specs=[SMEM, SMEM] + [VMEM] * 3 + ([VMEM] * 6 if moved else []),
+        out_specs=[VMEM] * 4 + [SMEM],
         out_shape=[jax.ShapeDtypeStruct(shape, F32) for shape in shapes] + [jax.ShapeDtypeStruct((8,), jnp.int32)],
-        scratch_shapes=[pltpu.VMEM(shape, F32) for shape in shapes]
-        + [pltpu.VMEM((capacity, PACKED, CELLS), F32), pltpu.VMEM((capacity, 24, CELLS), F32)]
-        + [pltpu.VMEM(held, F32)] * 4
-        + [pltpu.SemaphoreType.DMA((4, capacity))],
+        scratch_shapes=[pltpu.VMEM((capacity, PACKED, CELLS), F32), pltpu.VMEM((capacity, 24, CELLS), F32)]
+        + [pltpu.VMEM(held, F32)] * 4,
         input_output_aliases={7: 0, 8: 1, 9: 2, 10: 3} if moved else {},
-        compiler_params=params(40),
+        compiler_params=params(32),
         cost_estimate=pl.CostEstimate(flops=4 * 10**9, bytes_accessed=20 * 10**6, transcendentals=0),
     )(scal, table, spectra, courant, sym, *moved)
 
 
-def lower_kernel(scal, table, from_q1, from_c, from_face, from_out, below, above, sym, result, up, down, q1, cs, face, own, fy, fz, fx, q2, blank, sems, out_sems, blank_sems):
+def lower_kernel(scal, table, q1_in, cs, face, high_cells, below, above, sym, result, up, down, q1, low_cells, fy, fz, fx, q2, blank, sems, blank_sems):
     count = scal[MID1] - scal[MID0]
-    slots = scal[NEW1] - scal[NEW0]
-
-    def copy(k, l):
-        source, target = ((from_q1, q1), (from_c, cs), (from_face, face))[k]
-        return pltpu.make_async_copy(source.at[l], target.at[l], sems.at[k, l])
-
-    def copy_out(l):
-        return pltpu.make_async_copy(from_out.at[l], own.at[l, :, HALF:CELLS], sems.at[3, l])
-
-    def begin(l, _):
-        for k in range(3):
-            copy(k, l).start()
-        copy_out(l).start()
-        return 0
-
-    lax.fori_loop(0, count, begin, 0)
-
-    def clear(s):
-        return pltpu.make_async_copy(blank, result.at[s], blank_sems.at[s])
-
+    runs = lax.div(count, RUN)
+    shift, slots = scal[MID0] - scal[NEW0], scal[NEW1] - scal[NEW0]
+
+    def leave(half, act):
+        source = (low_cells, high_cells)[half]
+        cells = pl.ds(half * HALF, HALF)
+
+        def body(r, _):
+            first = r * RUN
+            block = source.at[pl.ds(first, RUN)]
+
+            @pl.when(r == 0)
+            def _():
+                act(pltpu.make_async_copy(block, down.at[:, :, cells], sems.at[half, 0]))
+
+            @pl.when(r == runs - 1)
+            def _():
+                act(pltpu.make_async_copy(block, up.at[:, :, cells], sems.at[half, 1]))
+
+            slot = first + shift
+            fits = (slot >= 0) & (slot + RUN <= slots)
+
+            @pl.when(fits)
+            def _():
+                act(pltpu.make_async_copy(block, result.at[pl.ds(slot, RUN), :, cells], sems.at[half, 2 + first]))
+
+            def one(l, _):
+                @pl.when((l + shift >= 0) & (l + shift < slots))
+                def _():
+                    act(pltpu.make_async_copy(source.at[l], result.at[l + shift, :, cells], sems.at[half, 2 + l]))
+
+                return 0
+
+            @pl.when(jnp.logical_not(fits))
+            def _():
+                lax.fori_loop(first, first + RUN, one, 0)
+
+            return 0
+
+        return body
+
+    def start(copy):
+        copy.start()
+
+    def wait(copy):
+        copy.wait()
+
+    def clear(act):
+        many = blank.shape[0]
+        dead = result.shape[0] - slots
+        whole = lax.div(dead, many)
+
+        def chunk(k, _):
+            at = slots + k * many
+            act(pltpu.make_async_copy(blank, result.at[pl.ds(at, many)], blank_sems.at[k]))
+            return 0
+
+        lax.fori_loop(0, whole, chunk, 0)
+
+        def one(s, _):
+            act(pltpu.make_async_copy(blank.at[0], result.at[s], blank_sems.at[s]))
+            return 0
+
+        lax.fori_loop(slots + whole * many, result.shape[0], one, 0)
+
+    lax.fori_loop(0, runs, leave(1, start), 0)
     blank[...] = jnp.zeros(blank.shape, F32)
-
-    def clear_start(s, _):
-        clear(s).start()
-        return 0
-
-    lax.fori_loop(slots, result.shape[0], clear_start, 0)
-
-    def arrive(l, _):
-        for k in range(3):
-            copy(k, l).wait()
-        copy_out(l).wait()
-        return 0
-
-    lax.fori_loop(0, count, arrive, 0)
+    clear(start)
 
     def fix(l, _):
         position = lax.rem(l, RUN)
         ux, _, _ = neighbours(table, l)
+        q1[l] = q1_in[l]
 
         def add_flux(flux):
             q1[l, :, span(0)] += flat(jnp.where(upper(), 0.0, flux))
@@ -509,43 +526,19 @@
     second(0)
 
     def third(l, _):
-        own[l, :, 0:HALF] = coalesce(q2[l], sym)[0:BINS]
+        low_cells[l] = coalesce(q2[l], sym)[0:BINS]
         second(jnp.minimum(l + 1, count - 1))
         return 0
-
-    def leave(act):
-        def body(l, _):
-            s = scal[MID0] + l - scal[NEW0]
-
-            @pl.when(l < RUN)
-            def _():
-                act(pltpu.make_async_copy(own.at[l], down.at[l], out_sems.at[0, l]))
-
-            @pl.when(l >= count - RUN)
-            def _():
-                act(pltpu.make_async_copy(own.at[l], up.at[l - (count - RUN)], out_sems.at[1, l]))
-
-            @pl.when((s >= 0) & (s < slots))
-            def _():
-                act(pltpu.make_async_copy(own.at[l], result.at[s], out_sems.at[2, l]))
-
-            return 0
-
-        return body
 
     def one_run(r, _):
         lax.fori_loop(r * RUN, r * RUN + RUN, third, 0)
-        lax.fori_loop(r * RUN, r * RUN + RUN, leave(lambda copy: copy.start()), 0)
-        return 0
-
-    lax.fori_loop(0, lax.div(count, RUN), one_run, 0)
-    lax.fori_loop(0, count, leave(lambda copy: copy.wait()), 0)
-
-    def clear_wait(s, _):
-        clear(s).wait()
-        return 0
-
-    lax.fori_loop(slots, result.shape[0], clear_wait, 0)
+        leave(0, start)(r, 0)
+        return 0
+
+    lax.fori_loop(0, runs, one_run, 0)
+    lax.fori_loop(0, runs, leave(0, wait), 0)
+    lax.fori_loop(0, runs, leave(1, wait), 0)
+    clear(wait)
 
 
 def lower_half(scal, table, arrays, below, above, sym):
@@ -555,24 +548,21 @@
     held = pltpu.VMEM((capacity, PACKED, HALF), F32)
     return pl.pallas_call(
         lower_kernel,
-        in_specs=[SMEM, SMEM] + [ANY] * 4 + [VMEM] * 3,
+        in_specs=[SMEM, SMEM] + [VMEM] * 7,
         out_specs=[ANY] * 3,
         out_shape=[whole, sent, sent],
         scratch_shapes=[
             held,
-            pltpu.VMEM((capacity, 24, HALF), F32),
-            pltpu.VMEM((capacity, 2 * PACKED, LANES), F32),
-            pltpu.VMEM((capacity, BINS, CELLS), F32),
+            pltpu.VMEM((capacity, BINS, HALF), F32),
             held,
             held,
             pltpu.VMEM((capacity, PACKED, LANES), F32),
             held,
-            pltpu.VMEM((BINS, CELLS), F32),
-            pltpu.SemaphoreType.DMA((4, capacity)),
-            pltpu.SemaphoreType.DMA((3, capacity)),
+            pltpu.VMEM((4, BINS, CELLS), F32),
+            pltpu.SemaphoreType.DMA((2, capacity + 2)),
             pltpu.SemaphoreType.DMA((capacity,)),
         ],
-        compiler_params=params(32),
+        compiler_params=params(30),
         cost_estimate=pl.CostEstimate(flops=8 * 10**9, bytes_accessed=20 * 10**6, transcendentals=0),
     )(scal, table, *arrays, below, above, sym)
 
@@ -627,7 +617,7 @@
     out[OLD0], out[OLD1], out[MID0], out[MID1], out[NEW0], out[NEW1] = old0, old1, mid0, mid1, new0, new1
     here0 = lax.div(jnp.maximum(old0 - mid0, 0) + RUN - 1, RUN) * RUN
     here1 = lax.div(jnp.minimum(old1, mid1) - mid0, RUN) * RUN
-    out[HERE0], out[HERE1] = here0, jnp.maximum(here0, here1)
+    out[HERE0], out[HERE1] = here0, jnp.clip(here1, here0, here0 + RUN)
 
 
 def bounds(device, old_count, new_count):

time: 141 us -> 110 us (0.78); the launches traced: 142 us -> 109 us
  Pallas kernels: 81.6 us -> 58.1 us
  starting transfers between devices: 19.8 us -> 13.4 us
  waiting for transfers between devices: 35.6 us -> 33.3 us
    pallas_call x2, Pallas kernels: 36.3 us -> 23.1 us  [upper_half(): pl.pallas_call(functools.partial(upper_kernel, bool(moved)), in_specs=[SM...]
    pallas_call x1, Pallas kernels: 29.1 us -> 18 us  [lower_half(): pl.pallas_call(lower_kernel, in_specs=[SMEM, SMEM] + [VMEM] * 7, out_spec...]
    ppermute x6, starting transfers between devices: 19.8 us -> 13.4 us  [move(): return lax.ppermute(block, 'blocks', route)]
    ppermute x6, waiting for transfers between devices: 35.6 us -> 33.3 us  [move(): return lax.ppermute(block, 'blocks', route)]
  transfers between devices with their start and end apart: 6 -> 6, of which waited for: 4 -> 4; matrix products, arithmetic and copies ran while one was open for 1% -> 2% of each run, Pallas kernels for 30% -> 27%
where the time goes in v5:
time: 110 us; the launch traced here: 109 us
  Pallas kernels  58.1 us (53%)
  waiting for transfers between devices  33.3 us (30%)
  starting transfers between devices  13.4 us (12%)
  local copies, waits for them, and re-layouts  4.21 us (4%)
    ppermute x6, waiting for transfers between devices, move(): return lax.ppermute(block, 'blocks', route)  33.3 us
    pallas_call x2, Pallas kernels, upper_half(): pl.pallas_call(functools.partial(upper_kernel, bool(moved)), in_specs=[SM...  23.1 us
    pallas_call x1, Pallas kernels, lower_half(): pl.pallas_call(lower_kernel, in_specs=[SMEM, SMEM] + [VMEM] * 7, out_spec...  18 us
    ppermute x6, starting transfers between devices, move(): return lax.ppermute(block, 'blocks', route)  13.4 us
    pallas_call x1, Pallas kernels, symmetric_kernel(): pl.pallas_call(symmetric_kernel_body, grid=(TERMS // 256,), in_specs=[pl....  5.07 us
    pallas_call x1, Pallas kernels, faces(): pl.pallas_call(face_kernel, grid=(1,), in_specs=[SMEM, SMEM, half(capacit...  4.76 us
    pallas_call x1, Pallas kernels, pack(): pl.pallas_call(pack_kernel, in_specs=[SMEM, SMEM, ANY, ANY], out_specs=[A...  4.18 us
  transfers between devices with their start and end apart: 6, of which 4 were waited for; matrix products, arithmetic and copies ran while one was open for 2% of the time, Pallas kernels for 27%

profile of v5, /device:TPU:111, one launch (start us, length us, event | category | flops | bytes accessed | tf_op | source)
XLA Modules:
  0.0 109.2 jit_solution(11646057920647617615)
XLA Ops:
  0.0 1.9 %copy.19.courant = f32[36,3,512]{2,1,0:T(4,128)} copy(f32[36,3,512]{2,0,1:T(8,128)} %param.8) | data formatting | bytes 442368 | tf_op args[1]
  1.9 4.2 %shard_map.76 = (f32[12,72,512]{2,1,0:T(8,128)}, f32[12,72,512]{2,1,0:T(8,128)}) custom-call(s32[128]{0:T(128)} %old_count.1, s32[1]{0:T(128)} %bitcast.device, f32[36,66,512]{2,1,0:T(8,128)} %spectra.7, f32[36,3,512]{2,1,0:T(4,128)} %copy.19.courant), custom_call_target="tpu_custom_call" | custom-call | tf_op jit(solution)/shard_map/pallas_call | solution.py:171
  6.1 2.3 %collective-permute-start = (f32[12,72,512]{2,1,0:T(8,128)}, f32[12,72,512]{2,1,0:T(8,128)S(1)}, u32[]{:S(2)}, u32[]{:S(2)}) collective-permute-start(f32[12,72,512]{2,1,0:T(8,128)} %get-tuple-element.23), channel_id=1, source_target_pairs={{0,1},{1,2},{2,3},{3,4},{4,5},{5,6},{6,7},{7,8},{8,9},{9,10},{10,1... | collective-permute-start | bytes 5308424 | tf_op jit(solution)/shard_map/ppermute | solution.py:640
  8.4 3.1 %collective-permute-start.1 = (f32[12,72,512]{2,1,0:T(8,128)}, f32[12,72,512]{2,1,0:T(8,128)}, u32[]{:S(2)}, u32[]{:S(2)}) collective-permute-start(f32[12,72,512]{2,1,0:T(8,128)} %get-tuple-element.24), channel_id=1, source_target_pairs={{1,0},{2,1},{3,2},{4,3},{5,4},{6,5},{7,6},{8,7},{9,8},{10,9},{11,1... | collective-permute-start | bytes 5308424 | tf_op jit(solution)/shard_map/ppermute | solution.py:640
  11.6 0.8 slice.3
  12.3 0.7 copy.18
  13.0 0.8 reshape.15.table
  13.8 1.3 %shard_map.73.scal = s32[8]{0:T(128)} custom-call(s32[1]{0:T(128)} %bitcast.device, s32[1,128]{1,0:T(1,128)} %bitcast.5, s32[1,128]{1,0:T(1,128)} %bitcast.6), custom_call_target="tpu_custom_call" | custom-call | tf_op jit(solution)/shard_map/pallas_call | solution.py:624
  15.1 0.0 slice-start.1
  15.1 0.1 pad.4.kernel
  15.2 5.1 %shard_map.74.sym = bf16[80,2304]{1,0:T(8,128)(2,1)S(1)} custom-call(s32[2,2304]{1,0:T(2,128)S(1)} %copy-done.2, bf16[80,4608]{1,0:T(8,128)(2,1)S(1)} %pad.4.kernel), custom_call_target="tpu_custom_call" | custom-call | flops 2000000000 | bytes 1000000 | tf_op jit(solution)/shard_map/pallas_call | solution.py:284
  20.4 11.0 %shard_map.75 = (f32[36,72,256]{2,1,0:T(8,128)S(1)}, f32[36,24,256]{2,1,0:T(8,128)S(1)}, f32[36,144,128]{2,1,0:T(8,128)S(1)}, f32[36,66,256]{2,1,0:T(8,128)S(1)}, s32[8]{0:T(128)S(1)}) custom-call(s32[8]{0:T(128)S(1)} %copy-done.1, s32[36]{0:T(128)S(1)} %reshape.15.table, f32[36,66,512]{2,1,0:T(8,128)S(1)} %bitcast.4, f32[36,3,512]{2,1,0:T(4,128)S(1)} %copy-done, ...), custom_call_target="tpu_custom_call" | custom-call | flops 4000000000 | bytes 20000000 | tf_op jit(solution)/shard_map/pallas_call | solution.py:401
  31.4 5.5 %collective-permute-done.1.rest_1_.high = f32[12,72,512]{2,1,0:T(8,128)} collective-permute-done((f32[12,72,512]{2,1,0:T(8,128)}, f32[12,72,512]{2,1,0:T(8,128)}, u32[]{:S(2)}, u32[]{:S(2)}) %collective-permute-start.1) | collective-permute-done | bytes 1769504 | tf_op jit(solution)/shard_map/ppermute | solution.py:640
  36.8 4.8 %shard_map.78 = (f32[18,72,128]{2,1,0:T(8,128)S(1)}, f32[18,72,128]{2,1,0:T(8,128)S(1)}) custom-call(s32[8]{0:T(128)S(1)} %get-tuple-element.22.scal, s32[36]{0:T(128)S(1)} %reshape.15.table, f32[36,66,512]{2,1,0:T(8,128)S(1)} %bitcast.4, f32[36,3,512]{2,1,0:T(4,128)S(1)} %copy-done, f32[12,72,512]{2,1,0:T(8,128)S(1)} %collective-permute-done.rest_0_.low, ...), custom_call_target="tpu_custom_call" | custom-call | tf_op jit(solution)/shard_map/pallas_call | solution.py:224
  41.6 0.1 collective-permute-start.2
  41.7 0.5 collective-permute-start.3
  42.2 12.2 %shard_map.77 = (f32[36,72,256]{2,1,0:T(8,128)S(1)}, f32[36,24,256]{2,1,0:T(8,128)S(1)}, f32[36,144,128]{2,1,0:T(8,128)S(1)}, f32[36,66,256]{2,1,0:T(8,128)S(1)}, s32[8]{0:T(128)S(1)}) custom-call(s32[8]{0:T(128)S(1)} %get-tuple-element.22.scal, s32[36]{0:T(128)S(1)} %reshape.15.table, ...), custom_call_target="tpu_custom_call", output_to_operand_aliasing={{0}: (7, {}), {1}: (8, {}), {2}: (9, {}), {3}: (10, {})} | custom-call | flops 4000000000 | bytes 20000000 | tf_op jit(solution)/shard_map/pallas_call | solution.py:401
  54.3 1.7 %collective-permute-done.3.above = f32[18,72,128]{2,1,0:T(8,128)S(1)} collective-permute-done((f32[18,72,128]{2,1,0:T(8,128)S(1)}, f32[18,72,128]{2,1,0:T(8,128)S(1)}, u32[]{:S(2)}, u32[]{:S(2)}) %collective-permute-start.3) | collective-permute-done | bytes 663584 | tf_op jit(solution)/shard_map/ppermute | solution.py:640
  56.1 18.0 %shard_map.79 = (f32[36,66,512]{2,1,0:T(8,128)}, f32[12,66,512]{2,1,0:T(8,128)S(1)}, f32[12,66,512]{2,1,0:T(8,128)S(1)}) custom-call(s32[8]{0:T(128)S(1)} %get-tuple-element.29.scal, s32[36]{0:T(128)S(1)} %reshape.15.table, f32[36,72,256]{2,1,0:T(8,128)S(1)} %get-tuple-element.30.q1_in, f32[36,24,256]{2,1,0:T(8,128)S(1)} %get-tuple-element.31.cs, ...), custom_call_target="tpu_custom_call" | custom-call | flops 8000000000 | bytes 20000000 | tf_op jit(solution)/shard_map/pallas_call | solution.py:549
  74.0 5.5 %collective-permute-start.4 = (f32[12,66,512]{2,1,0:T(8,128)S(1)}, f32[12,66,512]{2,1,0:T(8,128)S(1)}, u32[]{:S(2)}, u32[]{:S(2)}) collective-permute-start(f32[12,66,512]{2,1,0:T(8,128)S(1)} %get-tuple-element.36), channel_id=1, source_target_pairs={{0,1},{1,2},{2,3},{3,4},{4,5},{5,6},{6,7},{7,8},{8,9},{9,10},{10,1... | collective-permute-start | bytes 4866056 | tf_op jit(solution)/shard_map/ppermute | solution.py:640
  79.5 1.9 %collective-permute-start.5 = (f32[12,66,512]{2,1,0:T(8,128)S(1)}, f32[12,66,512]{2,1,0:T(8,128)S(1)}, u32[]{:S(2)}, u32[]{:S(2)}) collective-permute-start(f32[12,66,512]{2,1,0:T(8,128)S(1)} %get-tuple-element.37), channel_id=1, source_target_pairs={{1,0},{2,1},{3,2},{4,3},{5,4},{6,5},{7,6},{8,7},{9,8},{10,9},{11,1... | collective-permute-start | bytes 4866056 | tf_op jit(solution)/shard_map/ppermute | solution.py:640
  81.5 17.5 %collective-permute-done.4.low = f32[12,66,512]{2,1,0:T(8,128)S(1)} collective-permute-done((f32[12,66,512]{2,1,0:T(8,128)S(1)}, f32[12,66,512]{2,1,0:T(8,128)S(1)}, u32[]{:S(2)}, u32[]{:S(2)}) %collective-permute-start.4) | collective-permute-done | bytes 1622048 | tf_op jit(solution)/shard_map/ppermute | solution.py:640
  99.0 8.6 %collective-permute-done.5.high = f32[12,66,512]{2,1,0:T(8,128)S(1)} collective-permute-done((f32[12,66,512]{2,1,0:T(8,128)S(1)}, f32[12,66,512]{2,1,0:T(8,128)S(1)}, u32[]{:S(2)}, u32[]{:S(2)}) %collective-permute-start.5) | collective-permute-done | bytes 1622048 | tf_op jit(solution)/shard_map/ppermute | solution.py:640
  107.6 1.7 %shard_map.80 = f32[36,66,512]{2,1,0:T(8,128)} custom-call(s32[8]{0:T(128)S(1)} %get-tuple-element.29.scal, f32[12,66,512]{2,1,0:T(8,128)S(1)} %collective-permute-done.4.low, f32[12,66,512]{2,1,0:T(8,128)S(1)} %collective-permute-done.5.high, f32[36,66,512]{2,1,0:T(8,128)} %get-tuple-element.38._), custom_call_target="tpu_custom_call", output_to_operand_aliasing={{}: (3, {})} | custom-call | tf_op jit(solution)/shard_map/pallas_call | solution.py:592
  (14 shorter events, 0.0 us)
Async XLA Ops:
  0.0 20.3 %slice-start = ((s8[5308416]{0:T(1024)(128)(4,1)}), s8[1114112]{0:T(1024)(128)(4,1)S(1)}, s32[]{:S(2)}) async-start(s8[5308416]{0:T(1024)(128)(4,1)} %bitcast.3), calls=%async_computation | async-start | bytes 2228224
  1.9 13.2 %copy-start.3 = (bf16[66,4356]{1,0:T(8,128)(2,1)S(1)}, bf16[66,4356]{1,0:T(8,128)(2,1)}, u32[]{:S(2)}) copy-start(bf16[66,4356]{1,0:T(8,128)(2,1)} %param.9) | copy-start | bytes 1724980
  1.9 13.3 %copy-start.2 = (s32[2,2304]{1,0:T(2,128)S(1)}, s32[2,2304]{1,0:T(2,128)}, u32[]{:S(2)}) copy-start(s32[2,2304]{1,0:T(2,128)} %constant.9.clone.columns) | copy-start | bytes 55300
  6.1 25.2 %collective-permute-start = (f32[12,72,512]{2,1,0:T(8,128)}, f32[12,72,512]{2,1,0:T(8,128)S(1)}, u32[]{:S(2)}, u32[]{:S(2)}) collective-permute-start(f32[12,72,512]{2,1,0:T(8,128)} %get-tuple-element.23), channel_id=1, source_target_pairs={{0,1},{1,2},{2,3},{3,4},{4,5},{5,6},{6,7},{7,8},{8,9},{9,10},{10,1... | collective-permute-start | bytes 5308424 | tf_op jit(solution)/shard_map/ppermute | solution.py:640
  8.4 28.4 %collective-permute-start.1 = (f32[12,72,512]{2,1,0:T(8,128)}, f32[12,72,512]{2,1,0:T(8,128)}, u32[]{:S(2)}, u32[]{:S(2)}) collective-permute-start(f32[12,72,512]{2,1,0:T(8,128)} %get-tuple-element.24), channel_id=1, source_target_pairs={{1,0},{2,1},{3,2},{4,3},{5,4},{6,5},{7,6},{8,7},{9,8},{10,9},{11,1... | collective-permute-start | bytes 5308424 | tf_op jit(solution)/shard_map/ppermute | solution.py:640
  15.1 5.2 %slice-start.1 = ((s8[5308416]{0:T(1024)(128)(4,1)}), s8[4194304]{0:T(1024)(128)(4,1)S(1)}, s32[]{:S(2)}) async-start(s8[5308416]{0:T(1024)(128)(4,1)} %bitcast.3), calls=%async_computation.1 | async-start | bytes 8388608
  15.2 5.1 %copy-start = (f32[36,3,512]{2,1,0:T(4,128)S(1)}, f32[36,3,512]{2,1,0:T(4,128)}, u32[]{:S(2)}) copy-start(f32[36,3,512]{2,1,0:T(4,128)} %copy.19.courant) | copy-start | bytes 663556
  15.2 5.1 %copy-start.1 = (s32[8]{0:T(128)S(1)}, s32[8]{0:T(128)}, u32[]{:S(2)}) copy-start(s32[8]{0:T(128)} %shard_map.73.scal) | copy-start | bytes 100
  41.6 12.7 %collective-permute-start.2 = (f32[18,72,128]{2,1,0:T(8,128)S(1)}, f32[18,72,128]{2,1,0:T(8,128)S(1)}, u32[]{:S(2)}, u32[]{:S(2)}) collective-permute-start(f32[18,72,128]{2,1,0:T(8,128)S(1)} %get-tuple-element.34), channel_id=1, source_target_pairs={{0,1},{1,2},{2,3},{3,4},{4,5},{5,6},{6,7},{7,8},{8,9},{9,10},{10,1... | collective-permute-start | bytes 1990664 | tf_op jit(solution)/shard_map/ppermute | solution.py:640
  41.7 14.4 %collective-permute-start.3 = (f32[18,72,128]{2,1,0:T(8,128)S(1)}, f32[18,72,128]{2,1,0:T(8,128)S(1)}, u32[]{:S(2)}, u32[]{:S(2)}) collective-permute-start(f32[18,72,128]{2,1,0:T(8,128)S(1)} %get-tuple-element.35), channel_id=1, source_target_pairs={{1,0},{2,1},{3,2},{4,3},{5,4},{6,5},{7,6},{8,7},{9,8},{10,9},{11,1... | collective-permute-start | bytes 1990664 | tf_op jit(solution)/shard_map/ppermute | solution.py:640
  74.0 24.9 %collective-permute-start.4 = (f32[12,66,512]{2,1,0:T(8,128)S(1)}, f32[12,66,512]{2,1,0:T(8,128)S(1)}, u32[]{:S(2)}, u32[]{:S(2)}) collective-permute-start(f32[12,66,512]{2,1,0:T(8,128)S(1)} %get-tuple-element.36), channel_id=1, source_target_pairs={{0,1},{1,2},{2,3},{3,4},{4,5},{5,6},{6,7},{7,8},{8,9},{9,10},{10,1... | collective-permute-start | bytes 4866056 | tf_op jit(solution)/shard_map/ppermute | solution.py:640
  79.5 28.1 %collective-permute-start.5 = (f32[12,66,512]{2,1,0:T(8,128)S(1)}, f32[12,66,512]{2,1,0:T(8,128)S(1)}, u32[]{:S(2)}, u32[]{:S(2)}) collective-permute-start(f32[12,66,512]{2,1,0:T(8,128)S(1)} %get-tuple-element.37), channel_id=1, source_target_pairs={{1,0},{2,1},{3,2},{4,3},{5,4},{6,5},{7,6},{8,7},{9,8},{10,9},{11,1... | collective-permute-start | bytes 4866056 | tf_op jit(solution)/shard_map/ppermute | solution.py:640

commit v6 on v5

--- a/solution.py
+++ b/solution.py
@@ -21,7 +21,8 @@
 F32 = jnp.float32
 VMEM = pl.BlockSpec(memory_space=pltpu.VMEM)
 SMEM = pl.BlockSpec(memory_space=pltpu.SMEM)
-OLD0, OLD1, MID0, MID1, NEW0, NEW1, HERE0, HERE1 = range(8)
+OLD0, OLD1, MID0, MID1, NEW0, NEW1, HERE0, HERE1, ODD = range(9)
+SCALARS = 9
 ANY = pl.BlockSpec(memory_space=pl.ANY)
 
 
@@ -80,7 +81,7 @@
 
 
 def minmod(a, e):
-    return jnp.maximum(jnp.minimum(a, e), 0.0) + jnp.minimum(jnp.maximum(a, e), 0.0)
+    return jnp.maximum(jnp.minimum(a, e), 0.0)
 
 
 def limited(q, c, before):
@@ -90,6 +91,13 @@
 def upwind_of(table, position):
     back = table[3 * position] < RUN + position
     return back, table[3 * position + 1] - RUN, table[3 * position + 2] - RUN
+
+
+def by_side(scal, pair, other, act_low, act_high, is_low, is_high):
+    odd = scal[ODD] == 1
+    for mine, low, high in ((odd, pair, other), (jnp.logical_not(odd), other, pair)):
+        pl.when(mine & is_low)(functools.partial(act_low, low))
+        pl.when(mine & is_high)(functools.partial(act_high, high))
 
 
 def read(ref, l, v):
@@ -109,61 +117,64 @@
     return (1.0 - (cx + cy + cz)) * q + in_x + in_y + in_z
 
 
-def fetch(block, scal, spectra, courant, low, high, q_dst, c_dst, at):
+def fetch(block, scal, spectra, courant, moved, cells, q_dst, c_dst, at):
     own0, own1 = scal[OLD0], scal[OLD1]
 
-    def spread(ref, i, row):
+    def spread(d, row):
+        c_dst[at, 8 * d : 8 * d + 8] = jnp.broadcast_to(row, (8, row.shape[1]))
+
+    def owned():
+        q_dst[at, 0:BINS] = spectra[block - own0, :, cells]
         for d in range(3):
-            c_dst[at, 8 * d : 8 * d + 8] = jnp.broadcast_to(
-                ref[i, row + d : row + d + 1], (8,) + ref.shape[2:]
-            )
-
-    def owned():
-        q_dst[at, 0:BINS] = spectra[block - own0]
-        spread(courant, block - own0, 0)
-
-    if low is None:
+            spread(d, courant[d, pl.ds(block - own0, 1), cells])
+
+    if not moved:
         owned()
         return
     pl.when((block >= own0) & (block < own1))(owned)
 
-    def received(ref, i):
-        q_dst[at] = ref[i]
-        spread(ref, i, BINS)
-
-    @pl.when(block < own0)
-    def _():
-        received(low, block - own0 + RUN)
-
-    @pl.when(block >= own1)
-    def _():
-        received(high, block - own1)
-
-
-def pack_kernel(old_count, device, spectra, courant, up, down, raw, speeds, joined, in_sems, out_sems):
+    def received(i, ref):
+        q_dst[at] = ref[i, :, cells]
+        for d in range(3):
+            spread(d, ref[i, BINS + d : BINS + d + 1, cells])
+
+    from_low = functools.partial(received, block - own0 + RUN)
+    from_high = functools.partial(received, block - own1)
+    by_side(scal, *moved, from_low, from_high, block < own0, block >= own1)
+
+
+def pack_kernel(old_count, device, spectra, courant, pair, other, raw, speeds, joined, c_sem, in_sems, out_sems):
     tail = old_count[device[0]] - RUN
-    copies = []
-    for side, start in ((0, tail), (1, 0)):
-        copies.append(pltpu.make_async_copy(courant.at[pl.ds(start, RUN)], speeds.at[side], in_sems.at[side, RUN]))
-        copies[-1].start()
-    waits, sends = [], []
-    for k in range(0, RUN, 2):
-        for side, start, out in ((0, tail, up), (1, 0, down)):
-            here = pl.ds(k, 2)
-            copy = pltpu.make_async_copy(spectra.at[pl.ds(start + k, 2)], raw.at[side, here], in_sems.at[side, k])
-            copy.start()
-            waits.append((side, k, copy))
-            sends.append(pltpu.make_async_copy(joined.at[side, here], out.at[here], out_sems.at[side, k]))
-    for copy in copies:
-        copy.wait()
-    for (side, k, copy), send in zip(waits, sends):
-        copy.wait()
+    odd = lax.rem(device[0], 2) == 1
+    all_speeds = pltpu.make_async_copy(courant, speeds, c_sem)
+    all_speeds.start()
+    steps = [(k, side) for k in range(0, RUN, 2) for side in (0, 1)]
+    starts = (tail, 0)
+
+    def arrival(k, side):
+        return pltpu.make_async_copy(
+            spectra.at[pl.ds(starts[side] + k, 2)], raw.at[side, pl.ds(k, 2)], in_sems.at[side, k]
+        )
+
+    def leave(k, side, act):
+        def to(out):
+            act(pltpu.make_async_copy(joined.at[side, pl.ds(k, 2)], out.at[pl.ds(k, 2)], out_sems.at[side, k]))
+
+        pl.when(odd)(functools.partial(to, (other, pair)[side]))
+        pl.when(jnp.logical_not(odd))(functools.partial(to, (pair, other)[side]))
+
+    for k, side in steps:
+        arrival(k, side).start()
+    all_speeds.wait()
+    for k, side in steps:
+        arrival(k, side).wait()
         for i in (k, k + 1):
             joined[side, i, 0:BINS] = raw[side, i]
-            joined[side, i, BINS : BINS + 3] = speeds[side, i]
-        send.start()
-    for send in sends:
-        send.wait()
+            for d in range(3):
+                joined[side, i, BINS + d : BINS + d + 1] = speeds[d, pl.ds(starts[side] + i, 1)]
+        leave(k, side, lambda copy: copy.start())
+    for k, side in steps:
+        leave(k, side, lambda copy: copy.wait())
 
 
 def pack(old_count, device, spectra, courant):
@@ -175,68 +186,90 @@
         out_shape=[sent, sent],
         scratch_shapes=[
             pltpu.VMEM((2, RUN, BINS, CELLS), F32),
-            pltpu.VMEM((2, RUN, 3, CELLS), F32),
+            pltpu.VMEM(courant.shape, F32),
             pltpu.VMEM((2, RUN, PACKED, CELLS), F32),
-            pltpu.SemaphoreType.DMA((2, RUN + 1)),
+            pltpu.SemaphoreType.DMA(()),
+            pltpu.SemaphoreType.DMA((2, RUN)),
             pltpu.SemaphoreType.DMA((2, RUN)),
         ],
         compiler_params=params(56),
     )(old_count, device, spectra, courant)
 
 
-def face_kernel(scal, table, spectra, courant, low, high, up, down, q0, cs):
+def face_kernel(scal, table, spectra, courant, in_pair, in_other, early, pair, other, scal_out, q0, cs, up, down):
     count = scal[MID1] - scal[MID0]
-
-    def gather(j, _):
-        first = scal[MID0] + jnp.where(j < RUN, j, count - 2 * RUN + j)
-        fetch(first, scal, spectra, courant, low, high, q0, cs, j)
-        return 0
-
-    lax.fori_loop(0, 2 * RUN, gather, 0)
-
-    def face(j, position):
-        _, y, z = upwind_of(table, position)
-        uy, uz = y + (j - position), z + (j - position)
-        q1 = donor(q0, cs, j, 1, read(q0, j, 0), speed(cs, j, 0, 0), uy, uz)
-        other = swap(q1)
+    for k in range(SCALARS):
+        scal_out[k] = scal[k]
+
+    def face(j):
+        _, y, z = upwind_of(table, j)
+        q1 = donor(q0, cs, j, 1, read(q0, j, 0), speed(cs, j, 0, 0), y, z)
+        side = swap(q1)
         c = speed(cs, j, 0, 1)
-        return jnp.where(upper(), limited(q1, c, other), other), c * read(q0, j, 1)
-
-    for base, out in ((0, down), (RUN, up)):
-
-        def pair(i, _, base=base, out=out):
-            a0, b0 = face(base + 2 * i, 2 * i)
-            a1, b1 = face(base + 2 * i + 1, 2 * i + 1)
+        return jnp.where(upper(), limited(q1, c, side), side), c * read(q0, j, 1)
+
+    def one_run(start, out):
+        was_early = (start >= scal[HERE0]) & (start < scal[HERE1])
+
+        def put(i, a0, b0, a1, b1):
             out[2 * i] = flat(a0)
             out[2 * i + 1] = flat(a1)
             out[RUN + i] = flat(jnp.where(upper(), b1, swap(b0)))
+
+        def take(i, _):
+            at = start + 2 * i
+            parts = [view(early[l, k : k + PACKED]) for l in (at, at + 1) for k in (0, PACKED)]
+            put(i, *parts)
             return 0
 
-        lax.fori_loop(0, RUN // 2, pair, 0)
-
-
-def faces(scal, table, spectra, courant, low, high):
-    capacity = spectra.shape[0]
-
-    def half(*dims):
-        return pl.BlockSpec(dims + (HALF,), lambda i: (0, 0, 1))
-
+        def gather(j, _):
+            block = scal[MID0] + start + j
+            fetch(block, scal, spectra, courant, (in_pair, in_other), slice(HALF, CELLS), q0, cs, j)
+            return 0
+
+        def make(i, _):
+            put(i, *face(2 * i), *face(2 * i + 1))
+            return 0
+
+        @pl.when(was_early)
+        def _():
+            lax.fori_loop(0, RUN // 2, take, 0)
+
+        @pl.when(jnp.logical_not(was_early))
+        def _():
+            lax.fori_loop(0, RUN, gather, 0)
+            lax.fori_loop(0, RUN // 2, make, 0)
+
+    one_run(0, down)
+    one_run(count - RUN, up)
+    odd = scal[ODD] == 1
+
+    @pl.when(odd)
+    def _():
+        pair[...] = down[...]
+        other[...] = up[...]
+
+    @pl.when(jnp.logical_not(odd))
+    def _():
+        pair[...] = up[...]
+        other[...] = down[...]
+
+
+def faces(scal, table, spectra, courant, in_pair, in_other, early):
+    sent = jax.ShapeDtypeStruct((FACES, PACKED, LANES), F32)
     return pl.pallas_call(
         face_kernel,
-        grid=(1,),
-        in_specs=[
-            SMEM,
-            SMEM,
-            half(capacity, BINS),
-            half(capacity, 3),
-            half(RUN, PACKED),
-            half(RUN, PACKED),
+        in_specs=[SMEM, SMEM] + [VMEM] * 5,
+        out_specs=[VMEM, VMEM, SMEM],
+        out_shape=[sent, sent, jax.ShapeDtypeStruct((SCALARS,), jnp.int32)],
+        scratch_shapes=[
+            pltpu.VMEM((RUN, PACKED, HALF), F32),
+            pltpu.VMEM((RUN, 24, HALF), F32),
+            pltpu.VMEM(sent.shape, F32),
+            pltpu.VMEM(sent.shape, F32),
         ],
-        out_specs=[VMEM] * 2,
-        out_shape=[jax.ShapeDtypeStruct((FACES, PACKED, LANES), F32)] * 2,
-        scratch_shapes=[pltpu.VMEM((2 * RUN, PACKED, HALF), F32), pltpu.VMEM((2 * RUN, 24, HALF), F32)],
-        compiler_params=params(24),
-    )(scal, table, spectra, courant, low, high)
+        compiler_params=params(10),
+    )(scal, table, spectra, courant, in_pair, in_other, early)
 
 
 def pair_terms(q):
@@ -334,9 +367,8 @@
 
 
 def upper_kernel(moved, scal, table, spectra, courant, sym, *rest):
-    low, high = rest[:2] if moved else (None, None)
     low_q1, low_c, face, out, scal_out, q0, cs, q1, fy, fz, q2 = rest[6 if moved else 0 :]
-    for k in range(8):
+    for k in range(SCALARS):
         scal_out[k] = scal[k]
     here0, here = scal[HERE0], scal[HERE1] - scal[HERE0]
     count = scal[MID1] - scal[MID0] - here if moved else here
@@ -346,7 +378,7 @@
 
     def gather(i, _):
         l = block_at(i)
-        fetch(scal[MID0] + l, scal, spectra, courant, low, high, q0, cs, l)
+        fetch(scal[MID0] + l, scal, spectra, courant, rest[:2] if moved else (), slice(0, CELLS), q0, cs, l)
         low_c[l] = cs[l, :, 0:HALF]
         return 0
 
@@ -402,7 +434,7 @@
         functools.partial(upper_kernel, bool(moved)),
         in_specs=[SMEM, SMEM] + [VMEM] * 3 + ([VMEM] * 6 if moved else []),
         out_specs=[VMEM] * 4 + [SMEM],
-        out_shape=[jax.ShapeDtypeStruct(shape, F32) for shape in shapes] + [jax.ShapeDtypeStruct((8,), jnp.int32)],
+        out_shape=[jax.ShapeDtypeStruct(shape, F32) for shape in shapes] + [jax.ShapeDtypeStruct((SCALARS,), jnp.int32)],
         scratch_shapes=[pltpu.VMEM((capacity, PACKED, CELLS), F32), pltpu.VMEM((capacity, 24, CELLS), F32)]
         + [pltpu.VMEM(held, F32)] * 4,
         input_output_aliases={7: 0, 8: 1, 9: 2, 10: 3} if moved else {},
@@ -411,7 +443,7 @@
     )(scal, table, spectra, courant, sym, *moved)
 
 
-def lower_kernel(scal, table, q1_in, cs, face, high_cells, below, above, sym, result, up, down, q1, low_cells, fy, fz, fx, q2, blank, sems, blank_sems):
+def lower_kernel(scal, table, q1_in, cs, face, high_cells, in_pair, in_other, sym, result, pair, other, q1, low_cells, fy, fz, fx, q2, blank, sems, blank_sems):
     count = scal[MID1] - scal[MID0]
     runs = lax.div(count, RUN)
     shift, slots = scal[MID0] - scal[NEW0], scal[NEW1] - scal[NEW0]
@@ -424,13 +456,13 @@
             first = r * RUN
             block = source.at[pl.ds(first, RUN)]
 
-            @pl.when(r == 0)
-            def _():
-                act(pltpu.make_async_copy(block, down.at[:, :, cells], sems.at[half, 0]))
-
-            @pl.when(r == runs - 1)
-            def _():
-                act(pltpu.make_async_copy(block, up.at[:, :, cells], sems.at[half, 1]))
+            def down(ref):
+                act(pltpu.make_async_copy(block, ref.at[:, :, cells], sems.at[half, 0]))
+
+            def up(ref):
+                act(pltpu.make_async_copy(block, ref.at[:, :, cells], sems.at[half, 1]))
+
+            by_side(scal, pair, other, down, up, r == 0, r == runs - 1)
 
             slot = first + shift
             fits = (slot >= 0) & (slot + RUN <= slots)
@@ -495,13 +527,7 @@
             flux = view(side[RUN + position // 2])
             add_flux(jnp.where(lax.rem(position, 2) == 0, flux, swap(flux)))
 
-        @pl.when(ux < 0)
-        def _():
-            remote(below)
-
-        @pl.when(ux >= count)
-        def _():
-            remote(above)
+        by_side(scal, in_pair, in_other, remote, remote, ux < 0, ux >= count)
 
         @pl.when((ux >= 0) & (ux < count))
         def _():
@@ -541,7 +567,7 @@
     clear(wait)
 
 
-def lower_half(scal, table, arrays, below, above, sym):
+def lower_half(scal, table, arrays, in_pair, in_other, sym):
     capacity = arrays[0].shape[0]
     whole = jax.ShapeDtypeStruct((capacity, BINS, CELLS), F32)
     sent = jax.ShapeDtypeStruct((RUN, BINS, CELLS), F32)
@@ -564,31 +590,31 @@
         ],
         compiler_params=params(30),
         cost_estimate=pl.CostEstimate(flops=8 * 10**9, bytes_accessed=20 * 10**6, transcendentals=0),
-    )(scal, table, *arrays, below, above, sym)
-
-
-def place_moved_kernel(scal, low, high, _, out, sems):
+    )(scal, table, *arrays, in_pair, in_other, sym)
+
+
+def place_moved_kernel(scal, pair, other, _, out, sems):
     first, end = scal[NEW0], scal[NEW1]
 
     def copies(act):
         for k in range(RUN):
-            block = scal[MID0] - RUN + k
-
-            @pl.when((block >= first) & (block < end))
-            def _(k=k, block=block):
-                act(pltpu.make_async_copy(low.at[k], out.at[block - first], sems.at[0, k]))
-
-            above = scal[MID1] + k
-
-            @pl.when((above >= first) & (above < end))
-            def _(k=k, above=above):
-                act(pltpu.make_async_copy(high.at[k], out.at[above - first], sems.at[1, k]))
+            low, high = scal[MID0] - RUN + k, scal[MID1] + k
+
+            def from_low(ref, k=k, low=low):
+                act(pltpu.make_async_copy(ref.at[k], out.at[low - first], sems.at[0, k]))
+
+            def from_high(ref, k=k, high=high):
+                act(pltpu.make_async_copy(ref.at[k], out.at[high - first], sems.at[1, k]))
+
+            low_in = (low >= first) & (low < end)
+            high_in = (high >= first) & (high < end)
+            by_side(scal, pair, other, from_low, from_high, low_in, high_in)
 
     copies(lambda copy: copy.start())
     copies(lambda copy: copy.wait())
 
 
-def place_moved(scal, low, high, out):
+def place_moved(scal, pair, other, out):
     return pl.pallas_call(
         place_moved_kernel,
         in_specs=[SMEM, VMEM, VMEM, ANY],
@@ -597,7 +623,7 @@
         scratch_shapes=[pltpu.SemaphoreType.DMA((2, RUN))],
         input_output_aliases={3: 0},
         compiler_params=params(8),
-    )(scal, low, high, out)
+    )(scal, pair, other, out)
 
 
 def bounds_kernel(device, old_count, new_count, out):
@@ -617,6 +643,7 @@
     out[OLD0], out[OLD1], out[MID0], out[MID1], out[NEW0], out[NEW1] = old0, old1, mid0, mid1, new0, new1
     here0 = lax.div(jnp.maximum(old0 - mid0, 0) + RUN - 1, RUN) * RUN
     here1 = lax.div(jnp.minimum(old1, mid1) - mid0, RUN) * RUN
+    out[ODD] = lax.rem(device[0], 2)
     out[HERE0], out[HERE1] = here0, jnp.clip(here1, here0, here0 + RUN)
 
 
@@ -625,32 +652,32 @@
         bounds_kernel,
         in_specs=[SMEM, VMEM, VMEM],
         out_specs=SMEM,
-        out_shape=jax.ShapeDtypeStruct((8,), jnp.int32),
+        out_shape=jax.ShapeDtypeStruct((SCALARS,), jnp.int32),
     )(device, old_count.reshape(1, -1), new_count.reshape(1, -1))
 
 
 def on_device(devices, spectra, courant, kernel, old_count, new_count, upwind):
     device = lax.axis_index("blocks").astype(jnp.int32).reshape(1)
-    rise = [(i, i + 1) for i in range(devices - 1)]
-    fall = [(i + 1, i) for i in range(devices - 1)]
-    around = [(i, (i + 1) % devices) for i in range(devices)]
-    reverse = [(j, i) for i, j in around]
-
-    def move(block, route):
-        return lax.ppermute(block, "blocks", route)
-
-    tail, head = pack(old_count, device, spectra, courant)
-    low, high = move(tail, rise), move(head, fall)
+    pairs = [(i, i ^ 1) for i in range(devices)]
+    others = [(i, i + 1) for i in range(1, devices - 1, 2)]
+    others += [(j, i) for i, j in others]
+    ends = [(devices - 1, 0), (0, devices - 1)]
+
+    def exchange(pair, other, route):
+        from_other = lax.ppermute(other, "blocks", route)
+        return lax.ppermute(pair, "blocks", pairs), from_other
+
+    courant = jnp.swapaxes(courant, 0, 1)
+    moved = exchange(*pack(old_count, device, spectra, courant), others)
     scal = bounds(device, old_count, new_count)
     table = upwind[RUN : 2 * RUN].reshape(-1)
     sym = symmetric_kernel(kernel)
     *early, scal = upper_half(scal, table, spectra, courant, sym)
-    up, down = faces(scal, table, spectra, courant, low, high)
-    below, above = move(up, around), move(down, reverse)
-    *arrays, scal = upper_half(scal, table, spectra, courant, sym, low, high, *early)
-    result, up, down = lower_half(scal, table, arrays, below, above, sym)
-    low, high = move(up, rise), move(down, fall)
-    return place_moved(scal, low, high, result)
+    *sides, scal = faces(scal, table, spectra, courant, *moved, early[2])
+    sides = exchange(*sides, others + ends)
+    *arrays, scal = upper_half(scal, table, spectra, courant, sym, *moved, *early)
+    result, *results = lower_half(scal, table, arrays, *sides, sym)
+    return place_moved(scal, *exchange(*results, others), result)
 
 
 def solution(mesh):

time: 110 us -> 103 us (0.936)
  the two profiles are of different devices: /device:TPU:111 before, /device:TPU:8 now
where the time goes in v6:
time: 103 us; the launch traced here: 102 us
  Pallas kernels  56.6 us (55%)
  waiting for transfers between devices  23.7 us (23%)
  starting transfers between devices  19.1 us (19%)
  local copies, waits for them, and re-layouts  2.8 us (3%)
    ppermute x3, waiting for transfers between devices, exchange(): from_other = lax.ppermute(other, 'blocks', route)  23.7 us
    pallas_call x2, Pallas kernels, upper_half(): pl.pallas_call(functools.partial(upper_kernel, bool(moved)), in_specs=[SM...  22.1 us
    ppermute x3, starting transfers between devices, exchange(): from_other = lax.ppermute(other, 'blocks', route)  18.8 us
    pallas_call x1, Pallas kernels, lower_half(): pl.pallas_call(lower_kernel, in_specs=[SMEM, SMEM] + [VMEM] * 7, out_spec...  17.7 us
    pallas_call x1, Pallas kernels, symmetric_kernel(): pl.pallas_call(symmetric_kernel_body, grid=(TERMS // 256,), in_specs=[pl....  5.05 us
    pallas_call x1, Pallas kernels, pack(): pl.pallas_call(pack_kernel, in_specs=[SMEM, SMEM, ANY, ANY], out_specs=[A...  4.89 us
    pallas_call x1, Pallas kernels, faces(): pl.pallas_call(face_kernel, in_specs=[SMEM, SMEM] + [VMEM] * 5, out_specs...  3.58 us
  transfers between devices with their start and end apart: 6, of which 2 were waited for; matrix products, arithmetic and copies ran while one was open for 2% of the time, Pallas kernels for 28%

profile of v6, /device:TPU:8, one launch (start us, length us, event | category | flops | bytes accessed | tf_op | source)
XLA Modules:
  0.0 102.3 jit_solution(9006857660438780167)
XLA Ops:
  0.0 4.9 %shard_map.76 = (f32[12,72,512]{2,1,0:T(8,128)}, f32[12,72,512]{2,1,0:T(8,128)}) custom-call(s32[128]{0:T(128)} %old_count.1, s32[1]{0:T(128)} %bitcast.device, f32[36,66,512]{2,1,0:T(8,128)} %spectra.7, f32[3,36,512]{2,1,0:T(8,128)} %bitcast.4), custom_call_target="tpu_custom_call" | custom-call | tf_op jit(solution)/shard_map/pallas_call | solution.py:182
  4.9 0.1 collective-permute-start
  5.0 8.1 %collective-permute-start.1 = (f32[12,72,512]{2,1,0:T(8,128)}, f32[12,72,512]{2,1,0:T(8,128)S(1)}, u32[]{:S(2)}, u32[]{:S(2)}) collective-permute-start(f32[12,72,512]{2,1,0:T(8,128)} %get-tuple-element.25), channel_id=1, source_target_pairs={{1,2},{3,4},{5,6},{7,8},{9,10},{11,12},{13,14},{15,16},{17,18},{19... | collective-permute-start | bytes 5308424 | tf_op jit(solution)/shard_map/ppermute | solution.py:667
  13.1 0.8 slice.3
  13.8 0.1 copy.14
  13.9 0.1 reshape.15.table
  14.0 1.4 %shard_map.73.scal = s32[9]{0:T(128)} custom-call(s32[1]{0:T(128)} %bitcast.device, s32[1,128]{1,0:T(1,128)} %bitcast.8, s32[1,128]{1,0:T(1,128)} %bitcast.9), custom_call_target="tpu_custom_call" | custom-call | tf_op jit(solution)/shard_map/pallas_call | solution.py:651
  15.3 1.1 %pad.4.kernel = bf16[80,4608]{1,0:T(8,128)(2,1)S(1)} pad(bf16[66,4356]{1,0:T(8,128)(2,1)} %param.9, bf16[]{:T(256)} %constant.8.clone.1), padding=0_14x0_252 | pad | bytes 1312274 | tf_op jit(solution)/shard_map/jit(_pad)/pad | solution.py:316
  16.5 0.0 copy-start.3
  16.5 0.7 copy-done.3
  17.2 5.0 %shard_map.74.sym = bf16[80,2304]{1,0:T(8,128)(2,1)S(1)} custom-call(s32[2,2304]{1,0:T(2,128)S(1)} %copy-done.3, bf16[80,4608]{1,0:T(8,128)(2,1)S(1)} %pad.4.kernel), custom_call_target="tpu_custom_call" | custom-call | flops 2000000000 | bytes 1000000 | tf_op jit(solution)/shard_map/pallas_call | solution.py:317
  22.3 10.8 %shard_map.75 = (f32[36,72,256]{2,1,0:T(8,128)S(1)}, f32[36,24,256]{2,1,0:T(8,128)S(1)}, f32[36,144,128]{2,1,0:T(8,128)S(1)}, f32[36,66,256]{2,1,0:T(8,128)S(1)}, s32[9]{0:T(128)S(1)}) custom-call(s32[9]{0:T(128)S(1)} %copy-done.2, s32[36]{0:T(128)S(1)} %reshape.15.table, f32[36,66,512]{2,1,0:T(8,128)S(1)} %copy-done, f32[3,36,512]{2,1,0:T(8,128)S(1)} %bitcast.5, ...), custom_call_target="tpu_custom_call" | custom-call | flops 4000000000 | bytes 20000000 | tf_op jit(solution)/shard_map/pallas_call | solution.py:433
  33.1 0.0 collective-permute-done.in_pair.rest_0_
  33.1 0.4 collective-permute-done.1.in_other.rest_1_
  33.5 3.6 %shard_map.77 = (f32[18,72,128]{2,1,0:T(8,128)S(1)}, f32[18,72,128]{2,1,0:T(8,128)S(1)}, s32[9]{0:T(128)S(1)}) custom-call(s32[9]{0:T(128)S(1)} %get-tuple-element.23.scal, s32[36]{0:T(128)S(1)} %reshape.15.table, f32[36,66,512]{2,1,0:T(8,128)S(1)} %copy-done, f32[3,36,512]{2,1,0:T(8,128)S(1)} %bitcast.6, ...), custom_call_target="tpu_custom_call" | custom-call | tf_op jit(solution)/shard_map/pallas_call | solution.py:260
  37.0 0.1 collective-permute-start.2
  37.1 6.0 %collective-permute-start.3 = (f32[18,72,128]{2,1,0:T(8,128)S(1)}, f32[18,72,128]{2,1,0:T(8,128)S(1)}, u32[]{:S(2)}, u32[]{:S(2)}) collective-permute-start(f32[18,72,128]{2,1,0:T(8,128)S(1)} %get-tuple-element.37), channel_id=1, source_target_pairs={{1,2},{3,4},{5,6},{7,8},{9,10},{11,12},{13,14},{15,16},{17,18},{19... | collective-permute-start | bytes 1990664 | tf_op jit(solution)/shard_map/ppermute | solution.py:667
  43.2 11.3 %shard_map.78 = (f32[36,72,256]{2,1,0:T(8,128)S(1)}, f32[36,24,256]{2,1,0:T(8,128)S(1)}, f32[36,144,128]{2,1,0:T(8,128)S(1)}, f32[36,66,256]{2,1,0:T(8,128)S(1)}, s32[9]{0:T(128)S(1)}) custom-call(s32[9]{0:T(128)S(1)} %get-tuple-element.27.scal, s32[36]{0:T(128)S(1)} %reshape.15.table, ...), custom_call_target="tpu_custom_call", output_to_operand_aliasing={{0}: (7, {}), {1}: (8, {}), {2}: (9, {}), {3}: (10, {})} | custom-call | flops 4000000000 | bytes 20000000 | tf_op jit(solution)/shard_map/pallas_call | solution.py:433
  54.5 0.0 collective-permute-done.2.in_pair
  54.5 17.7 %shard_map.79 = (f32[36,66,512]{2,1,0:T(8,128)}, f32[12,66,512]{2,1,0:T(8,128)S(1)}, f32[12,66,512]{2,1,0:T(8,128)S(1)}) custom-call(s32[9]{0:T(128)S(1)} %get-tuple-element.31.scal, s32[36]{0:T(128)S(1)} %reshape.15.table, f32[36,72,256]{2,1,0:T(8,128)S(1)} %get-tuple-element.32.q1_in, f32[36,24,256]{2,1,0:T(8,128)S(1)} %get-tuple-element.33.cs, ...), custom_call_target="tpu_custom_call" | custom-call | flops 8000000000 | bytes 20000000 | tf_op jit(solution)/shard_map/pallas_call | solution.py:575
  72.2 0.1 collective-permute-start.4
  72.3 4.7 %collective-permute-start.5 = (f32[12,66,512]{2,1,0:T(8,128)S(1)}, f32[12,66,512]{2,1,0:T(8,128)S(1)}, u32[]{:S(2)}, u32[]{:S(2)}) collective-permute-start(f32[12,66,512]{2,1,0:T(8,128)S(1)} %get-tuple-element.39), channel_id=1, source_target_pairs={{1,2},{3,4},{5,6},{7,8},{9,10},{11,12},{13,14},{15,16},{17,18},{19... | collective-permute-start | bytes 4866056 | tf_op jit(solution)/shard_map/ppermute | solution.py:667
  77.1 23.3 %collective-permute-done.5.other = f32[12,66,512]{2,1,0:T(8,128)S(1)} collective-permute-done((f32[12,66,512]{2,1,0:T(8,128)S(1)}, f32[12,66,512]{2,1,0:T(8,128)S(1)}, u32[]{:S(2)}, u32[]{:S(2)}) %collective-permute-start.5) | collective-permute-done | bytes 1622048 | tf_op jit(solution)/shard_map/ppermute | solution.py:667
  100.4 1.9 %shard_map.80 = f32[36,66,512]{2,1,0:T(8,128)} custom-call(s32[9]{0:T(128)S(1)} %get-tuple-element.31.scal, f32[12,66,512]{2,1,0:T(8,128)S(1)} %collective-permute-done.4.pair, f32[12,66,512]{2,1,0:T(8,128)S(1)} %collective-permute-done.5.other, f32[36,66,512]{2,1,0:T(8,128)} %get-tuple-element.40._), custom_call_target="tpu_custom_call", output_to_operand_aliasing={{}: (3, {})} | custom-call | tf_op jit(solution)/shard_map/pallas_call | solution.py:618
  (8 shorter events, 0.0 us)
Async XLA Ops:
  4.9 28.2 %collective-permute-start = (f32[12,72,512]{2,1,0:T(8,128)}, f32[12,72,512]{2,1,0:T(8,128)S(1)}, u32[]{:S(2)}, u32[]{:S(2)}) collective-permute-start(f32[12,72,512]{2,1,0:T(8,128)} %get-tuple-element.24), channel_id=1, source_target_pairs={{0,1},{1,0},{2,3},{3,2},{4,5},{5,4},{6,7},{7,6},{8,9},{9,8},{10,11... | collective-permute-start | bytes 5308424 | tf_op jit(solution)/shard_map/ppermute | solution.py:668
  5.0 28.5 %collective-permute-start.1 = (f32[12,72,512]{2,1,0:T(8,128)}, f32[12,72,512]{2,1,0:T(8,128)S(1)}, u32[]{:S(2)}, u32[]{:S(2)}) collective-permute-start(f32[12,72,512]{2,1,0:T(8,128)} %get-tuple-element.25), channel_id=1, source_target_pairs={{1,2},{3,4},{5,6},{7,8},{9,10},{11,12},{13,14},{15,16},{17,18},{19... | collective-permute-start | bytes 5308424 | tf_op jit(solution)/shard_map/ppermute | solution.py:667
  16.5 0.7 copy-start.3
  17.2 5.1 %copy-start = (f32[36,66,512]{2,1,0:T(8,128)S(1)}, f32[36,66,512]{2,1,0:T(8,128)}, u32[]{:S(2)}) copy-start(f32[36,66,512]{2,1,0:T(8,128)} %spectra.7) | copy-start | bytes 14598148
  17.2 5.1 %copy-start.1 = (f32[36,3,512]{2,0,1:T(8,128)S(1)}, f32[36,3,512]{2,0,1:T(8,128)}, u32[]{:S(2)}) copy-start(f32[36,3,512]{2,0,1:T(8,128)} %param.8) | copy-start | bytes 663556
  17.2 5.1 %copy-start.2 = (s32[9]{0:T(128)S(1)}, s32[9]{0:T(128)}, u32[]{:S(2)}) copy-start(s32[9]{0:T(128)} %shard_map.73.scal) | copy-start | bytes 112
  37.0 17.4 %collective-permute-start.2 = (f32[18,72,128]{2,1,0:T(8,128)S(1)}, f32[18,72,128]{2,1,0:T(8,128)S(1)}, u32[]{:S(2)}, u32[]{:S(2)}) collective-permute-start(f32[18,72,128]{2,1,0:T(8,128)S(1)} %get-tuple-element.36), channel_id=1, source_target_pairs={{0,1},{1,0},{2,3},{3,2},{4,5},{5,4},{6,7},{7,6},{8,9},{9,8},{10,11... | collective-permute-start | bytes 1990664 | tf_op jit(solution)/shard_map/ppermute | solution.py:668
  37.1 17.4 %collective-permute-start.3 = (f32[18,72,128]{2,1,0:T(8,128)S(1)}, f32[18,72,128]{2,1,0:T(8,128)S(1)}, u32[]{:S(2)}, u32[]{:S(2)}) collective-permute-start(f32[18,72,128]{2,1,0:T(8,128)S(1)} %get-tuple-element.37), channel_id=1, source_target_pairs={{1,2},{3,4},{5,6},{7,8},{9,10},{11,12},{13,14},{15,16},{17,18},{19... | collective-permute-start | bytes 1990664 | tf_op jit(solution)/shard_map/ppermute | solution.py:667
  72.2 4.8 %collective-permute-start.4 = (f32[12,66,512]{2,1,0:T(8,128)S(1)}, f32[12,66,512]{2,1,0:T(8,128)S(1)}, u32[]{:S(2)}, u32[]{:S(2)}) collective-permute-start(f32[12,66,512]{2,1,0:T(8,128)S(1)} %get-tuple-element.38), channel_id=1, source_target_pairs={{0,1},{1,0},{2,3},{3,2},{4,5},{5,4},{6,7},{7,6},{8,9},{9,8},{10,11... | collective-permute-start | bytes 4866056 | tf_op jit(solution)/shard_map/ppermute | solution.py:668
  72.3 28.1 %collective-permute-start.5 = (f32[12,66,512]{2,1,0:T(8,128)S(1)}, f32[12,66,512]{2,1,0:T(8,128)S(1)}, u32[]{:S(2)}, u32[]{:S(2)}) collective-permute-start(f32[12,66,512]{2,1,0:T(8,128)S(1)} %get-tuple-element.39), channel_id=1, source_target_pairs={{1,2},{3,4},{5,6},{7,8},{9,10},{11,12},{13,14},{15,16},{17,18},{19... | collective-permute-start | bytes 4866056 | tf_op jit(solution)/shard_map/ppermute | solution.py:667

commit v7 on v6

--- a/solution.py
+++ b/solution.py
@@ -17,6 +17,8 @@
 FULL = 64
 TERMS = 2304
 GROUPS = 9
+STENCILS = 6
+PRODUCTS = 2
 FACES = 18
 F32 = jnp.float32
 VMEM = pl.BlockSpec(memory_space=pltpu.VMEM)
@@ -218,7 +220,7 @@
 
         def take(i, _):
             at = start + 2 * i
-            parts = [view(early[l, k : k + PACKED]) for l in (at, at + 1) for k in (0, PACKED)]
+            parts = [view(early[RUN + l, k : k + PACKED]) for l in (at, at + 1) for k in (0, PACKED)]
             put(i, *parts)
             return 0
 
@@ -337,6 +339,15 @@
     return q + gained[0:PACKED]
 
 
+def several(begin, end, body, at_once):
+    def step(k, _):
+        for j in range(at_once):
+            body(begin + k * at_once + j)
+        return 0
+
+    lax.fori_loop(0, lax.div(end - begin, at_once), step, 0)
+
+
 def neighbours(table, l):
     position = lax.rem(l, RUN)
     back, y, z = upwind_of(table, position)
@@ -344,7 +355,7 @@
 
 
 def cross_flux(count, block_at, table, q1, cs, fy, fz, v0, vf):
-    def cross_body(i, _):
+    def cross_body(i):
         l = block_at(i)
         _, uy, uz = neighbours(table, l)
         for w in range(2):
@@ -353,9 +364,8 @@
             before_z = step_z(jnp.where(last_z(), read(q1, uz, v0 + w), q))
             fy[l, :, span(w)] = flat(limited(q, speed(cs, l, 1, vf + w), before_y))
             fz[l, :, span(w)] = flat(limited(q, speed(cs, l, 2, vf + w), before_z))
-        return 0
-
-    lax.fori_loop(0, count, cross_body, 0)
+
+    several(0, count, cross_body, STENCILS)
 
 
 def cross(table, l, fy, fz, w):
@@ -366,6 +376,24 @@
     return (y_in - y_own) + (z_in - z_own)
 
 
+def coalesce_all(begin, end, count, block_at, second, q2, sym, out):
+    @pl.when((begin == 0) & (end > 0))
+    def _():
+        for j in range(PRODUCTS):
+            second(block_at(j))
+
+    def step(k, _):
+        i = begin + k * PRODUCTS
+        at = [block_at(i + j) for j in range(PRODUCTS)]
+        for l in at:
+            out[l] = coalesce(q2[l], sym)[0:BINS]
+        for j in range(PRODUCTS):
+            second(block_at(jnp.minimum(i + PRODUCTS + j, count - 1)))
+        return 0
+
+    lax.fori_loop(0, lax.div(end - begin, PRODUCTS), step, 0)
+
+
 def upper_kernel(moved, scal, table, spectra, courant, sym, *rest):
     low_q1, low_c, face, out, scal_out, q0, cs, q1, fy, fz, q2 = rest[6 if moved else 0 :]
     for k in range(SCALARS):
@@ -384,7 +412,7 @@
 
     lax.fori_loop(0, count, gather, 0)
 
-    def first(i, _):
+    def first(i):
         l = block_at(i)
         _, uy, uz = neighbours(table, l)
         q_prev = cx_prev = None
@@ -396,11 +424,10 @@
             else:
                 q1[l, :, span(v - 2)] = flat(new)
         other = swap(new)
-        face[l, 0:PACKED] = flat(jnp.where(upper(), limited(new, cx_prev, other), other))
-        face[l, PACKED : 2 * PACKED] = flat(cx_prev * q_prev)
-        return 0
-
-    lax.fori_loop(0, count, first, 0)
+        face[RUN + l, 0:PACKED] = flat(jnp.where(upper(), limited(new, cx_prev, other), other))
+        face[RUN + l, PACKED : 2 * PACKED] = flat(cx_prev * q_prev)
+
+    several(0, count, first, STENCILS)
     cross_flux(count, block_at, table, q1, cs, fy, fz, 0, 2)
 
     def second(l):
@@ -413,23 +440,13 @@
             q2[l, :, span(w)] = flat(new)
             q_prev, f_prev = q, f
 
-    @pl.when(count > 0)
-    def _():
-        second(block_at(0))
-
-    def third(i, _):
-        l = block_at(i)
-        out[l] = coalesce(q2[l], sym)[0:BINS]
-        second(block_at(jnp.minimum(i + 1, count - 1)))
-        return 0
-
-    lax.fori_loop(0, count, third, 0)
+    coalesce_all(0, count, count, block_at, second, q2, sym, out)
 
 
 def upper_half(scal, table, spectra, courant, sym, *moved):
     capacity = spectra.shape[0]
     held = (capacity, PACKED, HALF)
-    shapes = [held, (capacity, 24, HALF), (capacity, 2 * PACKED, LANES), (capacity, BINS, HALF)]
+    shapes = [held, (capacity, 24, HALF), (capacity + 2 * RUN, 2 * PACKED, LANES), (capacity, BINS, HALF)]
     return pl.pallas_call(
         functools.partial(upper_kernel, bool(moved)),
         in_specs=[SMEM, SMEM] + [VMEM] * 3 + ([VMEM] * 6 if moved else []),
@@ -443,7 +460,7 @@
     )(scal, table, spectra, courant, sym, *moved)
 
 
-def lower_kernel(scal, table, q1_in, cs, face, high_cells, in_pair, in_other, sym, result, pair, other, q1, low_cells, fy, fz, fx, q2, blank, sems, blank_sems):
+def lower_kernel(scal, table, _, cs, __, high_cells, in_pair, in_other, sym, result, pair, other, q1, face, low_cells, fy, fz, q2, blank, sems, blank_sems):
     count = scal[MID1] - scal[MID0]
     runs = lax.div(count, RUN)
     shift, slots = scal[MID0] - scal[NEW0], scal[NEW1] - scal[NEW0]
@@ -514,33 +531,28 @@
     blank[...] = jnp.zeros(blank.shape, F32)
     clear(start)
 
-    def fix(l, _):
-        position = lax.rem(l, RUN)
+    def expand(base, ref):
+        for i in range(RUN // 2):
+            flux = ref[RUN + i]
+            for k in (2 * i, 2 * i + 1):
+                face[base + k, 0:PACKED] = ref[k]
+            face[base + 2 * i, PACKED : 2 * PACKED] = pltpu.roll(flux, 64, 1)
+            face[base + 2 * i + 1, PACKED : 2 * PACKED] = flux
+
+    always = count > 0
+    at_high = functools.partial(expand, count + RUN)
+    by_side(scal, in_pair, in_other, functools.partial(expand, 0), at_high, always, always)
+
+    def fix(l):
         ux, _, _ = neighbours(table, l)
-        q1[l] = q1_in[l]
-
-        def add_flux(flux):
-            q1[l, :, span(0)] += flat(jnp.where(upper(), 0.0, flux))
-
-        def remote(side):
-            fx[l] = side[position]
-            flux = view(side[RUN + position // 2])
-            add_flux(jnp.where(lax.rem(position, 2) == 0, flux, swap(flux)))
-
-        by_side(scal, in_pair, in_other, remote, remote, ux < 0, ux >= count)
-
-        @pl.when((ux >= 0) & (ux < count))
-        def _():
-            fx[l] = face[ux, 0:PACKED]
-            add_flux(swap(view(face[ux, PACKED : 2 * PACKED])))
-
-        return 0
-
-    lax.fori_loop(0, count, fix, 0)
+        flux = swap(view(face[RUN + ux, PACKED : 2 * PACKED]))
+        q1[l, :, span(0)] += flat(jnp.where(upper(), 0.0, flux))
+
+    several(0, count, fix, STENCILS)
     cross_flux(count, lambda i: i, table, q1, cs, fy, fz, 0, 0)
 
     def second(l):
-        side = view(fx[l])
+        side = view(face[RUN + neighbours(table, l)[0], 0:PACKED])
         q = read(q1, l, 0)
         f = limited(q, speed(cs, l, 0, 0), jnp.where(upper(), swap(q), side))
         q2[l, :, span(0)] = flat(q - f + swap(jnp.where(upper(), side, f)) + cross(table, l, fy, fz, 0))
@@ -549,15 +561,8 @@
         f = limited(q, speed(cs, l, 0, 1), swap(jnp.where(upper(), q_prev, q)))
         q2[l, :, span(1)] = flat(q - f + swap(jnp.where(upper(), f_prev, f)) + cross(table, l, fy, fz, 1))
 
-    second(0)
-
-    def third(l, _):
-        low_cells[l] = coalesce(q2[l], sym)[0:BINS]
-        second(jnp.minimum(l + 1, count - 1))
-        return 0
-
     def one_run(r, _):
-        lax.fori_loop(r * RUN, r * RUN + RUN, third, 0)
+        coalesce_all(r * RUN, r * RUN + RUN, count, lambda i: i, second, q2, sym, low_cells)
         leave(0, start)(r, 0)
         return 0
 
@@ -575,14 +580,13 @@
     return pl.pallas_call(
         lower_kernel,
         in_specs=[SMEM, SMEM] + [VMEM] * 7,
-        out_specs=[ANY] * 3,
-        out_shape=[whole, sent, sent],
+        out_specs=[ANY] * 3 + [VMEM] * 2,
+        out_shape=[whole, sent, sent] + [jax.ShapeDtypeStruct(x.shape, F32) for x in (arrays[0], arrays[2])],
+        input_output_aliases={2: 3, 4: 4},
         scratch_shapes=[
-            held,
             pltpu.VMEM((capacity, BINS, HALF), F32),
             held,
             held,
-            pltpu.VMEM((capacity, PACKED, LANES), F32),
             held,
             pltpu.VMEM((4, BINS, CELLS), F32),
             pltpu.SemaphoreType.DMA((2, capacity + 2)),
@@ -590,7 +594,7 @@
         ],
         compiler_params=params(30),
         cost_estimate=pl.CostEstimate(flops=8 * 10**9, bytes_accessed=20 * 10**6, transcendentals=0),
-    )(scal, table, *arrays, in_pair, in_other, sym)
+    )(scal, table, *arrays, in_pair, in_other, sym)[:3]
 
 
 def place_moved_kernel(scal, pair, other, _, out, sems):

time: 103 us -> 96.4 us (0.936)
  the two profiles are of different devices: /device:TPU:8 before, /device:TPU:111 now
where the time goes in v7:
time: 96.4 us; the launch traced here: 94.8 us
  Pallas kernels  47.8 us (50%)
  waiting for transfers between devices  38 us (39%)
  starting transfers between devices  6.1 us (6%)
  local copies, waits for them, and re-layouts  2.8 us (3%)
    ppermute x3, waiting for transfers between devices, exchange(): from_other = lax.ppermute(other, 'blocks', route)  37.3 us
    pallas_call x2, Pallas kernels, upper_half(): pl.pallas_call(functools.partial(upper_kernel, bool(moved)), in_specs=[SM...  18.4 us
    pallas_call x1, Pallas kernels, lower_half(): pl.pallas_call(lower_kernel, in_specs=[SMEM, SMEM] + [VMEM] * 7, out_spec...  13.5 us
    pallas_call x1, Pallas kernels, symmetric_kernel(): pl.pallas_call(symmetric_kernel_body, grid=(TERMS // 256,), in_specs=[pl....  5.05 us
    ppermute x3, starting transfers between devices, exchange(): from_other = lax.ppermute(other, 'blocks', route)  4.96 us
    pallas_call x1, Pallas kernels, pack(): pl.pallas_call(pack_kernel, in_specs=[SMEM, SMEM, ANY, ANY], out_specs=[A...  4.82 us
    pallas_call x1, Pallas kernels, faces(): pl.pallas_call(face_kernel, in_specs=[SMEM, SMEM] + [VMEM] * 5, out_specs...  3.58 us
  transfers between devices with their start and end apart: 6, of which 4 were waited for; matrix products, arithmetic and copies ran while one was open for 2% of the time, Pallas kernels for 26%

profile of v7, /device:TPU:111, one launch (start us, length us, event | category | flops | bytes accessed | tf_op | source)
XLA Modules:
  0.0 94.8 jit_solution(10189609073566346656)
XLA Ops:
  0.0 4.8 %shard_map.76 = (f32[12,72,512]{2,1,0:T(8,128)}, f32[12,72,512]{2,1,0:T(8,128)}) custom-call(s32[128]{0:T(128)} %old_count.1, s32[1]{0:T(128)} %bitcast.device, f32[36,66,512]{2,1,0:T(8,128)} %spectra.7, f32[3,36,512]{2,1,0:T(8,128)} %bitcast.4), custom_call_target="tpu_custom_call" | custom-call | tf_op jit(solution)/shard_map/pallas_call | solution.py:184
  4.8 1.0 %collective-permute-start = (f32[12,72,512]{2,1,0:T(8,128)}, f32[12,72,512]{2,1,0:T(8,128)S(1)}, u32[]{:S(2)}, u32[]{:S(2)}) collective-permute-start(f32[12,72,512]{2,1,0:T(8,128)} %get-tuple-element.24), channel_id=1, source_target_pairs={{0,1},{1,0},{2,3},{3,2},{4,5},{5,4},{6,7},{7,6},{8,9},{9,8},{10,11... | collective-permute-start | bytes 5308424 | tf_op jit(solution)/shard_map/ppermute | solution.py:672
  5.8 1.9 %collective-permute-start.1 = (f32[12,72,512]{2,1,0:T(8,128)}, f32[12,72,512]{2,1,0:T(8,128)S(1)}, u32[]{:S(2)}, u32[]{:S(2)}) collective-permute-start(f32[12,72,512]{2,1,0:T(8,128)} %get-tuple-element.25), channel_id=1, source_target_pairs={{1,2},{3,4},{5,6},{7,8},{9,10},{11,12},{13,14},{15,16},{17,18},{19... | collective-permute-start | bytes 5308424 | tf_op jit(solution)/shard_map/ppermute | solution.py:671
  7.7 0.8 slice.3
  8.5 0.1 copy.16
  8.6 0.1 reshape.15.table
  8.7 1.4 %shard_map.73.scal = s32[9]{0:T(128)} custom-call(s32[1]{0:T(128)} %bitcast.device, s32[1,128]{1,0:T(1,128)} %bitcast.8, s32[1,128]{1,0:T(1,128)} %bitcast.9), custom_call_target="tpu_custom_call" | custom-call | tf_op jit(solution)/shard_map/pallas_call | solution.py:655
  10.0 1.1 %pad.4.kernel = bf16[80,4608]{1,0:T(8,128)(2,1)S(1)} pad(bf16[66,4356]{1,0:T(8,128)(2,1)} %param.9, bf16[]{:T(256)} %constant.8.clone.1), padding=0_14x0_252 | pad | bytes 1312274 | tf_op jit(solution)/shard_map/jit(_pad)/pad | solution.py:318
  11.2 0.0 copy-start.3
  11.2 0.7 copy-done.3
  11.9 5.0 %shard_map.74.sym = bf16[80,2304]{1,0:T(8,128)(2,1)S(1)} custom-call(s32[2,2304]{1,0:T(2,128)S(1)} %copy-done.3, bf16[80,4608]{1,0:T(8,128)(2,1)S(1)} %pad.4.kernel), custom_call_target="tpu_custom_call" | custom-call | flops 2000000000 | bytes 1000000 | tf_op jit(solution)/shard_map/pallas_call | solution.py:319
  17.0 9.0 %shard_map.75 = (f32[36,72,256]{2,1,0:T(8,128)S(1)}, f32[36,24,256]{2,1,0:T(8,128)S(1)}, f32[60,144,128]{2,1,0:T(8,128)S(1)}, f32[36,66,256]{2,1,0:T(8,128)S(1)}, s32[9]{0:T(128)S(1)}) custom-call(s32[9]{0:T(128)S(1)} %copy-done.2, s32[36]{0:T(128)S(1)} %reshape.15.table, f32[36,66,512]{2,1,0:T(8,128)S(1)} %copy-done, f32[3,36,512]{2,1,0:T(8,128)S(1)} %bitcast.5, ...), custom_call_target="tpu_custom_call" | custom-call | flops 4000000000 | bytes 20000000 | tf_op jit(solution)/shard_map/pallas_call | solution.py:450
  26.0 8.0 %collective-permute-done.1.in_other.rest_1_ = f32[12,72,512]{2,1,0:T(8,128)S(1)} collective-permute-done((f32[12,72,512]{2,1,0:T(8,128)}, f32[12,72,512]{2,1,0:T(8,128)S(1)}, u32[]{:S(2)}, u32[]{:S(2)}) %collective-permute-start.1) | collective-permute-done | bytes 1769504 | tf_op jit(solution)/shard_map/ppermute | solution.py:671
  34.1 3.6 %shard_map.77 = (f32[18,72,128]{2,1,0:T(8,128)S(1)}, f32[18,72,128]{2,1,0:T(8,128)S(1)}, s32[9]{0:T(128)S(1)}) custom-call(s32[9]{0:T(128)S(1)} %get-tuple-element.23.scal, s32[36]{0:T(128)S(1)} %reshape.15.table, f32[36,66,512]{2,1,0:T(8,128)S(1)} %copy-done, f32[3,36,512]{2,1,0:T(8,128)S(1)} %bitcast.6, ...), custom_call_target="tpu_custom_call" | custom-call | tf_op jit(solution)/shard_map/pallas_call | solution.py:262
  37.6 0.1 collective-permute-start.2
  37.7 0.1 collective-permute-start.3
  37.8 9.4 %shard_map.78 = (f32[36,72,256]{2,1,0:T(8,128)S(1)}, f32[36,24,256]{2,1,0:T(8,128)S(1)}, f32[60,144,128]{2,1,0:T(8,128)S(1)}, f32[36,66,256]{2,1,0:T(8,128)S(1)}, s32[9]{0:T(128)S(1)}) custom-call(s32[9]{0:T(128)S(1)} %get-tuple-element.27.scal, s32[36]{0:T(128)S(1)} %reshape.15.table, ...), custom_call_target="tpu_custom_call", output_to_operand_aliasing={{0}: (7, {}), {1}: (8, {}), {2}: (9, {}), {3}: (10, {})} | custom-call | flops 4000000000 | bytes 20000000 | tf_op jit(solution)/shard_map/pallas_call | solution.py:450
  47.2 4.9 %collective-permute-done.3.in_other = f32[18,72,128]{2,1,0:T(8,128)S(1)} collective-permute-done((f32[18,72,128]{2,1,0:T(8,128)S(1)}, f32[18,72,128]{2,1,0:T(8,128)S(1)}, u32[]{:S(2)}, u32[]{:S(2)}) %collective-permute-start.3) | collective-permute-done | bytes 663584 | tf_op jit(solution)/shard_map/ppermute | solution.py:671
  52.1 13.5 %shard_map.79 = (f32[36,66,512]{2,1,0:T(8,128)}, f32[12,66,512]{2,1,0:T(8,128)S(1)}, f32[12,66,512]{2,1,0:T(8,128)S(1)}, f32[36,72,256]{2,1,0:T(8,128)S(1)}, f32[60,144,128]{2,1,0:T(8,128)S(1)}) custom-call(s32[9]{0:T(128)S(1)} %get-tuple-element.31.scal, s32[36]{0:T(128)S(1)} %reshape.15.table, ...), custom_call_target="tpu_custom_call", output_to_operand_aliasing={{3}: (2, {}), {4}: (4, {})} | custom-call | flops 8000000000 | bytes 20000000 | tf_op jit(solution)/shard_map/pallas_call | solution.py:580
  65.7 0.1 collective-permute-start.4
  65.8 3.0 %collective-permute-start.5 = (f32[12,66,512]{2,1,0:T(8,128)S(1)}, f32[12,66,512]{2,1,0:T(8,128)S(1)}, u32[]{:S(2)}, u32[]{:S(2)}) collective-permute-start(f32[12,66,512]{2,1,0:T(8,128)S(1)} %get-tuple-element.39), channel_id=1, source_target_pairs={{1,2},{3,4},{5,6},{7,8},{9,10},{11,12},{13,14},{15,16},{17,18},{19... | collective-permute-start | bytes 4866056 | tf_op jit(solution)/shard_map/ppermute | solution.py:671
  68.7 0.7 collective-permute-done.4.pair
  69.5 24.4 %collective-permute-done.5.other = f32[12,66,512]{2,1,0:T(8,128)S(1)} collective-permute-done((f32[12,66,512]{2,1,0:T(8,128)S(1)}, f32[12,66,512]{2,1,0:T(8,128)S(1)}, u32[]{:S(2)}, u32[]{:S(2)}) %collective-permute-start.5) | collective-permute-done | bytes 1622048 | tf_op jit(solution)/shard_map/ppermute | solution.py:671
  93.8 1.0 %shard_map.80 = f32[36,66,512]{2,1,0:T(8,128)} custom-call(s32[9]{0:T(128)S(1)} %get-tuple-element.31.scal, f32[12,66,512]{2,1,0:T(8,128)S(1)} %collective-permute-done.4.pair, f32[12,66,512]{2,1,0:T(8,128)S(1)} %collective-permute-done.5.other, f32[36,66,512]{2,1,0:T(8,128)} %get-tuple-element.40._), custom_call_target="tpu_custom_call", output_to_operand_aliasing={{}: (3, {})} | custom-call | tf_op jit(solution)/shard_map/pallas_call | solution.py:622
  (8 shorter events, 0.0 us)
Async XLA Ops:
  4.8 21.2 %collective-permute-start = (f32[12,72,512]{2,1,0:T(8,128)}, f32[12,72,512]{2,1,0:T(8,128)S(1)}, u32[]{:S(2)}, u32[]{:S(2)}) collective-permute-start(f32[12,72,512]{2,1,0:T(8,128)} %get-tuple-element.24), channel_id=1, source_target_pairs={{0,1},{1,0},{2,3},{3,2},{4,5},{5,4},{6,7},{7,6},{8,9},{9,8},{10,11... | collective-permute-start | bytes 5308424 | tf_op jit(solution)/shard_map/ppermute | solution.py:672
  5.8 28.3 %collective-permute-start.1 = (f32[12,72,512]{2,1,0:T(8,128)}, f32[12,72,512]{2,1,0:T(8,128)S(1)}, u32[]{:S(2)}, u32[]{:S(2)}) collective-permute-start(f32[12,72,512]{2,1,0:T(8,128)} %get-tuple-element.25), channel_id=1, source_target_pairs={{1,2},{3,4},{5,6},{7,8},{9,10},{11,12},{13,14},{15,16},{17,18},{19... | collective-permute-start | bytes 5308424 | tf_op jit(solution)/shard_map/ppermute | solution.py:671
  11.2 0.7 copy-start.3
  11.9 5.1 %copy-start = (f32[36,66,512]{2,1,0:T(8,128)S(1)}, f32[36,66,512]{2,1,0:T(8,128)}, u32[]{:S(2)}) copy-start(f32[36,66,512]{2,1,0:T(8,128)} %spectra.7) | copy-start | bytes 14598148
  11.9 5.1 %copy-start.1 = (f32[36,3,512]{2,0,1:T(8,128)S(1)}, f32[36,3,512]{2,0,1:T(8,128)}, u32[]{:S(2)}) copy-start(f32[36,3,512]{2,0,1:T(8,128)} %param.8) | copy-start | bytes 663556
  11.9 5.1 %copy-start.2 = (s32[9]{0:T(128)S(1)}, s32[9]{0:T(128)}, u32[]{:S(2)}) copy-start(s32[9]{0:T(128)} %shard_map.73.scal) | copy-start | bytes 112
  37.6 9.6 %collective-permute-start.2 = (f32[18,72,128]{2,1,0:T(8,128)S(1)}, f32[18,72,128]{2,1,0:T(8,128)S(1)}, u32[]{:S(2)}, u32[]{:S(2)}) collective-permute-start(f32[18,72,128]{2,1,0:T(8,128)S(1)} %get-tuple-element.36), channel_id=1, source_target_pairs={{0,1},{1,0},{2,3},{3,2},{4,5},{5,4},{6,7},{7,6},{8,9},{9,8},{10,11... | collective-permute-start | bytes 1990664 | tf_op jit(solution)/shard_map/ppermute | solution.py:672
  37.7 14.4 %collective-permute-start.3 = (f32[18,72,128]{2,1,0:T(8,128)S(1)}, f32[18,72,128]{2,1,0:T(8,128)S(1)}, u32[]{:S(2)}, u32[]{:S(2)}) collective-permute-start(f32[18,72,128]{2,1,0:T(8,128)S(1)} %get-tuple-element.37), channel_id=1, source_target_pairs={{1,2},{3,4},{5,6},{7,8},{9,10},{11,12},{13,14},{15,16},{17,18},{19... | collective-permute-start | bytes 1990664 | tf_op jit(solution)/shard_map/ppermute | solution.py:671
  65.7 3.8 %collective-permute-start.4 = (f32[12,66,512]{2,1,0:T(8,128)S(1)}, f32[12,66,512]{2,1,0:T(8,128)S(1)}, u32[]{:S(2)}, u32[]{:S(2)}) collective-permute-start(f32[12,66,512]{2,1,0:T(8,128)S(1)} %get-tuple-element.38), channel_id=1, source_target_pairs={{0,1},{1,0},{2,3},{3,2},{4,5},{5,4},{6,7},{7,6},{8,9},{9,8},{10,11... | collective-permute-start | bytes 4866056 | tf_op jit(solution)/shard_map/ppermute | solution.py:672
  65.8 28.1 %collective-permute-start.5 = (f32[12,66,512]{2,1,0:T(8,128)S(1)}, f32[12,66,512]{2,1,0:T(8,128)S(1)}, u32[]{:S(2)}, u32[]{:S(2)}) collective-permute-start(f32[12,66,512]{2,1,0:T(8,128)S(1)} %get-tuple-element.39), channel_id=1, source_target_pairs={{1,2},{3,4},{5,6},{7,8},{9,10},{11,12},{13,14},{15,16},{17,18},{19... | collective-permute-start | bytes 4866056 | tf_op jit(solution)/shard_map/ppermute | solution.py:671

commit v8 on v7

--- a/solution.py
+++ b/solution.py
@@ -395,7 +395,10 @@
 
 
 def upper_kernel(moved, scal, table, spectra, courant, sym, *rest):
-    low_q1, low_c, face, out, scal_out, q0, cs, q1, fy, fz, q2 = rest[6 if moved else 0 :]
+    rest_out = rest[6 if moved else 0 :]
+    low_q1, low_c, face, out, scal_out = rest_out[:5]
+    pair, other = rest_out[5:7] if moved else (None, None)
+    q0, cs, q1, fy, fz, q2, sems = rest_out[7 if moved else 5 :]
     for k in range(SCALARS):
         scal_out[k] = scal[k]
     here0, here = scal[HERE0], scal[HERE1] - scal[HERE0]
@@ -441,6 +444,21 @@
             q_prev, f_prev = q, f
 
     coalesce_all(0, count, count, block_at, second, q2, sym, out)
+    if not moved:
+        return
+    whole = scal[MID1] - scal[MID0]
+
+    def leave(act):
+        def down(ref):
+            act(pltpu.make_async_copy(out.at[pl.ds(0, RUN)], ref, sems.at[0]))
+
+        def up(ref):
+            act(pltpu.make_async_copy(out.at[pl.ds(whole - RUN, RUN)], ref, sems.at[1]))
+
+        by_side(scal, pair, other, down, up, whole > 0, whole > 0)
+
+    leave(lambda copy: copy.start())
+    leave(lambda copy: copy.wait())
 
 
 def upper_half(scal, table, spectra, courant, sym, *moved):
@@ -450,10 +468,13 @@
     return pl.pallas_call(
         functools.partial(upper_kernel, bool(moved)),
         in_specs=[SMEM, SMEM] + [VMEM] * 3 + ([VMEM] * 6 if moved else []),
-        out_specs=[VMEM] * 4 + [SMEM],
-        out_shape=[jax.ShapeDtypeStruct(shape, F32) for shape in shapes] + [jax.ShapeDtypeStruct((SCALARS,), jnp.int32)],
+        out_specs=[VMEM] * 4 + [SMEM] + ([ANY] * 2 if moved else []),
+        out_shape=[jax.ShapeDtypeStruct(shape, F32) for shape in shapes]
+        + [jax.ShapeDtypeStruct((SCALARS,), jnp.int32)]
+        + ([jax.ShapeDtypeStruct((RUN, BINS, HALF), F32)] * 2 if moved else []),
         scratch_shapes=[pltpu.VMEM((capacity, PACKED, CELLS), F32), pltpu.VMEM((capacity, 24, CELLS), F32)]
-        + [pltpu.VMEM(held, F32)] * 4,
+        + [pltpu.VMEM(held, F32)] * 4
+        + [pltpu.SemaphoreType.DMA((2,))],
         input_output_aliases={7: 0, 8: 1, 9: 2, 10: 3} if moved else {},
         compiler_params=params(32),
         cost_estimate=pl.CostEstimate(flops=4 * 10**9, bytes_accessed=20 * 10**6, transcendentals=0),
@@ -474,12 +495,13 @@
             block = source.at[pl.ds(first, RUN)]
 
             def down(ref):
-                act(pltpu.make_async_copy(block, ref.at[:, :, cells], sems.at[half, 0]))
+                act(pltpu.make_async_copy(block, ref, sems.at[half, 0]))
 
             def up(ref):
-                act(pltpu.make_async_copy(block, ref.at[:, :, cells], sems.at[half, 1]))
-
-            by_side(scal, pair, other, down, up, r == 0, r == runs - 1)
+                act(pltpu.make_async_copy(block, ref, sems.at[half, 1]))
+
+            if half == 0:
+                by_side(scal, pair, other, down, up, r == 0, r == runs - 1)
 
             slot = first + shift
             fits = (slot >= 0) & (slot + RUN <= slots)
@@ -575,7 +597,7 @@
 def lower_half(scal, table, arrays, in_pair, in_other, sym):
     capacity = arrays[0].shape[0]
     whole = jax.ShapeDtypeStruct((capacity, BINS, CELLS), F32)
-    sent = jax.ShapeDtypeStruct((RUN, BINS, CELLS), F32)
+    sent = jax.ShapeDtypeStruct((RUN, BINS, HALF), F32)
     held = pltpu.VMEM((capacity, PACKED, HALF), F32)
     return pl.pallas_call(
         lower_kernel,
@@ -597,37 +619,38 @@
     )(scal, table, *arrays, in_pair, in_other, sym)[:3]
 
 
-def place_moved_kernel(scal, pair, other, _, out, sems):
+def place_moved_kernel(scal, *rest):
+    halves, out, sems = (rest[0:2], rest[2:4]), rest[5], rest[6]
     first, end = scal[NEW0], scal[NEW1]
 
     def copies(act):
-        for k in range(RUN):
-            low, high = scal[MID0] - RUN + k, scal[MID1] + k
-
-            def from_low(ref, k=k, low=low):
-                act(pltpu.make_async_copy(ref.at[k], out.at[low - first], sems.at[0, k]))
-
-            def from_high(ref, k=k, high=high):
-                act(pltpu.make_async_copy(ref.at[k], out.at[high - first], sems.at[1, k]))
-
-            low_in = (low >= first) & (low < end)
-            high_in = (high >= first) & (high < end)
-            by_side(scal, pair, other, from_low, from_high, low_in, high_in)
+        for half in range(2):
+            cells = pl.ds(half * HALF, HALF)
+            for k in range(RUN):
+                low, high = scal[MID0] - RUN + k, scal[MID1] + k
+
+                def put(side, block, ref, k=k, half=half, cells=cells):
+                    act(pltpu.make_async_copy(ref.at[k], out.at[block - first, :, cells], sems.at[half, side, k]))
+
+                low_in = (low >= first) & (low < end)
+                high_in = (high >= first) & (high < end)
+                from_low, from_high = functools.partial(put, 0, low), functools.partial(put, 1, high)
+                by_side(scal, *halves[half], from_low, from_high, low_in, high_in)
 
     copies(lambda copy: copy.start())
     copies(lambda copy: copy.wait())
 
 
-def place_moved(scal, pair, other, out):
+def place_moved(scal, lower, upper_, out):
     return pl.pallas_call(
         place_moved_kernel,
-        in_specs=[SMEM, VMEM, VMEM, ANY],
+        in_specs=[SMEM] + [VMEM] * 4 + [ANY],
         out_specs=ANY,
         out_shape=jax.ShapeDtypeStruct(out.shape, F32),
-        scratch_shapes=[pltpu.SemaphoreType.DMA((2, RUN))],
-        input_output_aliases={3: 0},
+        scratch_shapes=[pltpu.SemaphoreType.DMA((2, 2, RUN))],
+        input_output_aliases={5: 0},
         compiler_params=params(8),
-    )(scal, pair, other, out)
+    )(scal, *lower, *upper_, out)
 
 
 def bounds_kernel(device, old_count, new_count, out):
@@ -679,9 +702,10 @@
     *early, scal = upper_half(scal, table, spectra, courant, sym)
     *sides, scal = faces(scal, table, spectra, courant, *moved, early[2])
     sides = exchange(*sides, others + ends)
-    *arrays, scal = upper_half(scal, table, spectra, courant, sym, *moved, *early)
+    *arrays, scal, pair, other = upper_half(scal, table, spectra, courant, sym, *moved, *early)
+    upper_results = exchange(pair, other, others)
     result, *results = lower_half(scal, table, arrays, *sides, sym)
-    return place_moved(scal, *exchange(*results, others), result)
+    return place_moved(scal, exchange(*results, others), upper_results, result)
 
 
 def solution(mesh):

time: 96.4 us -> 92.3 us (0.957); the launches traced: 94.8 us -> 91.7 us
  waiting for transfers between devices: 38 us -> 26 us
  starting transfers between devices: 6.1 us -> 13.3 us
  Pallas kernels: 47.8 us -> 51.2 us
  local copies, waits for them, and re-layouts: 2.8 us -> 1.01 us
    ppermute x3 -> x4, waiting for transfers between devices: 37.3 us -> 26 us  [exchange(): from_other = lax.ppermute(other, 'blocks', route)]
    ppermute x3 -> x4, starting transfers between devices: 4.96 us -> 11.8 us  [exchange(): from_other = lax.ppermute(other, 'blocks', route)]
    pallas_call x2, Pallas kernels: 18.4 us -> 19.9 us  [upper_half(): pl.pallas_call(functools.partial(upper_kernel, bool(moved)), in_specs=[SM...]
    pad x1, local copies, waits for them, and re-layouts: 1.14 us -> 0.05 us  [symmetric_kernel(): padded = jnp.pad(kernel, ((0, 80 - BINS), (0, wide - kernel.shape[1])))]
    pallas_call x1, Pallas kernels: 0.98 us -> 2.01 us  [place_moved(): pl.pallas_call(place_moved_kernel, in_specs=[SMEM] + [VMEM] * 4 + [ANY],...]
  transfers between devices with their start and end apart: 6 -> 8, of which waited for: 4 -> 2; matrix products, arithmetic and copies ran while one was open for 2% -> 1% of each run, Pallas kernels for 26% -> 43%
where the time goes in v8:
time: 92.3 us; the launch traced here: 91.7 us
  Pallas kernels  51.2 us (55%)
  waiting for transfers between devices  26 us (28%)
  starting transfers between devices  13.3 us (14%)
  local copies, waits for them, and re-layouts  1.01 us (1%)
    ppermute x4, waiting for transfers between devices, exchange(): from_other = lax.ppermute(other, 'blocks', route)  26 us
    pallas_call x2, Pallas kernels, upper_half(): pl.pallas_call(functools.partial(upper_kernel, bool(moved)), in_specs=[SM...  19.9 us
    pallas_call x1, Pallas kernels, lower_half(): pl.pallas_call(lower_kernel, in_specs=[SMEM, SMEM] + [VMEM] * 7, out_spec...  13.4 us
    ppermute x4, starting transfers between devices, exchange(): from_other = lax.ppermute(other, 'blocks', route)  11.8 us
    pallas_call x1, Pallas kernels, symmetric_kernel(): pl.pallas_call(symmetric_kernel_body, grid=(TERMS // 256,), in_specs=[pl....  5.07 us
    pallas_call x1, Pallas kernels, pack(): pl.pallas_call(pack_kernel, in_specs=[SMEM, SMEM, ANY, ANY], out_specs=[A...  4.96 us
    pallas_call x1, Pallas kernels, faces(): pl.pallas_call(face_kernel, in_specs=[SMEM, SMEM] + [VMEM] * 5, out_specs...  4.52 us
    pallas_call x1, Pallas kernels, place_moved(): pl.pallas_call(place_moved_kernel, in_specs=[SMEM] + [VMEM] * 4 + [ANY],...  2.01 us
  transfers between devices with their start and end apart: 8, of which 2 were waited for; matrix products, arithmetic and copies ran while one was open for 1% of the time, Pallas kernels for 43%

profile of v8, /device:TPU:111, one launch (start us, length us, event | category | flops | bytes accessed | tf_op | source)
XLA Modules:
  0.0 91.7 jit_solution(6935603527930363451)
XLA Ops:
  0.0 5.0 %shard_map.76 = (f32[12,72,512]{2,1,0:T(8,128)}, f32[12,72,512]{2,1,0:T(8,128)}) custom-call(s32[128]{0:T(128)} %old_count.1, s32[1]{0:T(128)} %bitcast.device, f32[36,66,512]{2,1,0:T(8,128)} %spectra.7, f32[3,36,512]{2,1,0:T(8,128)} %bitcast.4), custom_call_target="tpu_custom_call" | custom-call | tf_op jit(solution)/shard_map/pallas_call | solution.py:184
  5.0 0.8 collective-permute-start
  5.7 1.9 %collective-permute-start.1 = (f32[12,72,512]{2,1,0:T(8,128)}, f32[12,72,512]{2,1,0:T(8,128)}, u32[]{:S(2)}, u32[]{:S(2)}) collective-permute-start(f32[12,72,512]{2,1,0:T(8,128)} %get-tuple-element.27), channel_id=1, source_target_pairs={{1,2},{3,4},{5,6},{7,8},{9,10},{11,12},{13,14},{15,16},{17,18},{19... | collective-permute-start | bytes 5308424 | tf_op jit(solution)/shard_map/ppermute | solution.py:694
  7.6 0.8 slice.3
  8.4 0.1 copy.16
  8.5 0.1 reshape.15.table
  8.6 1.4 %shard_map.73.scal = s32[9]{0:T(128)} custom-call(s32[1]{0:T(128)} %bitcast.device, s32[1,128]{1,0:T(1,128)} %bitcast.8, s32[1,128]{1,0:T(1,128)} %bitcast.9), custom_call_target="tpu_custom_call" | custom-call | tf_op jit(solution)/shard_map/pallas_call | solution.py:678
  10.0 0.1 pad.4.kernel
  10.0 0.0 copy-start
  10.0 0.0 copy-start.1
  10.1 5.1 %shard_map.74.sym = bf16[80,2304]{1,0:T(8,128)(2,1)S(1)} custom-call(s32[2,2304]{1,0:T(2,128)S(1)} %copy-done.3, bf16[80,4608]{1,0:T(8,128)(2,1)S(1)} %pad.4.kernel), custom_call_target="tpu_custom_call" | custom-call | flops 2000000000 | bytes 1000000 | tf_op jit(solution)/shard_map/pallas_call | solution.py:319
  15.2 9.1 %shard_map.75 = (f32[36,72,256]{2,1,0:T(8,128)S(1)}, f32[36,24,256]{2,1,0:T(8,128)S(1)}, f32[60,144,128]{2,1,0:T(8,128)S(1)}, f32[36,66,256]{2,1,0:T(8,128)S(1)}, s32[9]{0:T(128)S(1)}) custom-call(s32[9]{0:T(128)S(1)} %copy-done.2, s32[36]{0:T(128)S(1)} %reshape.15.table, f32[36,66,512]{2,1,0:T(8,128)S(1)} %copy-done, f32[3,36,512]{2,1,0:T(8,128)S(1)} %bitcast.5, ...), custom_call_target="tpu_custom_call" | custom-call | flops 4000000000 | bytes 20000000 | tf_op jit(solution)/shard_map/pallas_call | solution.py:468
  24.3 9.8 %collective-permute-done.1.in_other.rest_1_ = f32[12,72,512]{2,1,0:T(8,128)} collective-permute-done((f32[12,72,512]{2,1,0:T(8,128)}, f32[12,72,512]{2,1,0:T(8,128)}, u32[]{:S(2)}, u32[]{:S(2)}) %collective-permute-start.1) | collective-permute-done | bytes 1769504 | tf_op jit(solution)/shard_map/ppermute | solution.py:694
  34.1 4.5 %shard_map.77 = (f32[18,72,128]{2,1,0:T(8,128)S(1)}, f32[18,72,128]{2,1,0:T(8,128)S(1)}, s32[9]{0:T(128)S(1)}) custom-call(s32[9]{0:T(128)S(1)} %get-tuple-element.25.scal, s32[36]{0:T(128)S(1)} %reshape.15.table, f32[36,66,512]{2,1,0:T(8,128)S(1)} %copy-done, f32[3,36,512]{2,1,0:T(8,128)S(1)} %bitcast.6, ...), custom_call_target="tpu_custom_call" | custom-call | tf_op jit(solution)/shard_map/pallas_call | solution.py:262
  38.6 0.1 collective-permute-start.2
  38.7 0.1 collective-permute-start.3
  38.8 10.8 %shard_map.78 = (f32[36,72,256]{2,1,0:T(8,128)S(1)}, f32[36,24,256]{2,1,0:T(8,128)S(1)}, f32[60,144,128]{2,1,0:T(8,128)S(1)}, f32[36,66,256]{2,1,0:T(8,128)S(1)}...) custom-call(s32[9]{0:T(128)S(1)} %get-tuple-element.29.scal, ...), custom_call_target="tpu_custom_call", output_to_operand_aliasing={{0}: (7, {}), {1}: (8, {}), {2}: (9, {}), {3}: (10, {})} | custom-call | flops 4000000000 | bytes 20000000 | tf_op jit(solution)/shard_map/pallas_call | solution.py:468
  49.7 0.5 collective-permute-start.6
  50.1 7.5 %collective-permute-start.7 = (f32[12,66,256]{2,1,0:T(8,128)S(1)}, f32[12,66,256]{2,1,0:T(8,128)S(1)}, u32[]{:S(2)}, u32[]{:S(2)}) collective-permute-start(f32[12,66,256]{2,1,0:T(8,128)S(1)} %get-tuple-element.43), channel_id=1, source_target_pairs={{1,2},{3,4},{5,6},{7,8},{9,10},{11,12},{13,14},{15,16},{17,18},{19... | collective-permute-start | bytes 2433032 | tf_op jit(solution)/shard_map/ppermute | solution.py:694
  57.6 13.4 %shard_map.79 = (f32[36,66,512]{2,1,0:T(8,128)}, f32[12,66,256]{2,1,0:T(8,128)S(1)}, f32[12,66,256]{2,1,0:T(8,128)S(1)}, f32[36,72,256]{2,1,0:T(8,128)S(1)}, f32[60,144,128]{2,1,0:T(8,128)S(1)}) custom-call(s32[9]{0:T(128)S(1)} %get-tuple-element.33.scal, s32[36]{0:T(128)S(1)} %reshape.15.table, ...), custom_call_target="tpu_custom_call", output_to_operand_aliasing={{3}: (2, {}), {4}: (4, {})} | custom-call | flops 8000000000 | bytes 20000000 | tf_op jit(solution)/shard_map/pallas_call | solution.py:602
  71.0 0.1 collective-permute-start.4
  71.1 2.4 %collective-permute-start.5 = (f32[12,66,256]{2,1,0:T(8,128)S(1)}, f32[12,66,256]{2,1,0:T(8,128)S(1)}, u32[]{:S(2)}, u32[]{:S(2)}) collective-permute-start(f32[12,66,256]{2,1,0:T(8,128)S(1)} %get-tuple-element.41), channel_id=1, source_target_pairs={{1,2},{3,4},{5,6},{7,8},{9,10},{11,12},{13,14},{15,16},{17,18},{19... | collective-permute-start | bytes 2433032 | tf_op jit(solution)/shard_map/ppermute | solution.py:694
  73.5 16.1 %collective-permute-done.5.rest_1_ = f32[12,66,256]{2,1,0:T(8,128)S(1)} collective-permute-done((f32[12,66,256]{2,1,0:T(8,128)S(1)}, f32[12,66,256]{2,1,0:T(8,128)S(1)}, u32[]{:S(2)}, u32[]{:S(2)}) %collective-permute-start.5) | collective-permute-done | bytes 811040 | tf_op jit(solution)/shard_map/ppermute | solution.py:694
  89.7 2.0 %shard_map.80 = f32[36,66,512]{2,1,0:T(8,128)} custom-call(s32[9]{0:T(128)S(1)} %get-tuple-element.33.scal, f32[12,66,256]{2,1,0:T(8,128)S(1)} %collective-permute-done.4.rest_0_, f32[12,66,256]{2,1,0:T(8,128)S(1)} %collective-permute-done.5.rest_1_, f32[12,66,256]{2,1,0:T(8,128)S(1)} %collective-permute-done.6.rest_2_, ...), custom_call_target="tpu_custom_call", output_to_operand_aliasing={{}: (5, {})} | custom-call | tf_op jit(solution)/shard_map/pallas_call | solution.py:645
  (14 shorter events, 0.0 us)
Async XLA Ops:
  0.0 9.9 %copy-start.4 = (bf16[66,4356]{1,0:T(8,128)(2,1)S(1)}, bf16[66,4356]{1,0:T(8,128)(2,1)}, u32[]{:S(2)}) copy-start(bf16[66,4356]{1,0:T(8,128)(2,1)} %param.9) | copy-start | bytes 1724980
  0.0 10.0 %copy-start.3 = (s32[2,2304]{1,0:T(2,128)S(1)}, s32[2,2304]{1,0:T(2,128)}, u32[]{:S(2)}) copy-start(s32[2,2304]{1,0:T(2,128)} %constant.9.clone.columns) | copy-start | bytes 55300
  5.0 19.3 %collective-permute-start = (f32[12,72,512]{2,1,0:T(8,128)}, f32[12,72,512]{2,1,0:T(8,128)S(1)}, u32[]{:S(2)}, u32[]{:S(2)}) collective-permute-start(f32[12,72,512]{2,1,0:T(8,128)} %get-tuple-element.26), channel_id=1, source_target_pairs={{0,1},{1,0},{2,3},{3,2},{4,5},{5,4},{6,7},{7,6},{8,9},{9,8},{10,11... | collective-permute-start | bytes 5308424 | tf_op jit(solution)/shard_map/ppermute | solution.py:695
  5.7 28.4 %collective-permute-start.1 = (f32[12,72,512]{2,1,0:T(8,128)}, f32[12,72,512]{2,1,0:T(8,128)}, u32[]{:S(2)}, u32[]{:S(2)}) collective-permute-start(f32[12,72,512]{2,1,0:T(8,128)} %get-tuple-element.27), channel_id=1, source_target_pairs={{1,2},{3,4},{5,6},{7,8},{9,10},{11,12},{13,14},{15,16},{17,18},{19... | collective-permute-start | bytes 5308424 | tf_op jit(solution)/shard_map/ppermute | solution.py:694
  10.0 5.1 %copy-start = (f32[36,66,512]{2,1,0:T(8,128)S(1)}, f32[36,66,512]{2,1,0:T(8,128)}, u32[]{:S(2)}) copy-start(f32[36,66,512]{2,1,0:T(8,128)} %spectra.7) | copy-start | bytes 14598148
  10.0 5.1 %copy-start.1 = (f32[36,3,512]{2,0,1:T(8,128)S(1)}, f32[36,3,512]{2,0,1:T(8,128)}, u32[]{:S(2)}) copy-start(f32[36,3,512]{2,0,1:T(8,128)} %param.8) | copy-start | bytes 663556
  10.0 5.1 %copy-start.2 = (s32[9]{0:T(128)S(1)}, s32[9]{0:T(128)}, u32[]{:S(2)}) copy-start(s32[9]{0:T(128)} %shard_map.73.scal) | copy-start | bytes 112
  38.6 19.0 %collective-permute-start.2 = (f32[18,72,128]{2,1,0:T(8,128)S(1)}, f32[18,72,128]{2,1,0:T(8,128)S(1)}, u32[]{:S(2)}, u32[]{:S(2)}) collective-permute-start(f32[18,72,128]{2,1,0:T(8,128)S(1)} %get-tuple-element.38), channel_id=1, source_target_pairs={{0,1},{1,0},{2,3},{3,2},{4,5},{5,4},{6,7},{7,6},{8,9},{9,8},{10,11... | collective-permute-start | bytes 1990664 | tf_op jit(solution)/shard_map/ppermute | solution.py:695
  38.7 18.9 %collective-permute-start.3 = (f32[18,72,128]{2,1,0:T(8,128)S(1)}, f32[18,72,128]{2,1,0:T(8,128)S(1)}, u32[]{:S(2)}, u32[]{:S(2)}) collective-permute-start(f32[18,72,128]{2,1,0:T(8,128)S(1)} %get-tuple-element.39), channel_id=1, source_target_pairs={{1,2},{3,4},{5,6},{7,8},{9,10},{11,12},{13,14},{15,16},{17,18},{19... | collective-permute-start | bytes 1990664 | tf_op jit(solution)/shard_map/ppermute | solution.py:694
  49.7 23.9 %collective-permute-start.6 = (f32[12,66,256]{2,1,0:T(8,128)S(1)}, f32[12,66,256]{2,1,0:T(8,128)S(1)}, u32[]{:S(2)}, u32[]{:S(2)}) collective-permute-start(f32[12,66,256]{2,1,0:T(8,128)S(1)} %get-tuple-element.42), channel_id=1, source_target_pairs={{0,1},{1,0},{2,3},{3,2},{4,5},{5,4},{6,7},{7,6},{8,9},{9,8},{10,11... | collective-permute-start | bytes 2433032 | tf_op jit(solution)/shard_map/ppermute | solution.py:695
  50.1 23.4 %collective-permute-start.7 = (f32[12,66,256]{2,1,0:T(8,128)S(1)}, f32[12,66,256]{2,1,0:T(8,128)S(1)}, u32[]{:S(2)}, u32[]{:S(2)}) collective-permute-start(f32[12,66,256]{2,1,0:T(8,128)S(1)} %get-tuple-element.43), channel_id=1, source_target_pairs={{1,2},{3,4},{5,6},{7,8},{9,10},{11,12},{13,14},{15,16},{17,18},{19... | collective-permute-start | bytes 2433032 | tf_op jit(solution)/shard_map/ppermute | solution.py:694
  71.0 2.5 %collective-permute-start.4 = (f32[12,66,256]{2,1,0:T(8,128)S(1)}, f32[12,66,256]{2,1,0:T(8,128)S(1)}, u32[]{:S(2)}, u32[]{:S(2)}) collective-permute-start(f32[12,66,256]{2,1,0:T(8,128)S(1)} %get-tuple-element.40), channel_id=1, source_target_pairs={{0,1},{1,0},{2,3},{3,2},{4,5},{5,4},{6,7},{7,6},{8,9},{9,8},{10,11... | collective-permute-start | bytes 2433032 | tf_op jit(solution)/shard_map/ppermute | solution.py:695
  71.1 18.6 %collective-permute-start.5 = (f32[12,66,256]{2,1,0:T(8,128)S(1)}, f32[12,66,256]{2,1,0:T(8,128)S(1)}, u32[]{:S(2)}, u32[]{:S(2)}) collective-permute-start(f32[12,66,256]{2,1,0:T(8,128)S(1)} %get-tuple-element.41), channel_id=1, source_target_pairs={{1,2},{3,4},{5,6},{7,8},{9,10},{11,12},{13,14},{15,16},{17,18},{19... | collective-permute-start | bytes 2433032 | tf_op jit(solution)/shard_map/ppermute | solution.py:694

commit v9 on v8

--- a/solution.py
+++ b/solution.py
@@ -476,7 +476,7 @@
         + [pltpu.VMEM(held, F32)] * 4
         + [pltpu.SemaphoreType.DMA((2,))],
         input_output_aliases={7: 0, 8: 1, 9: 2, 10: 3} if moved else {},
-        compiler_params=params(32),
+        compiler_params=params(28),
         cost_estimate=pl.CostEstimate(flops=4 * 10**9, bytes_accessed=20 * 10**6, transcendentals=0),
     )(scal, table, spectra, courant, sym, *moved)
 

time: 92.3 us -> 90.1 us (0.976)
  Pallas kernels: 51.2 us -> 48.7 us
  waiting for transfers between devices: 26 us -> 23.8 us
  local copies, waits for them, and re-layouts: 1.01 us -> 2.8 us
    ppermute x4, waiting for transfers between devices: 26 us -> 23.8 us  [exchange(): from_other = lax.ppermute(other, 'blocks', route)]
    pad x1, local copies, waits for them, and re-layouts: 0.05 us -> 1.14 us  [symmetric_kernel(): padded = jnp.pad(kernel, ((0, 80 - BINS), (0, wide - kernel.shape[1])))]
    pallas_call x1, Pallas kernels: 4.52 us -> 3.59 us  [faces(): pl.pallas_call(face_kernel, in_specs=[SMEM, SMEM] + [VMEM] * 5, out_specs...]
  transfers between devices with their start and end apart: 8 -> 8, of which waited for: 2 -> 2; matrix products, arithmetic and copies ran while one was open for 1% -> 2% of each run, Pallas kernels for 43% -> 43%
where the time goes in v9:
time: 90.1 us; the launch traced here: 89.1 us
  Pallas kernels  48.7 us (54%)
  waiting for transfers between devices  23.8 us (26%)
  starting transfers between devices  13.6 us (15%)
  local copies, waits for them, and re-layouts  2.8 us (3%)
    ppermute x4, waiting for transfers between devices, exchange(): from_other = lax.ppermute(other, 'blocks', route)  23.8 us
    pallas_call x2, Pallas kernels, upper_half(): pl.pallas_call(functools.partial(upper_kernel, bool(moved)), in_specs=[SM...  19 us
    pallas_call x1, Pallas kernels, lower_half(): pl.pallas_call(lower_kernel, in_specs=[SMEM, SMEM] + [VMEM] * 7, out_spec...  13.1 us
    ppermute x4, starting transfers between devices, exchange(): from_other = lax.ppermute(other, 'blocks', route)  12.2 us
    pallas_call x1, Pallas kernels, symmetric_kernel(): pl.pallas_call(symmetric_kernel_body, grid=(TERMS // 256,), in_specs=[pl....  5.05 us
    pallas_call x1, Pallas kernels, pack(): pl.pallas_call(pack_kernel, in_specs=[SMEM, SMEM, ANY, ANY], out_specs=[A...  4.82 us
    pallas_call x1, Pallas kernels, faces(): pl.pallas_call(face_kernel, in_specs=[SMEM, SMEM] + [VMEM] * 5, out_specs...  3.59 us
    pallas_call x1, Pallas kernels, place_moved(): pl.pallas_call(place_moved_kernel, in_specs=[SMEM] + [VMEM] * 4 + [ANY],...  1.82 us
  transfers between devices with their start and end apart: 8, of which 2 were waited for; matrix products, arithmetic and copies ran while one was open for 2% of the time, Pallas kernels for 43%

profile of v9, /device:TPU:111, one launch (start us, length us, event | category | flops | bytes accessed | tf_op | source)
XLA Modules:
  0.0 89.1 jit_solution(7499393092514408549)
XLA Ops:
  0.0 4.8 %shard_map.76 = (f32[12,72,512]{2,1,0:T(8,128)}, f32[12,72,512]{2,1,0:T(8,128)}) custom-call(s32[128]{0:T(128)} %old_count.1, s32[1]{0:T(128)} %bitcast.device, f32[36,66,512]{2,1,0:T(8,128)} %spectra.7, f32[3,36,512]{2,1,0:T(8,128)} %bitcast.4), custom_call_target="tpu_custom_call" | custom-call | tf_op jit(solution)/shard_map/pallas_call | solution.py:184
  4.8 0.8 collective-permute-start
  5.6 1.9 %collective-permute-start.1 = (f32[12,72,512]{2,1,0:T(8,128)}, f32[12,72,512]{2,1,0:T(8,128)S(1)}, u32[]{:S(2)}, u32[]{:S(2)}) collective-permute-start(f32[12,72,512]{2,1,0:T(8,128)} %get-tuple-element.27), channel_id=1, source_target_pairs={{1,2},{3,4},{5,6},{7,8},{9,10},{11,12},{13,14},{15,16},{17,18},{19... | collective-permute-start | bytes 5308424 | tf_op jit(solution)/shard_map/ppermute | solution.py:694
  7.5 0.8 slice.3
  8.3 0.1 copy.16
  8.4 0.1 reshape.15.table
  8.4 1.4 %shard_map.73.scal = s32[9]{0:T(128)} custom-call(s32[1]{0:T(128)} %bitcast.device, s32[1,128]{1,0:T(1,128)} %bitcast.8, s32[1,128]{1,0:T(1,128)} %bitcast.9), custom_call_target="tpu_custom_call" | custom-call | tf_op jit(solution)/shard_map/pallas_call | solution.py:678
  9.8 1.1 %pad.4.kernel = bf16[80,4608]{1,0:T(8,128)(2,1)S(1)} pad(bf16[66,4356]{1,0:T(8,128)(2,1)} %param.9, bf16[]{:T(256)} %constant.8.clone.1), padding=0_14x0_252 | pad | bytes 1312274 | tf_op jit(solution)/shard_map/jit(_pad)/pad | solution.py:318
  10.9 0.0 copy-start.3
  11.0 0.7 copy-done.3
  11.7 5.0 %shard_map.74.sym = bf16[80,2304]{1,0:T(8,128)(2,1)S(1)} custom-call(s32[2,2304]{1,0:T(2,128)S(1)} %copy-done.3, bf16[80,4608]{1,0:T(8,128)(2,1)S(1)} %pad.4.kernel), custom_call_target="tpu_custom_call" | custom-call | flops 2000000000 | bytes 1000000 | tf_op jit(solution)/shard_map/pallas_call | solution.py:319
  16.8 9.1 %shard_map.75 = (f32[36,72,256]{2,1,0:T(8,128)S(1)}, f32[36,24,256]{2,1,0:T(8,128)S(1)}, f32[60,144,128]{2,1,0:T(8,128)S(1)}, f32[36,66,256]{2,1,0:T(8,128)S(1)}, s32[9]{0:T(128)S(1)}) custom-call(s32[9]{0:T(128)S(1)} %copy-done.2, s32[36]{0:T(128)S(1)} %reshape.15.table, f32[36,66,512]{2,1,0:T(8,128)S(1)} %copy-done, f32[3,36,512]{2,1,0:T(8,128)S(1)} %bitcast.5, ...), custom_call_target="tpu_custom_call" | custom-call | flops 4000000000 | bytes 20000000 | tf_op jit(solution)/shard_map/pallas_call | solution.py:468
  25.9 8.0 %collective-permute-done.1.in_other.rest_1_ = f32[12,72,512]{2,1,0:T(8,128)S(1)} collective-permute-done((f32[12,72,512]{2,1,0:T(8,128)}, f32[12,72,512]{2,1,0:T(8,128)S(1)}, u32[]{:S(2)}, u32[]{:S(2)}) %collective-permute-start.1) | collective-permute-done | bytes 1769504 | tf_op jit(solution)/shard_map/ppermute | solution.py:694
  33.9 3.6 %shard_map.77 = (f32[18,72,128]{2,1,0:T(8,128)S(1)}, f32[18,72,128]{2,1,0:T(8,128)S(1)}, s32[9]{0:T(128)S(1)}) custom-call(s32[9]{0:T(128)S(1)} %get-tuple-element.25.scal, s32[36]{0:T(128)S(1)} %reshape.15.table, f32[36,66,512]{2,1,0:T(8,128)S(1)} %copy-done, f32[3,36,512]{2,1,0:T(8,128)S(1)} %bitcast.6, ...), custom_call_target="tpu_custom_call" | custom-call | tf_op jit(solution)/shard_map/pallas_call | solution.py:262
  37.4 0.1 collective-permute-start.2
  37.5 0.1 collective-permute-start.3
  37.6 9.9 %shard_map.78 = (f32[36,72,256]{2,1,0:T(8,128)S(1)}, f32[36,24,256]{2,1,0:T(8,128)S(1)}, f32[60,144,128]{2,1,0:T(8,128)S(1)}, f32[36,66,256]{2,1,0:T(8,128)S(1)}...) custom-call(s32[9]{0:T(128)S(1)} %get-tuple-element.29.scal, ...), custom_call_target="tpu_custom_call", output_to_operand_aliasing={{0}: (7, {}), {1}: (8, {}), {2}: (9, {}), {3}: (10, {})} | custom-call | flops 4000000000 | bytes 20000000 | tf_op jit(solution)/shard_map/pallas_call | solution.py:468
  47.6 0.5 collective-permute-start.6
  48.0 7.5 %collective-permute-start.7 = (f32[12,66,256]{2,1,0:T(8,128)S(1)}, f32[12,66,256]{2,1,0:T(8,128)S(1)}, u32[]{:S(2)}, u32[]{:S(2)}) collective-permute-start(f32[12,66,256]{2,1,0:T(8,128)S(1)} %get-tuple-element.43), channel_id=1, source_target_pairs={{1,2},{3,4},{5,6},{7,8},{9,10},{11,12},{13,14},{15,16},{17,18},{19... | collective-permute-start | bytes 2433032 | tf_op jit(solution)/shard_map/ppermute | solution.py:694
  55.5 13.1 %shard_map.79 = (f32[36,66,512]{2,1,0:T(8,128)}, f32[12,66,256]{2,1,0:T(8,128)S(1)}, f32[12,66,256]{2,1,0:T(8,128)S(1)}, f32[36,72,256]{2,1,0:T(8,128)S(1)}, f32[60,144,128]{2,1,0:T(8,128)S(1)}) custom-call(s32[9]{0:T(128)S(1)} %get-tuple-element.33.scal, s32[36]{0:T(128)S(1)} %reshape.15.table, ...), custom_call_target="tpu_custom_call", output_to_operand_aliasing={{3}: (2, {}), {4}: (4, {})} | custom-call | flops 8000000000 | bytes 20000000 | tf_op jit(solution)/shard_map/pallas_call | solution.py:602
  68.6 0.1 collective-permute-start.4
  68.7 2.7 %collective-permute-start.5 = (f32[12,66,256]{2,1,0:T(8,128)S(1)}, f32[12,66,256]{2,1,0:T(8,128)S(1)}, u32[]{:S(2)}, u32[]{:S(2)}) collective-permute-start(f32[12,66,256]{2,1,0:T(8,128)S(1)} %get-tuple-element.41), channel_id=1, source_target_pairs={{1,2},{3,4},{5,6},{7,8},{9,10},{11,12},{13,14},{15,16},{17,18},{19... | collective-permute-start | bytes 2433032 | tf_op jit(solution)/shard_map/ppermute | solution.py:694
  71.5 15.8 %collective-permute-done.5.rest_1_ = f32[12,66,256]{2,1,0:T(8,128)S(1)} collective-permute-done((f32[12,66,256]{2,1,0:T(8,128)S(1)}, f32[12,66,256]{2,1,0:T(8,128)S(1)}, u32[]{:S(2)}, u32[]{:S(2)}) %collective-permute-start.5) | collective-permute-done | bytes 811040 | tf_op jit(solution)/shard_map/ppermute | solution.py:694
  87.3 1.8 %shard_map.80 = f32[36,66,512]{2,1,0:T(8,128)} custom-call(s32[9]{0:T(128)S(1)} %get-tuple-element.33.scal, f32[12,66,256]{2,1,0:T(8,128)S(1)} %collective-permute-done.4.rest_0_, f32[12,66,256]{2,1,0:T(8,128)S(1)} %collective-permute-done.5.rest_1_, f32[12,66,256]{2,1,0:T(8,128)S(1)} %collective-permute-done.6.rest_2_, ...), custom_call_target="tpu_custom_call", output_to_operand_aliasing={{}: (5, {})} | custom-call | tf_op jit(solution)/shard_map/pallas_call | solution.py:645
  (12 shorter events, 0.0 us)
Async XLA Ops:
  4.8 21.0 %collective-permute-start = (f32[12,72,512]{2,1,0:T(8,128)}, f32[12,72,512]{2,1,0:T(8,128)S(1)}, u32[]{:S(2)}, u32[]{:S(2)}) collective-permute-start(f32[12,72,512]{2,1,0:T(8,128)} %get-tuple-element.26), channel_id=1, source_target_pairs={{0,1},{1,0},{2,3},{3,2},{4,5},{5,4},{6,7},{7,6},{8,9},{9,8},{10,11... | collective-permute-start | bytes 5308424 | tf_op jit(solution)/shard_map/ppermute | solution.py:695
  5.6 28.3 %collective-permute-start.1 = (f32[12,72,512]{2,1,0:T(8,128)}, f32[12,72,512]{2,1,0:T(8,128)S(1)}, u32[]{:S(2)}, u32[]{:S(2)}) collective-permute-start(f32[12,72,512]{2,1,0:T(8,128)} %get-tuple-element.27), channel_id=1, source_target_pairs={{1,2},{3,4},{5,6},{7,8},{9,10},{11,12},{13,14},{15,16},{17,18},{19... | collective-permute-start | bytes 5308424 | tf_op jit(solution)/shard_map/ppermute | solution.py:694
  10.9 0.7 copy-start.3
  11.7 5.1 %copy-start = (f32[36,66,512]{2,1,0:T(8,128)S(1)}, f32[36,66,512]{2,1,0:T(8,128)}, u32[]{:S(2)}) copy-start(f32[36,66,512]{2,1,0:T(8,128)} %spectra.7) | copy-start | bytes 14598148
  11.7 5.1 %copy-start.1 = (f32[36,3,512]{2,0,1:T(8,128)S(1)}, f32[36,3,512]{2,0,1:T(8,128)}, u32[]{:S(2)}) copy-start(f32[36,3,512]{2,0,1:T(8,128)} %param.8) | copy-start | bytes 663556
  11.7 5.1 %copy-start.2 = (s32[9]{0:T(128)S(1)}, s32[9]{0:T(128)}, u32[]{:S(2)}) copy-start(s32[9]{0:T(128)} %shard_map.73.scal) | copy-start | bytes 112
  37.4 18.1 %collective-permute-start.2 = (f32[18,72,128]{2,1,0:T(8,128)S(1)}, f32[18,72,128]{2,1,0:T(8,128)S(1)}, u32[]{:S(2)}, u32[]{:S(2)}) collective-permute-start(f32[18,72,128]{2,1,0:T(8,128)S(1)} %get-tuple-element.38), channel_id=1, source_target_pairs={{0,1},{1,0},{2,3},{3,2},{4,5},{5,4},{6,7},{7,6},{8,9},{9,8},{10,11... | collective-permute-start | bytes 1990664 | tf_op jit(solution)/shard_map/ppermute | solution.py:695
  37.5 18.0 %collective-permute-start.3 = (f32[18,72,128]{2,1,0:T(8,128)S(1)}, f32[18,72,128]{2,1,0:T(8,128)S(1)}, u32[]{:S(2)}, u32[]{:S(2)}) collective-permute-start(f32[18,72,128]{2,1,0:T(8,128)S(1)} %get-tuple-element.39), channel_id=1, source_target_pairs={{1,2},{3,4},{5,6},{7,8},{9,10},{11,12},{13,14},{15,16},{17,18},{19... | collective-permute-start | bytes 1990664 | tf_op jit(solution)/shard_map/ppermute | solution.py:694
  47.6 23.9 %collective-permute-start.6 = (f32[12,66,256]{2,1,0:T(8,128)S(1)}, f32[12,66,256]{2,1,0:T(8,128)S(1)}, u32[]{:S(2)}, u32[]{:S(2)}) collective-permute-start(f32[12,66,256]{2,1,0:T(8,128)S(1)} %get-tuple-element.42), channel_id=1, source_target_pairs={{0,1},{1,0},{2,3},{3,2},{4,5},{5,4},{6,7},{7,6},{8,9},{9,8},{10,11... | collective-permute-start | bytes 2433032 | tf_op jit(solution)/shard_map/ppermute | solution.py:695
  48.0 23.4 %collective-permute-start.7 = (f32[12,66,256]{2,1,0:T(8,128)S(1)}, f32[12,66,256]{2,1,0:T(8,128)S(1)}, u32[]{:S(2)}, u32[]{:S(2)}) collective-permute-start(f32[12,66,256]{2,1,0:T(8,128)S(1)} %get-tuple-element.43), channel_id=1, source_target_pairs={{1,2},{3,4},{5,6},{7,8},{9,10},{11,12},{13,14},{15,16},{17,18},{19... | collective-permute-start | bytes 2433032 | tf_op jit(solution)/shard_map/ppermute | solution.py:694
  68.6 2.9 %collective-permute-start.4 = (f32[12,66,256]{2,1,0:T(8,128)S(1)}, f32[12,66,256]{2,1,0:T(8,128)S(1)}, u32[]{:S(2)}, u32[]{:S(2)}) collective-permute-start(f32[12,66,256]{2,1,0:T(8,128)S(1)} %get-tuple-element.40), channel_id=1, source_target_pairs={{0,1},{1,0},{2,3},{3,2},{4,5},{5,4},{6,7},{7,6},{8,9},{9,8},{10,11... | collective-permute-start | bytes 2433032 | tf_op jit(solution)/shard_map/ppermute | solution.py:695
  68.7 18.6 %collective-permute-start.5 = (f32[12,66,256]{2,1,0:T(8,128)S(1)}, f32[12,66,256]{2,1,0:T(8,128)S(1)}, u32[]{:S(2)}, u32[]{:S(2)}) collective-permute-start(f32[12,66,256]{2,1,0:T(8,128)S(1)} %get-tuple-element.41), channel_id=1, source_target_pairs={{1,2},{3,4},{5,6},{7,8},{9,10},{11,12},{13,14},{15,16},{17,18},{19... | collective-permute-start | bytes 2433032 | tf_op jit(solution)/shard_map/ppermute | solution.py:694

commit v10 on v9

--- a/solution.py
+++ b/solution.py
@@ -17,8 +17,8 @@
 FULL = 64
 TERMS = 2304
 GROUPS = 9
-STENCILS = 6
-PRODUCTS = 2
+STENCILS = 12
+PRODUCTS = 3
 FACES = 18
 F32 = jnp.float32
 VMEM = pl.BlockSpec(memory_space=pltpu.VMEM)

time: 90.1 us -> 89.7 us (level)
  transfers between devices with their start and end apart: 8 -> 8, of which waited for: 2 -> 3; matrix products, arithmetic and copies ran while one was open for 2% -> 2% of each run, Pallas kernels for 43% -> 43%
where the time goes in v10:
time: 89.7 us; the launch traced here: 89.2 us
  Pallas kernels  48.8 us (54%)
  waiting for transfers between devices  24.4 us (27%)
  starting transfers between devices  12.9 us (14%)
  local copies, waits for them, and re-layouts  2.8 us (3%)
    ppermute x4, waiting for transfers between devices, exchange(): from_other = lax.ppermute(other, 'blocks', route)  24.2 us
    pallas_call x2, Pallas kernels, upper_half(): pl.pallas_call(functools.partial(upper_kernel, bool(moved)), in_specs=[SM...  18.8 us
    pallas_call x1, Pallas kernels, lower_half(): pl.pallas_call(lower_kernel, in_specs=[SMEM, SMEM] + [VMEM] * 7, out_spec...  13 us
    ppermute x4, starting transfers between devices, exchange(): from_other = lax.ppermute(other, 'blocks', route)  11.7 us
    pallas_call x1, Pallas kernels, symmetric_kernel(): pl.pallas_call(symmetric_kernel_body, grid=(TERMS // 256,), in_specs=[pl....  5.04 us
    pallas_call x1, Pallas kernels, pack(): pl.pallas_call(pack_kernel, in_specs=[SMEM, SMEM, ANY, ANY], out_specs=[A...  5.04 us
    pallas_call x1, Pallas kernels, faces(): pl.pallas_call(face_kernel, in_specs=[SMEM, SMEM] + [VMEM] * 5, out_specs...  3.56 us
    pallas_call x1, Pallas kernels, place_moved(): pl.pallas_call(place_moved_kernel, in_specs=[SMEM] + [VMEM] * 4 + [ANY],...  2.01 us
  transfers between devices with their start and end apart: 8, of which 3 were waited for; matrix products, arithmetic and copies ran while one was open for 2% of the time, Pallas kernels for 43%

profile of v10, /device:TPU:111, one launch (start us, length us, event | category | flops | bytes accessed | tf_op | source)
XLA Modules:
  0.0 89.2 jit_solution(17686727718622499284)
XLA Ops:
  0.0 5.0 %shard_map.76 = (f32[12,72,512]{2,1,0:T(8,128)}, f32[12,72,512]{2,1,0:T(8,128)}) custom-call(s32[128]{0:T(128)} %old_count.1, s32[1]{0:T(128)} %bitcast.device, f32[36,66,512]{2,1,0:T(8,128)} %spectra.7, f32[3,36,512]{2,1,0:T(8,128)} %bitcast.4), custom_call_target="tpu_custom_call" | custom-call | tf_op jit(solution)/shard_map/pallas_call | solution.py:184
  5.0 0.5 collective-permute-start
  5.6 1.9 %collective-permute-start.1 = (f32[12,72,512]{2,1,0:T(8,128)}, f32[12,72,512]{2,1,0:T(8,128)S(1)}, u32[]{:S(2)}, u32[]{:S(2)}) collective-permute-start(f32[12,72,512]{2,1,0:T(8,128)} %get-tuple-element.27), channel_id=1, source_target_pairs={{1,2},{3,4},{5,6},{7,8},{9,10},{11,12},{13,14},{15,16},{17,18},{19... | collective-permute-start | bytes 5308424 | tf_op jit(solution)/shard_map/ppermute | solution.py:694
  7.5 0.8 slice.3
  8.3 0.1 copy.16
  8.4 0.1 reshape.15.table
  8.4 1.4 %shard_map.73.scal = s32[9]{0:T(128)} custom-call(s32[1]{0:T(128)} %bitcast.device, s32[1,128]{1,0:T(1,128)} %bitcast.8, s32[1,128]{1,0:T(1,128)} %bitcast.9), custom_call_target="tpu_custom_call" | custom-call | tf_op jit(solution)/shard_map/pallas_call | solution.py:678
  9.8 1.1 %pad.4.kernel = bf16[80,4608]{1,0:T(8,128)(2,1)S(1)} pad(bf16[66,4356]{1,0:T(8,128)(2,1)} %param.9, bf16[]{:T(256)} %constant.8.clone.1), padding=0_14x0_252 | pad | bytes 1312274 | tf_op jit(solution)/shard_map/jit(_pad)/pad | solution.py:318
  11.0 0.7 copy-done.3
  11.7 5.0 %shard_map.74.sym = bf16[80,2304]{1,0:T(8,128)(2,1)S(1)} custom-call(s32[2,2304]{1,0:T(2,128)S(1)} %copy-done.3, bf16[80,4608]{1,0:T(8,128)(2,1)S(1)} %pad.4.kernel), custom_call_target="tpu_custom_call" | custom-call | flops 2000000000 | bytes 1000000 | tf_op jit(solution)/shard_map/pallas_call | solution.py:319
  16.8 9.0 %shard_map.75 = (f32[36,72,256]{2,1,0:T(8,128)S(1)}, f32[36,24,256]{2,1,0:T(8,128)S(1)}, f32[60,144,128]{2,1,0:T(8,128)S(1)}, f32[36,66,256]{2,1,0:T(8,128)S(1)}, s32[9]{0:T(128)S(1)}) custom-call(s32[9]{0:T(128)S(1)} %copy-done.2, s32[36]{0:T(128)S(1)} %reshape.15.table, f32[36,66,512]{2,1,0:T(8,128)S(1)} %copy-done, f32[3,36,512]{2,1,0:T(8,128)S(1)} %bitcast.5, ...), custom_call_target="tpu_custom_call" | custom-call | flops 4000000000 | bytes 20000000 | tf_op jit(solution)/shard_map/pallas_call | solution.py:468
  25.8 8.0 %collective-permute-done.1.in_other.rest_1_ = f32[12,72,512]{2,1,0:T(8,128)S(1)} collective-permute-done((f32[12,72,512]{2,1,0:T(8,128)}, f32[12,72,512]{2,1,0:T(8,128)S(1)}, u32[]{:S(2)}, u32[]{:S(2)}) %collective-permute-start.1) | collective-permute-done | bytes 1769504 | tf_op jit(solution)/shard_map/ppermute | solution.py:694
  33.9 3.6 %shard_map.77 = (f32[18,72,128]{2,1,0:T(8,128)S(1)}, f32[18,72,128]{2,1,0:T(8,128)S(1)}, s32[9]{0:T(128)S(1)}) custom-call(s32[9]{0:T(128)S(1)} %get-tuple-element.25.scal, s32[36]{0:T(128)S(1)} %reshape.15.table, f32[36,66,512]{2,1,0:T(8,128)S(1)} %copy-done, f32[3,36,512]{2,1,0:T(8,128)S(1)} %bitcast.6, ...), custom_call_target="tpu_custom_call" | custom-call | tf_op jit(solution)/shard_map/pallas_call | solution.py:262
  37.4 0.1 collective-permute-start.2
  37.5 0.1 collective-permute-start.3
  37.6 9.7 %shard_map.78 = (f32[36,72,256]{2,1,0:T(8,128)S(1)}, f32[36,24,256]{2,1,0:T(8,128)S(1)}, f32[60,144,128]{2,1,0:T(8,128)S(1)}, f32[36,66,256]{2,1,0:T(8,128)S(1)}...) custom-call(s32[9]{0:T(128)S(1)} %get-tuple-element.29.scal, ...), custom_call_target="tpu_custom_call", output_to_operand_aliasing={{0}: (7, {}), {1}: (8, {}), {2}: (9, {}), {3}: (10, {})} | custom-call | flops 4000000000 | bytes 20000000 | tf_op jit(solution)/shard_map/pallas_call | solution.py:468
  47.4 0.5 collective-permute-start.6
  47.9 7.5 %collective-permute-start.7 = (f32[12,66,256]{2,1,0:T(8,128)S(1)}, f32[12,66,256]{2,1,0:T(8,128)S(1)}, u32[]{:S(2)}, u32[]{:S(2)}) collective-permute-start(f32[12,66,256]{2,1,0:T(8,128)S(1)} %get-tuple-element.43), channel_id=1, source_target_pairs={{1,2},{3,4},{5,6},{7,8},{9,10},{11,12},{13,14},{15,16},{17,18},{19... | collective-permute-start | bytes 2433032 | tf_op jit(solution)/shard_map/ppermute | solution.py:694
  55.4 13.0 %shard_map.79 = (f32[36,66,512]{2,1,0:T(8,128)}, f32[12,66,256]{2,1,0:T(8,128)S(1)}, f32[12,66,256]{2,1,0:T(8,128)S(1)}, f32[36,72,256]{2,1,0:T(8,128)S(1)}, f32[60,144,128]{2,1,0:T(8,128)S(1)}) custom-call(s32[9]{0:T(128)S(1)} %get-tuple-element.33.scal, s32[36]{0:T(128)S(1)} %reshape.15.table, ...), custom_call_target="tpu_custom_call", output_to_operand_aliasing={{3}: (2, {}), {4}: (4, {})} | custom-call | flops 8000000000 | bytes 20000000 | tf_op jit(solution)/shard_map/pallas_call | solution.py:602
  68.3 0.1 collective-permute-start.4
  68.4 2.3 %collective-permute-start.5 = (f32[12,66,256]{2,1,0:T(8,128)S(1)}, f32[12,66,256]{2,1,0:T(8,128)S(1)}, u32[]{:S(2)}, u32[]{:S(2)}) collective-permute-start(f32[12,66,256]{2,1,0:T(8,128)S(1)} %get-tuple-element.41), channel_id=1, source_target_pairs={{1,2},{3,4},{5,6},{7,8},{9,10},{11,12},{13,14},{15,16},{17,18},{19... | collective-permute-start | bytes 2433032 | tf_op jit(solution)/shard_map/ppermute | solution.py:694
  70.7 0.1 collective-permute-done.4.rest_0_
  70.8 16.2 %collective-permute-done.5.rest_1_ = f32[12,66,256]{2,1,0:T(8,128)S(1)} collective-permute-done((f32[12,66,256]{2,1,0:T(8,128)S(1)}, f32[12,66,256]{2,1,0:T(8,128)S(1)}, u32[]{:S(2)}, u32[]{:S(2)}) %collective-permute-start.5) | collective-permute-done | bytes 811040 | tf_op jit(solution)/shard_map/ppermute | solution.py:694
  87.0 2.0 %shard_map.80 = f32[36,66,512]{2,1,0:T(8,128)} custom-call(s32[9]{0:T(128)S(1)} %get-tuple-element.33.scal, f32[12,66,256]{2,1,0:T(8,128)S(1)} %collective-permute-done.4.rest_0_, f32[12,66,256]{2,1,0:T(8,128)S(1)} %collective-permute-done.5.rest_1_, f32[12,66,256]{2,1,0:T(8,128)S(1)} %collective-permute-done.6.rest_2_, ...), custom_call_target="tpu_custom_call", output_to_operand_aliasing={{}: (5, {})} | custom-call | tf_op jit(solution)/shard_map/pallas_call | solution.py:645
  (12 shorter events, 0.0 us)
Async XLA Ops:
  5.0 20.8 %collective-permute-start = (f32[12,72,512]{2,1,0:T(8,128)}, f32[12,72,512]{2,1,0:T(8,128)S(1)}, u32[]{:S(2)}, u32[]{:S(2)}) collective-permute-start(f32[12,72,512]{2,1,0:T(8,128)} %get-tuple-element.26), channel_id=1, source_target_pairs={{0,1},{1,0},{2,3},{3,2},{4,5},{5,4},{6,7},{7,6},{8,9},{9,8},{10,11... | collective-permute-start | bytes 5308424 | tf_op jit(solution)/shard_map/ppermute | solution.py:695
  5.6 28.3 %collective-permute-start.1 = (f32[12,72,512]{2,1,0:T(8,128)}, f32[12,72,512]{2,1,0:T(8,128)S(1)}, u32[]{:S(2)}, u32[]{:S(2)}) collective-permute-start(f32[12,72,512]{2,1,0:T(8,128)} %get-tuple-element.27), channel_id=1, source_target_pairs={{1,2},{3,4},{5,6},{7,8},{9,10},{11,12},{13,14},{15,16},{17,18},{19... | collective-permute-start | bytes 5308424 | tf_op jit(solution)/shard_map/ppermute | solution.py:694
  10.9 0.7 copy-start.3
  11.7 5.1 %copy-start = (f32[36,66,512]{2,1,0:T(8,128)S(1)}, f32[36,66,512]{2,1,0:T(8,128)}, u32[]{:S(2)}) copy-start(f32[36,66,512]{2,1,0:T(8,128)} %spectra.7) | copy-start | bytes 14598148
  11.7 5.1 %copy-start.1 = (f32[36,3,512]{2,0,1:T(8,128)S(1)}, f32[36,3,512]{2,0,1:T(8,128)}, u32[]{:S(2)}) copy-start(f32[36,3,512]{2,0,1:T(8,128)} %param.8) | copy-start | bytes 663556
  11.7 5.1 %copy-start.2 = (s32[9]{0:T(128)S(1)}, s32[9]{0:T(128)}, u32[]{:S(2)}) copy-start(s32[9]{0:T(128)} %shard_map.73.scal) | copy-start | bytes 112
  37.4 17.9 %collective-permute-start.2 = (f32[18,72,128]{2,1,0:T(8,128)S(1)}, f32[18,72,128]{2,1,0:T(8,128)S(1)}, u32[]{:S(2)}, u32[]{:S(2)}) collective-permute-start(f32[18,72,128]{2,1,0:T(8,128)S(1)} %get-tuple-element.38), channel_id=1, source_target_pairs={{0,1},{1,0},{2,3},{3,2},{4,5},{5,4},{6,7},{7,6},{8,9},{9,8},{10,11... | collective-permute-start | bytes 1990664 | tf_op jit(solution)/shard_map/ppermute | solution.py:695
  37.5 17.8 %collective-permute-start.3 = (f32[18,72,128]{2,1,0:T(8,128)S(1)}, f32[18,72,128]{2,1,0:T(8,128)S(1)}, u32[]{:S(2)}, u32[]{:S(2)}) collective-permute-start(f32[18,72,128]{2,1,0:T(8,128)S(1)} %get-tuple-element.39), channel_id=1, source_target_pairs={{1,2},{3,4},{5,6},{7,8},{9,10},{11,12},{13,14},{15,16},{17,18},{19... | collective-permute-start | bytes 1990664 | tf_op jit(solution)/shard_map/ppermute | solution.py:694
  47.4 23.3 %collective-permute-start.6 = (f32[12,66,256]{2,1,0:T(8,128)S(1)}, f32[12,66,256]{2,1,0:T(8,128)S(1)}, u32[]{:S(2)}, u32[]{:S(2)}) collective-permute-start(f32[12,66,256]{2,1,0:T(8,128)S(1)} %get-tuple-element.42), channel_id=1, source_target_pairs={{0,1},{1,0},{2,3},{3,2},{4,5},{5,4},{6,7},{7,6},{8,9},{9,8},{10,11... | collective-permute-start | bytes 2433032 | tf_op jit(solution)/shard_map/ppermute | solution.py:695
  47.9 22.8 %collective-permute-start.7 = (f32[12,66,256]{2,1,0:T(8,128)S(1)}, f32[12,66,256]{2,1,0:T(8,128)S(1)}, u32[]{:S(2)}, u32[]{:S(2)}) collective-permute-start(f32[12,66,256]{2,1,0:T(8,128)S(1)} %get-tuple-element.43), channel_id=1, source_target_pairs={{1,2},{3,4},{5,6},{7,8},{9,10},{11,12},{13,14},{15,16},{17,18},{19... | collective-permute-start | bytes 2433032 | tf_op jit(solution)/shard_map/ppermute | solution.py:694
  68.3 2.5 %collective-permute-start.4 = (f32[12,66,256]{2,1,0:T(8,128)S(1)}, f32[12,66,256]{2,1,0:T(8,128)S(1)}, u32[]{:S(2)}, u32[]{:S(2)}) collective-permute-start(f32[12,66,256]{2,1,0:T(8,128)S(1)} %get-tuple-element.40), channel_id=1, source_target_pairs={{0,1},{1,0},{2,3},{3,2},{4,5},{5,4},{6,7},{7,6},{8,9},{9,8},{10,11... | collective-permute-start | bytes 2433032 | tf_op jit(solution)/shard_map/ppermute | solution.py:695
  68.4 18.6 %collective-permute-start.5 = (f32[12,66,256]{2,1,0:T(8,128)S(1)}, f32[12,66,256]{2,1,0:T(8,128)S(1)}, u32[]{:S(2)}, u32[]{:S(2)}) collective-permute-start(f32[12,66,256]{2,1,0:T(8,128)S(1)} %get-tuple-element.41), channel_id=1, source_target_pairs={{1,2},{3,4},{5,6},{7,8},{9,10},{11,12},{13,14},{15,16},{17,18},{19... | collective-permute-start | bytes 2433032 | tf_op jit(solution)/shard_map/ppermute | solution.py:694
